TPU v7x, 32 devices: a whole 2x2x4 slice. The times are simulated.
32 devices in a mesh: groups: 2 (over y), node: 4 (over z), row: 2 (over x), sub: 2 (over core).
Axes of the slice: x: 2, y: 2, z: 4, core: 2. Of those that a mesh axis runs over, the one named last changes fastest.
Arguments:
- root_inverse: float32 [8, 256, 4, 256], P(('groups', 'node'), 'row'), parts along dimension 0
- panel_one: float32 [16, 4, 256, 256], P(('groups', 'node'), None, 'row', 'sub'), parts along dimension 0, may hold values from -0.1875 to 0.1875
- diag_one: float32 [16, 256, 256], P(('groups', 'node'), 'row', 'sub'), parts along dimension 0, may hold values from -3 to 3
- panel_two: float32 [32, 4, 256, 256], P(('groups', 'node'), None, 'row', 'sub'), parts along dimension 0, may hold values from -0.1875 to 0.1875
- diag_two: float32 [32, 256, 256], P(('groups', 'node'), 'row', 'sub'), parts along dimension 0, may hold values from -3 to 3
- ancestors: int32 [16, 4], P('groups'), parts along dimension 0, may hold values from 0 to 3, as said below
- counts: int32 [16], P('groups'), parts along dimension 0, may hold values from 1 to 4
- owners: int32 [32], P('groups'), parts along dimension 0, may hold values from 0 to 3, as said below
- slots: int32 [32], P('groups'), parts along dimension 0, may hold values from 0 to 1
- offsets: int32 [32, 3], P('groups'), parts along dimension 0, may hold values from 0 to 3, as said below
Outputs:
- cov_panel_one: float32 [16, 4, 256, 256], P(('groups', 'node'), None, 'row', 'sub'), parts along dimension 0
- cov_diag_one: float32 [16, 256, 256], P(('groups', 'node'), 'row', 'sub'), parts along dimension 0
- cov_panel_two: float32 [32, 4, 256, 256], P(('groups', 'node'), None, 'row', 'sub'), parts along dimension 0
- cov_diag_two: float32 [32, 256, 256], P(('groups', 'node'), 'row', 'sub'), parts along dimension 0
There are 2 independent parts, one for each index of `groups`. A program takes and returns all parts, laid end to end along the dimension named above; each array names one. Nothing has to cross between parts.
Inputs may be any that keep to these rules, and one draw needn't show every extreme that they name: `ancestors`: the ids of one supernode are distinct; all 2 supernodes of one node index share their first id. `owners`: the 4 supernodes of one node index have parents on different node indices. `offsets`: distinct within a row; the first min(3, counts of the parent) entries are below that count.
All inputs are finite; a program needn't handle non-finite values.
Results may differ from a plain program's by a relative error of at most 0.0003.
Values sent between devices are 32-bit elements; how exact they have to be, the bound alone decides.
No kernel may reach another device: no remote copies, remote signals or barrier semaphores. Data moves between devices by JAX's collectives and lax.ppermute only.
A program may use at most 64 MiB of HBM per device.

v0:
```python
import jax
import jax.numpy as jnp
from jax import lax
from jax.sharding import PartitionSpec as P

A = 4


PRECISE = lax.Precision.HIGHEST


def pick_blocks(gathered, block_ids):
    return gathered[block_ids[:, :, None], :, block_ids[:, None, :]]


def apply_panel(matrix, masked):
    return jnp.einsum(
        "kabic,kbcj->kaij",
        matrix,
        lax.all_gather(masked, "row", axis=2, tiled=True),
        precision=PRECISE,
    )


def diag_update(masked, column, diagonal):
    full_cols = lax.all_gather(masked, "sub", axis=3, tiled=True)
    summed = lax.psum_scatter(
        jnp.einsum("kaij,kail->jkl", full_cols, column, precision=PRECISE),
        "row",
        scatter_dimension=0,
        tiled=True,
    )
    return diagonal - jnp.transpose(summed, (1, 0, 2))


def shards(
    root_inverse,
    panel_one,
    diag_one,
    panel_two,
    diag_two,
    ancestors,
    counts,
    owners,
    slots,
    offsets,
):
    nodes = lax.axis_size("node")
    own_index = lax.axis_index("node")
    per_one = panel_one.shape[0]
    per_two = panel_two.shape[0]
    rows_here = panel_one.shape[2]
    width = root_inverse.shape[3]
    positions = jnp.arange(A, dtype=jnp.int32)
    my_ids = lax.dynamic_slice_in_dim(ancestors, own_index * per_one, per_one, 0)
    my_counts = lax.dynamic_slice_in_dim(counts, own_index * per_one, per_one, 0)
    valid_one = (positions[None, :] < my_counts[:, None]).astype(jnp.float32)
    my_owner = lax.dynamic_slice_in_dim(owners, own_index * per_two, per_two, 0)
    my_slot = lax.dynamic_slice_in_dim(slots, own_index * per_two, per_two, 0)
    my_offsets = lax.dynamic_slice_in_dim(offsets, own_index * per_two, per_two, 0)
    my_parent = my_owner * per_one + my_slot
    parent_count = jnp.take(counts, my_parent)
    valid_two = (positions[None, :] < jnp.minimum(A, 1 + parent_count)[:, None]).astype(jnp.float32)
    gathered = lax.all_gather(root_inverse, "node", axis=0, tiled=True)
    block_one = pick_blocks(gathered, my_ids)
    parent_ids = jnp.take_along_axis(jnp.take(ancestors, my_parent, axis=0), my_offsets, axis=1)
    separator = pick_blocks(gathered, parent_ids)
    block_one = block_one * valid_one[:, :, None, None, None]
    masked_one = panel_one * valid_one[:, :, None, None]
    cov_panel_one = -apply_panel(block_one, masked_one)
    cov_diag_one = diag_update(masked_one, cov_panel_one, diag_one)
    full_cross, full_diag = (
        lax.all_gather(cov_panel_one, "sub", axis=3, tiled=True),
        lax.all_gather(cov_diag_one, "sub", axis=2, tiled=True),
    )
    owner_grid = owners.reshape(nodes, per_two)
    child_match = (owner_grid == own_index).astype(jnp.int32)
    has_child = jnp.sum(child_match, axis=1)
    child_pos = jnp.sum(child_match * jnp.arange(per_two, dtype=jnp.int32)[None, :], axis=1)
    child_index = jnp.arange(nodes, dtype=jnp.int32) * per_two + child_pos
    parent_slot = jnp.take(slots, child_index)
    parent_pos = jnp.take(offsets, child_index, axis=0)
    present = has_child.astype(jnp.float32)
    top_send = jnp.take(full_diag, parent_slot, axis=0) * present[:, None, None]
    cross_pick = jnp.take(
        full_cross.reshape(per_one * A, rows_here, width),
        parent_slot[:, None] * A + parent_pos,
        axis=0,
    )
    cross_pick = cross_pick * present[:, None, None, None]
    got_top, got_cross = (
        lax.all_to_all(top_send, "node", split_axis=0, concat_axis=0, tiled=True),
        lax.all_to_all(cross_pick, "node", split_axis=0, concat_axis=0, tiled=True),
    )
    my_cross = jnp.take(got_cross, my_owner, axis=0)
    my_lower = jnp.concatenate([my_cross[:, :, None], separator], axis=2)
    my_top = jnp.take(got_top, my_owner, axis=0)
    empty_blocks = jnp.zeros((per_two, 1, A - 1, rows_here, width), jnp.float32)
    first_row = jnp.concatenate([my_top[:, None, None], empty_blocks], axis=2)
    block_two = jnp.concatenate([first_row, my_lower], axis=1) * valid_two[:, :, None, None, None]
    masked_two = panel_two * valid_two[:, :, None, None]
    lower_part = apply_panel(block_two, masked_two)
    beside = my_lower[:, :, 0]
    further = masked_two[:, 1:]
    upper_part = lax.psum_scatter(
        jnp.einsum("ktci,ktcj->ikj", beside, further, precision=PRECISE),
        "row",
        scatter_dimension=0,
        tiled=True,
    )
    first_block = lower_part[:, 0] + jnp.transpose(upper_part, (1, 0, 2))
    cov_panel_two = -jnp.concatenate([first_block[:, None], lower_part[:, 1:]], axis=1)
    cov_diag_two = diag_update(masked_two, cov_panel_two, diag_two)
    return (cov_panel_one, cov_diag_one, cov_panel_two, cov_diag_two)


def solution(mesh):
    return jax.shard_map(
        shards,
        mesh=mesh,
        in_specs=(
            P(("groups", "node"), "row", None, None),
            P(("groups", "node"), None, "row", "sub"),
            P(("groups", "node"), "row", "sub"),
            P(("groups", "node"), None, "row", "sub"),
            P(("groups", "node"), "row", "sub"),
            P("groups", None),
            P("groups"),
            P("groups"),
            P("groups"),
            P("groups", None),
        ),
        out_specs=(
            P(("groups", "node"), None, "row", "sub"),
            P(("groups", "node"), "row", "sub"),
            P(("groups", "node"), None, "row", "sub"),
            P(("groups", "node"), "row", "sub"),
        ),
        check_vma=False,
    )
```

profile of v0, /device:TPU:18, one launch (start us, length us, event | category | flops | bytes accessed | tf_op | source)
XLA Modules:
  0.0 218.3 jit_solution(15259905522130772412)
XLA Ops:
  7.3 1.9 copy.48
  9.3 0.7 dynamic_slice.16
  10.0 0.1 compare_convert_fusion
  10.1 1.9 broadcast_multiply_fusion.1
  12.1 0.7 all-gather.11.cloned.1.call-update
  12.8 0.1 broadcast_shift-left_fusion.2
  12.9 0.1 copy.49
  13.0 0.1 copy.50
  13.1 0.1 broadcast_or_fusion.1
  13.2 0.1 reshape.335
  13.3 0.1 eq.11
  13.4 0.1 copy.53
  13.4 0.1 convert_reduce_fusion
  13.6 0.6 gather_fusion.1
  14.3 0.6 gather_fusion.4
  14.8 41.0 %all-gather.7.cloned.1.call-done = f32[4,128,4,256]{3,1,2,0:T(8,128)} async-done(((f32[1,128,4,256]{3,1,2,0:T(8,128)}), f32[4,128,4,256]{3,1,2,0:T(8,128)}) %all-gather.7.cloned.1.call-update) | async-done | bytes 2097168 | tf_op jit(solution)/shard_map/all_gather | solution.py:64
  55.8 4.4 %gather_fusion = f32[32,128,256]{2,1,0:T(8,128)} fusion(f32[4,128,4,256]{3,1,2,0:T(8,128)} %all-gather.7.cloned.1.call-done, s32[32]{0:T(128)S(1)} %reshape.335), kind=kCustom, calls=%fused_computation | custom fusion | bytes 8388864 | tf_op jit(solution)/shard_map/gather | solution.py:13
  60.2 18.3 %all-gather.9.cloned.1.call-done = f32[2,4,256,128]{3,2,1,0:T(8,128)} async-done(((f32[2,4,128,128]{3,2,1,0:T(8,128)}), f32[2,4,256,128]{3,2,1,0:T(8,128)}) %all-gather.9.cloned.1.call-update) | async-done | bytes 1048592 | tf_op jit(solution)/shard_map/all_gather | solution.py:20
  78.5 7.1 %fusion.27 = f32[2,4,128,128]{3,2,1,0:T(8,128)} fusion(f32[2,4,4,128,256]{4,3,2,1,0:T(8,128)} %bitcast.95, f32[2,4]{1,0:T(2,128)S(1)} %compare_convert_fusion, f32[2,4,256,128]{3,2,1,0:T(8,128)} %all-gather.9.cloned.1.call-done), kind=kOutput, calls=%fused_computation.34 | convolution fusion | flops 1611792384 | bytes 5767200 | tf_op jit(solution)/shard_map/kabic,kbcj->kaij/dot_general | solution.py:17
  85.7 0.1 compare_select_fusion.2
  85.7 0.1 reshape.375
  85.8 0.1 compare_and_fusion.4
  85.9 0.6 gather_fusion.9
  86.6 0.1 compare_and_fusion.1
  86.7 4.2 %all-gather.11.cloned.1.call-done = f32[2,4,128,256]{3,2,1,0:T(8,128)} async-done(((f32[2,4,128,128]{3,2,1,0:T(8,128)}), f32[2,4,128,256]{3,2,1,0:T(8,128)}) %all-gather.11.cloned.1.call-update) | async-done | bytes 1048592 | tf_op jit(solution)/shard_map/all_gather | solution.py:26
  90.8 3.1 %convolution_bitcast_fusion.1 = f32[256,2,128]{0,2,1:T(8,128)} fusion(f32[2,4,128,128]{3,2,1,0:T(8,128)} %fusion.27, f32[2,4,128,256]{3,2,1,0:T(8,128)} %all-gather.11.cloned.1.call-done), kind=kOutput, calls=%fused_computation.35 | convolution fusion | flops 402653184 | bytes 1835008 | tf_op jit(solution)/shard_map/kaij,kail->jkl/dot_general | solution.py:28
  94.0 9.0 %all-gather.13.cloned.1.call-done = f32[2,4,128,256]{3,2,1,0:T(8,128)} async-done(((f32[2,4,128,128]{3,2,1,0:T(8,128)}), f32[2,4,128,256]{3,2,1,0:T(8,128)}) %all-gather.13.cloned.1.call-update) | async-done | bytes 1048592 | tf_op jit(solution)/shard_map/all_gather | solution.py:73
  103.0 1.9 gather_fusion.5
  104.9 1.4 select_multiply_fusion
  106.3 5.2 %all-to-all-start.1 = ((f32[4,3,128,256]{3,2,1,0:T(8,128)}), f32[4,3,128,256]{3,2,1,0:T(8,128)}, u32[]{:S(2)}, u32[]{:S(2)}) async-start(f32[4,3,128,256]{3,2,1,0:T(8,128)} %select_multiply_fusion), calls=%async_computation.2 | async-start | bytes 3145728 | tf_op jit(solution)/shard_map/all_to_all | solution.py:93
  111.6 1.2 broadcast_multiply_fusion
  112.9 32.8 %all-to-all-done.1 = f32[4,3,128,256]{3,2,1,0:T(8,128)} async-done(((f32[4,3,128,256]{3,2,1,0:T(8,128)}), f32[4,3,128,256]{3,2,1,0:T(8,128)}, u32[]{:S(2)}, u32[]{:S(2)}) %all-to-all-start.1) | async-done | bytes 1572896 | tf_op jit(solution)/shard_map/all_to_all | solution.py:93
  145.6 2.1 gather_fusion.6
  147.7 3.5 %fusion.21 = f32[256,4,128]{2,0,1:T(8,128)} fusion(f32[4,4,128,128]{3,2,1,0:T(8,128)S(1)} %copy-done.3, f32[4,3,128,256]{3,2,1,0:T(8,128)S(1)} %gather_fusion.6, pred[4]{0:T(512)(128)(4,1)S(1)} %get-tuple-element.24), kind=kOutput, calls=%fused_computation.31 | convolution fusion | flops 604372992 | bytes 3145732 | tf_op jit(solution)/shard_map/ktci,ktcj->ikj/dot_general | solution.py:106
  151.3 0.7 all-gather.17.cloned.1.call-update
  152.1 0.1 copy.55
  152.2 0.1 copy.52
  152.3 0.6 gather_fusion.7
  152.9 0.1 reshape.411
  153.0 0.9 bitcast_subtract_fusion.1
  153.9 2.0 all_gather.24
  155.9 0.6 gather_fusion.2
  156.5 0.9 select_multiply_fusion.1
  157.4 6.8 %all-to-all-start = ((f32[4,128,256]{1,2,0:T(8,128)}), f32[4,128,256]{1,2,0:T(8,128)S(1)}, u32[]{:S(2)}, u32[]{:S(2)}) async-start(f32[4,128,256]{1,2,0:T(8,128)} %select_multiply_fusion.1), calls=%async_computation.1 | async-start | bytes 1048576 | tf_op jit(solution)/shard_map/all_to_all | solution.py:92
  164.2 0.1 broadcast_select_fusion
  164.3 0.7 gather_fusion.10
  165.0 0.1 reshape.414
  165.1 0.1 broadcast_or_fusion
  165.2 0.1 reshape.397
  165.3 3.2 %gather_fusion.8 = f32[36,128,256]{2,1,0:T(8,128)} fusion(f32[4,128,4,256]{3,1,2,0:T(8,128)S(1)} %copy-done.2, s32[36]{0:T(128)S(1)} %reshape.397), kind=kCustom, calls=%fused_computation.8 | custom fusion | bytes 9437472 | tf_op jit(solution)/shard_map/gather | solution.py:13
  168.6 7.5 %all-to-all-done = f32[4,128,256]{1,2,0:T(8,128)S(1)} async-done(((f32[4,128,256]{1,2,0:T(8,128)}), f32[4,128,256]{1,2,0:T(8,128)S(1)}, u32[]{:S(2)}, u32[]{:S(2)}) %all-to-all-start) | async-done | bytes 524320 | tf_op jit(solution)/shard_map/all_to_all | solution.py:92
  176.0 0.6 gather_fusion.3
  176.6 0.1 bitcast_select_fusion.1
  176.7 1.0 copy.76
  177.7 0.2 bitcast_select_fusion
  178.0 10.5 %fusion.16 = f32[4,4,128,128]{3,2,1,0:T(8,128)S(1)} fusion(f32[4,4,256,128]{3,2,1,0:T(8,128)} %all-gather.15.cloned.1.call-done, f32[4,1,1,128,256]{4,3,2,1,0:T(8,128)} %copy.76, f32[4,3,3,128,256]{4,3,2,1,0:T(8,128)} %bitcast.97, f32[4,3,1,128,256]{4,3,2,1,0:T(8,128)S(1)} %bitcast_select_fusion, f32[4,4]{1,0:T(4,128)S(1)} %fusion.38), kind=kOutput, calls=%fused_computation.30 | convolution fusion | flops 3231711232 | bytes 9961536 | tf_op jit(solution)/shard_map/kabic,kbcj->kaij/dot_general | solution.py:17
  188.5 1.0 fusion.34
  189.5 0.1 maximum_negate_fusion
  189.7 4.7 %convolution_bitcast_fusion = f32[256,4,128]{0,2,1:T(8,128)} fusion(f32[4,4,128,128]{3,2,1,0:T(8,128)S(1)} %maximum_negate_fusion, f32[4,4,128,256]{3,2,1,0:T(8,128)} %all-gather.17.cloned.1.call-done), kind=kOutput, calls=%fused_computation.32 | convolution fusion | flops 805306368 | bytes 3670016 | tf_op jit(solution)/shard_map/kaij,kail->jkl/dot_general | solution.py:28
  194.4 0.1 copy.61
  194.5 0.8 copy.62
  195.3 14.7 %reduce-scatter.8.cloned.1.call-done = f32[128,4,128]{0,2,1:T(8,128)} async-done(((f32[256,4,128]{0,2,1:T(8,128)}), f32[128,4,128]{0,2,1:T(8,128)}) %reduce-scatter.8.cloned.1.call-update) | async-done | bytes 262160 | tf_op jit(solution)/shard_map/reduce_scatter | solution.py:27
  209.9 1.0 bitcast_subtract_fusion
  210.9 0.8 copy.63
  (63 shorter events, 0.8 us)
Async XLA Ops:
  7.2 5.7 %copy-start.10 = (s32[8,4]{0,1:T(4,128)S(1)}, s32[8,4]{0,1:T(4,128)}, u32[]{:S(2)}) copy-start(s32[8,4]{0,1:T(4,128)} %param.15) | copy-start | bytes 388
  7.2 6.0 %copy-start.12 = (s32[16]{0:T(128)S(1)}, s32[16]{0:T(128)}, u32[]{:S(2)}) copy-start(s32[16]{0:T(128)} %param.17) | copy-start | bytes 196
  7.2 6.2 %copy-start.11 = (s32[16,3]{0,1:T(4,128)S(1)}, s32[16,3]{0,1:T(4,128)}, u32[]{:S(2)}) copy-start(s32[16,3]{0,1:T(4,128)} %param.19) | copy-start | bytes 580
  7.2 6.4 %copy-start = (s32[16]{0:T(128)S(1)}, s32[16]{0:T(128)}, u32[]{:S(2)}) copy-start(s32[16]{0:T(128)} %param.18) | copy-start | bytes 196
  7.2 48.6 %all-gather.7.cloned.1.call-start = ((), (), s32[]{:S(2)}) async-start(), calls=%async_computation.5 | async-start | bytes 2621440 | tf_op jit(solution)/shard_map/all_gather | solution.py:64
  9.2 69.2 %all-gather.9.cloned.1.call-start = ((), (), s32[]{:S(2)}) async-start(), calls=%async_computation.6 | async-start | bytes 1572864 | tf_op jit(solution)/shard_map/all_gather | solution.py:20
  12.0 78.8 %all-gather.11.cloned.1.call-start = ((), (), s32[]{:S(2)}) async-start(), calls=%async_computation.7 | async-start | bytes 1572864 | tf_op jit(solution)/shard_map/all_gather | solution.py:26
  12.8 90.2 %all-gather.13.cloned.1.call-start = ((), (), s32[]{:S(2)}) async-start(), calls=%async_computation.9 | async-start | bytes 1572864 | tf_op jit(solution)/shard_map/all_gather | solution.py:73
  78.5 7.5 %copy-start.1 = (s32[8]{0:T(128)S(1)}, s32[8]{0:T(128)}, u32[]{:S(2)}) copy-start(s32[8]{0:T(128)} %param.16) | copy-start | bytes 100
  85.6 67.4 %reduce-scatter.4.cloned.1.call-start = ((), (), s32[]{:S(2)}) async-start(), calls=%async_computation.8 | async-start | bytes 393216 | tf_op jit(solution)/shard_map/reduce_scatter | solution.py:27
  106.3 5.3 %copy-start.7 = (f32[4,4,128,128]{3,2,1,0:T(8,128)S(1)}, f32[4,4,128,128]{3,2,1,0:T(8,128)}, u32[]{:S(2)}) copy-start(f32[4,4,128,128]{3,2,1,0:T(8,128)} %param.13) | copy-start | bytes 3145732
  106.3 39.4 %all-to-all-start.1 = ((f32[4,3,128,256]{3,2,1,0:T(8,128)}), f32[4,3,128,256]{3,2,1,0:T(8,128)}, u32[]{:S(2)}, u32[]{:S(2)}) async-start(f32[4,3,128,256]{3,2,1,0:T(8,128)} %select_multiply_fusion), calls=%async_computation.2 | async-start | bytes 3145728 | tf_op jit(solution)/shard_map/all_to_all | solution.py:93
  111.5 66.5 %all-gather.15.cloned.1.call-start = ((), (), s32[]{:S(2)}) async-start(), calls=%async_computation.10 | async-start | bytes 3145728 | tf_op jit(solution)/shard_map/all_gather | solution.py:20
  112.8 34.9 %copy-start.3 = (f32[4,4,128,128]{3,2,1,0:T(8,128)S(1)}, f32[4,4,128,128]{3,2,1,0:T(8,128)}, u32[]{:S(2)}) copy-start(f32[4,4,128,128]{3,2,1,0:T(8,128)} %broadcast_multiply_fusion) | copy-start | bytes 3145732
  112.8 75.7 %reduce-scatter.6.cloned.1.call-start = ((), (), s32[]{:S(2)}) async-start(), calls=%async_computation.11 | async-start | bytes 786432 | tf_op jit(solution)/shard_map/reduce_scatter | solution.py:105
  147.7 4.4 %copy-start.4 = (f32[4,3,128,256]{3,2,1,0:T(8,128)}, f32[4,3,128,256]{3,2,1,0:T(8,128)S(1)}, u32[]{:S(2)}) copy-start(f32[4,3,128,256]{3,2,1,0:T(8,128)S(1)} %gather_fusion.6) | copy-start | bytes 4718596
  147.7 4.5 %copy-start.9 = (f32[2,128,128]{2,1,0:T(8,128)S(1)}, f32[2,128,128]{2,1,0:T(8,128)}, u32[]{:S(2)}) copy-start(f32[2,128,128]{2,1,0:T(8,128)} %param.12) | copy-start | bytes 393220
  151.3 38.4 %all-gather.17.cloned.1.call-start = ((), (), s32[]{:S(2)}) async-start(), calls=%async_computation.12 | async-start | bytes 3145728 | tf_op jit(solution)/shard_map/all_gather | solution.py:26
  156.5 8.8 %copy-start.2 = (f32[4,128,4,256]{3,1,2,0:T(8,128)S(1)}, f32[4,128,4,256]{3,1,2,0:T(8,128)}, u32[]{:S(2)}) copy-start(f32[4,128,4,256]{3,1,2,0:T(8,128)} %all-gather.7.cloned.1.call-done) | copy-start | bytes 6291460
  157.4 18.6 %all-to-all-start = ((f32[4,128,256]{1,2,0:T(8,128)}), f32[4,128,256]{1,2,0:T(8,128)S(1)}, u32[]{:S(2)}, u32[]{:S(2)}) async-start(f32[4,128,256]{1,2,0:T(8,128)} %select_multiply_fusion.1), calls=%async_computation.1 | async-start | bytes 1048576 | tf_op jit(solution)/shard_map/all_to_all | solution.py:92
  164.2 45.7 %reduce-scatter.8.cloned.1.call-start = ((), (), s32[]{:S(2)}) async-start(), calls=%async_computation.13 | async-start | bytes 786432 | tf_op jit(solution)/shard_map/reduce_scatter | solution.py:27
  168.5 9.2 %copy-start.5 = (f32[4,3,128,256]{3,2,1,0:T(8,128)S(1)}, f32[4,3,128,256]{3,2,1,0:T(8,128)}, u32[]{:S(2)}) copy-start(f32[4,3,128,256]{3,2,1,0:T(8,128)} %copy-done.4) | copy-start | bytes 4718596
  189.6 4.7 %copy-start.6 = (f32[4,4,128,128]{3,2,1,0:T(8,128)}, f32[4,4,128,128]{3,2,1,0:T(8,128)S(1)}, u32[]{:S(2)}) copy-start(f32[4,4,128,128]{3,2,1,0:T(8,128)S(1)} %maximum_negate_fusion) | copy-start | bytes 3145732
  189.6 4.7 %copy-start.8 = (f32[4,128,128]{2,1,0:T(8,128)S(1)}, f32[4,128,128]{2,1,0:T(8,128)}, u32[]{:S(2)}) copy-start(f32[4,128,128]{2,1,0:T(8,128)} %param.14) | copy-start | bytes 786436
Sparse Core Ops, SparseCore 0:
  10.2 45.6 all-gather.6
  58.0 20.4 all-gather.8
  80.6 10.1 all-gather.10
  92.8 10.1 all-gather.12
  105.6 11.6 reduce-scatter.3
  118.8 33.1 all-gather.14
  154.3 14.5 reduce-scatter.5
  170.4 11.5 all-gather.16
  194.5 15.4 reduce-scatter.7
where the time goes:
time: 221 us; the launch traced here: 218 us
  waiting for transfers between devices  129 us (58%)
  matrix products  28.9 us (13%)
  local copies, waits for them, and re-layouts  22.3 us (10%)
  between operations  14.2 us (6%)
  starting transfers between devices  12.4 us (6%)
  other arithmetic  9.65 us (4%)
    all_gather x1, waiting for transfers between devices, shards(): gathered = lax.all_gather(root_inverse, 'node', axis=0, tiled=True)  41 us
    all_to_all x1, waiting for transfers between devices, shards(): lax.all_to_all(cross_pick, 'node', split_axis=0, concat_axis=0, tiled=True)  32.8 us
    all_gather x2, waiting for transfers between devices, apply_panel(): lax.all_gather(masked, 'row', axis=2, tiled=True)  18.3 us
    dot_general x2, matrix products, apply_panel(): jnp.einsum('kabic,kbcj->kaij', matrix, lax.all_gather(masked, 'row', axis...  17.6 us
    reduce_scatter x2, waiting for transfers between devices, diag_update(): lax.psum_scatter(jnp.einsum('kaij,kail->jkl', full_cols, column, precisio...  14.7 us
    all_gather x1, waiting for transfers between devices, shards(): lax.all_gather(cov_panel_one, 'sub', axis=3, tiled=True)  9.02 us
    dot_general x2, matrix products, diag_update(): jnp.einsum('kaij,kail->jkl', full_cols, column, precision=PRECISE)  7.81 us
    gather x2, local copies, waits for them, and re-layouts, pick_blocks(): return gathered[block_ids[:, :, None], :, block_ids[:, None, :]]  7.61 us
  transfers between devices with their start and end apart: 11, of which 7 were waited for; matrix products, arithmetic and copies ran while one was open for 24% of the time, Pallas kernels for 0%

commit v1 on v0

--- a/solution.py
+++ b/solution.py
@@ -1,12 +1,333 @@
+import functools
+
 import jax
 import jax.numpy as jnp
 from jax import lax
+from jax.experimental import pallas as pl
+from jax.experimental.pallas import tpu as pltpu
 from jax.sharding import PartitionSpec as P
 
 A = 4
 
 
 PRECISE = lax.Precision.HIGHEST
+THREE_PASS = lax.Precision.HIGH
+F32 = jnp.float32
+SMEM = pl.BlockSpec(memory_space=pltpu.SMEM)
+VMEM = pl.BlockSpec(memory_space=pltpu.VMEM)
+
+
+def mm(a, b):
+    return jnp.dot(a, b, precision=THREE_PASS, preferred_element_type=F32)
+
+
+def mm_t(a, b):
+    return lax.dot_general(
+        a, b, (((0,), (0,)), ((), ())), precision=THREE_PASS, preferred_element_type=F32
+    )
+
+
+def call(body, out_shapes, operands, n_smem, scratch=(), aliases=None, flops=0):
+    size = sum(4 * o.size for o in operands) + sum(4 * o.size for o in out_shapes)
+    return pl.pallas_call(
+        body,
+        out_shape=tuple(out_shapes),
+        in_specs=[SMEM] * n_smem + [VMEM] * (len(operands) - n_smem),
+        out_specs=tuple([VMEM] * len(out_shapes)),
+        scratch_shapes=list(scratch),
+        input_output_aliases=aliases or {},
+        compiler_params=pltpu.CompilerParams(vmem_limit_bytes=40 * 1024 * 1024),
+        cost_estimate=pl.CostEstimate(flops=flops, bytes_accessed=size, transcendentals=0),
+    )(*operands)
+
+
+def find_child(owners, node, owner, per_two):
+    found = jnp.int32(0)
+    for c in range(per_two):
+        found = jnp.where(owners[node * per_two + c] == owner, c, found)
+    return found
+
+
+def spot(index, size):
+    return pl.ds(pl.multiple_of(index * size, size), size)
+
+
+def level_one_kernel(nodes, place, ids, counts, owners, slots, offsets, *refs):
+    shifts = nodes - 1
+    root = refs[0]
+    far = refs[1 : 1 + shifts]
+    near = refs[1 + shifts : 1 + 2 * shifts]
+    own, beside, across = refs[1 + 2 * shifts : 4 + 2 * shifts]
+    outs = refs[4 + 2 * shifts :]
+    whole, cov, keep, send = outs[:4]
+    picks = outs[4 : 4 + nodes]
+    spread, wide, tall, part = outs[4 + nodes :]
+    me, row, sub = place[0], place[1], place[2]
+    per_one, a_count, rows, cols = own.shape
+    half = rows // 2
+    width = root.shape[2]
+    blocks = root.shape[1]
+    for b in range(blocks):
+        whole[spot(me, rows), b * width : (b + 1) * width] = root[:, b, :]
+    for k in range(1, nodes):
+        block = lax.rem(me - k + nodes, nodes)
+        for b in range(blocks):
+            lanes = slice(b * width, (b + 1) * width)
+            whole[spot(block * 2 + sub, half), lanes] = far[k - 1][:, b, :]
+            whole[spot(block * 2 + 1 - sub, half), lanes] = near[k - 1][:, b, :]
+    for g in range(per_one):
+        for a in range(a_count):
+            at = ids[me * per_one + g, a]
+            valid = (a < counts[me * per_one + g]).astype(F32)
+            lanes = slice(g * cols, (g + 1) * cols)
+            spread[spot(at * 2 + row, rows), lanes] = own[g, a] * valid
+            spread[spot(at * 2 + 1 - row, rows), lanes] = beside[g, a] * valid
+    total = mm(whole[...], spread[...])
+    for g in range(per_one):
+        tall[g] = total[:, g * cols : (g + 1) * cols]
+    for g in range(per_one):
+        for a in range(a_count):
+            at = ids[me * per_one + g, a]
+            valid = (a < counts[me * per_one + g]).astype(F32)
+            cov[g, a] = tall[g, spot(at, rows), :] * (-valid)
+            wide[a * rows : (a + 1) * rows, spot(sub, cols)] = own[g, a] * valid
+            wide[a * rows : (a + 1) * rows, spot(1 - sub, cols)] = across[g, a] * valid
+        part[...] = -mm_t(wide[...], cov[g].reshape(a_count * rows, cols))
+        keep[g] = part[spot(row, rows), :]
+        send[g] = part[spot(1 - row, rows), :]
+    per_two = owners.shape[0] // nodes
+    for k in range(nodes):
+        target = lax.rem(me + k, nodes)
+        child = target * per_two + find_child(owners, target, me, per_two)
+        for t in range(a_count - 1):
+            picks[k][t] = cov[slots[child], offsets[child, t]]
+
+
+def diag_one_kernel(nodes, place, owners, slots, diagonal, keep, got, *outs):
+    me = place[0]
+    outs[0][...] = diagonal[...] + (keep[...] + got[...])
+    per_two = owners.shape[0] // nodes
+    for k in range(nodes):
+        target = lax.rem(me + k, nodes)
+        child = target * per_two + find_child(owners, target, me, per_two)
+        outs[1 + k][...] = outs[0][slots[child]]
+
+
+def parent_facts(me, h, ids, counts, owners, slots, offsets, per_one, per_two):
+    child = me * per_two + h
+    parent = owners[child] * per_one + slots[child]
+    count = counts[parent]
+    valid = [(t < 1 + count).astype(F32) for t in range(A)]
+    blocks = [ids[parent, offsets[child, t]] for t in range(A - 1)]
+    return valid, blocks
+
+
+def root_two_kernel(per_one, place, ids, counts, owners, slots, offsets, whole, own, beside, across, lower, inner, spread, wide, tall):
+    me, row, sub = place[0], place[1], place[2]
+    per_two, a_count, rows, cols = own.shape
+    spread[...] = jnp.zeros_like(spread)
+    for h in range(per_two):
+        valid, at = parent_facts(me, h, ids, counts, owners, slots, offsets, per_one, per_two)
+        lanes = slice(h * cols, (h + 1) * cols)
+        for t in range(1, a_count):
+            spread[spot(at[t - 1] * 2 + row, rows), lanes] = own[h, t] * valid[t]
+            spread[spot(at[t - 1] * 2 + 1 - row, rows), lanes] = beside[h, t] * valid[t]
+    total = mm(whole[...], spread[...])
+    for h in range(per_two):
+        tall[h] = total[:, h * cols : (h + 1) * cols]
+    for h in range(per_two):
+        valid, at = parent_facts(me, h, ids, counts, owners, slots, offsets, per_one, per_two)
+        for t in range(1, a_count):
+            lower[h, t - 1] = tall[h, spot(at[t - 1], rows), :] * valid[t]
+            wide[(t - 1) * rows : t * rows, spot(sub, cols)] = own[h, t] * valid[t]
+            wide[(t - 1) * rows : t * rows, spot(1 - sub, cols)] = across[h, t] * valid[t]
+        inner[h] = mm_t(wide[...], lower[h].reshape((a_count - 1) * rows, cols))
+
+
+def parent_two_kernel(nodes, per_one, shifts, chained, place, ids, counts, owners, slots, offsets, own, beside, across, corner, lower, inner, diagonal, *refs):
+    me, row, sub = place[0], place[1], place[2]
+    per_two, a_count, rows, cols = own.shape
+    refs = list(refs)
+    ins = [refs[4 * i : 4 * i + 4] for i in range(len(shifts))]
+    refs = refs[4 * len(shifts) :]
+    if chained:
+        refs = refs[2:]
+    panel, diag = refs[:2]
+    sends = refs[2 : 2 + len(shifts)]
+    cross, top, first, local, wide, part, more = refs[2 + len(shifts) :]
+    low = (a_count - 1) * rows
+    for i, k in enumerate(shifts):
+        cross_own, cross_side, top_own, top_side = ins[i]
+        source = lax.rem(me - k + nodes, nodes)
+        h = find_child(owners, me, source, per_two)
+        valid, _ = parent_facts(me, h, ids, counts, owners, slots, offsets, per_one, per_two)
+        for t in range(1, a_count):
+            span = slice((t - 1) * rows, t * rows)
+            cross[span, spot(sub, cols)] = cross_own[t - 1]
+            cross[span, spot(1 - sub, cols)] = cross_side[t - 1]
+            local[span, :] = own[h, t] * valid[t]
+            wide[span, spot(sub, cols)] = own[h, t] * valid[t]
+            wide[span, spot(1 - sub, cols)] = across[h, t] * valid[t]
+        top[:, spot(sub, cols)] = top_own[...]
+        top[:, spot(1 - sub, cols)] = top_side[...]
+        first[spot(row, rows), :] = own[h, 0]
+        first[spot(1 - row, rows), :] = beside[h, 0]
+        mine, other = low + row * rows, low + (1 - row) * rows
+        mine, other = pl.multiple_of(mine, rows), pl.multiple_of(other, rows)
+        wide[pl.ds(mine, rows), spot(sub, cols)] = own[h, 0]
+        wide[pl.ds(mine, rows), spot(1 - sub, cols)] = across[h, 0]
+        wide[pl.ds(other, rows), spot(sub, cols)] = beside[h, 0]
+        wide[pl.ds(other, rows), spot(1 - sub, cols)] = corner[h]
+        below = mm(cross[...], first[...])
+        for t in range(1, a_count):
+            span = slice((t - 1) * rows, t * rows)
+            part[span, :] = below[span, :] * valid[t]
+            panel[h, t] = -(lower[h, t - 1] + part[span, :])
+        part[low:, :] = mm_t(cross[...], local[...])
+        part[pl.ds(mine, rows), :] += mm(top[...], first[...])
+        more[...] = inner[h] + mm_t(wide[...], part[...])
+        panel[h, 0] = -part[pl.ds(mine, rows), :]
+        sends[i][0] = part[pl.ds(other, rows), :]
+        diag[h] = diagonal[h] + more[spot(row, rows), :]
+        sends[i][1] = more[spot(1 - row, rows), :]
+
+
+def finish_kernel(nodes, place, owners, *refs):
+    me = place[0]
+    per_two = owners.shape[0] // nodes
+    got = refs[:nodes]
+    panel, diag, panel_out, diag_out = refs[nodes:]
+    for k in range(nodes):
+        h = find_child(owners, me, lax.rem(me - k + nodes, nodes), per_two)
+        panel_out[h, 0] = panel[h, 0] - got[k][0]
+        diag_out[h] = diag[h] + got[k][1]
+
+
+def shift(x, axis, k):
+    n = lax.axis_size(axis)
+    return lax.ppermute(x, axis, [(i, (i + k) % n) for i in range(n)])
+
+
+def paired_shards(root_inverse, panel_one, diag_one, panel_two, diag_two, ancestors, counts, owners, slots, offsets):
+    nodes = lax.axis_size("node")
+    me, row, sub = lax.axis_index("node"), lax.axis_index("row"), lax.axis_index("sub")
+    place = jnp.stack([me, row, sub]).astype(jnp.int32)
+    per_one, a_count, rows, cols = panel_one.shape
+    per_two = panel_two.shape[0]
+    width = root_inverse.shape[3]
+    full = root_inverse.shape[2] * width
+    root = root_inverse[0]
+    half = lax.dynamic_slice_in_dim(root, sub * (rows // 2), rows // 2, 0)
+    far = [shift(half, "node", k) for k in range(1, nodes)]
+    near = [shift(x, "sub", 1) for x in far]
+    beside_one = shift(panel_one, "row", 1)
+    across_one = shift(panel_one, "sub", 1)
+    beside_two = shift(panel_two, "row", 1)
+    across_two = shift(panel_two, "sub", 1)
+    corner_two = shift(beside_two[:, 0], "sub", 1)
+    S = lambda *shape: jax.ShapeDtypeStruct(shape, F32)
+    tables = [place, ancestors, counts, owners, slots, offsets]
+
+    out = call(
+        functools.partial(level_one_kernel, nodes),
+        [S(rows * nodes, full), S(*panel_one.shape), S(per_one, rows, cols), S(per_one, rows, cols)]
+        + [S(a_count - 1, rows, cols)] * nodes,
+        tables + [root] + far + near + [panel_one, beside_one, across_one],
+        len(tables),
+        [
+            pltpu.VMEM((full, per_one * cols), F32),
+            pltpu.VMEM((a_count * rows, 2 * cols), F32),
+            pltpu.VMEM((per_one, rows * nodes, cols), F32),
+            pltpu.VMEM((2 * rows, cols), F32),
+        ],
+        flops=6 * rows * nodes * full * per_one * cols,
+    )
+    whole, cov_panel_one, keep, send = out[:4]
+    picks = out[4:]
+    got_cross = [picks[0]] + [shift(picks[k], "node", k) for k in range(1, nodes)]
+    cross_side = [shift(x, "sub", 1) for x in got_cross]
+    got_diag = shift(send, "row", 1)
+    out = call(
+        functools.partial(diag_one_kernel, nodes),
+        [S(*diag_one.shape)] + [S(rows, cols)] * nodes,
+        [place, owners, slots, diag_one, keep, got_diag],
+        3,
+    )
+    cov_diag_one = out[0]
+    got_top = [out[1]] + [shift(out[1 + k], "node", k) for k in range(1, nodes)]
+    top_side = [shift(x, "sub", 1) for x in got_top]
+
+    lower, inner = call(
+        functools.partial(root_two_kernel, per_one),
+        [S(per_two, a_count - 1, rows, cols), S(per_two, 2 * rows, cols)],
+        tables + [whole, panel_two, beside_two, across_two],
+        len(tables),
+        [
+            pltpu.VMEM((full, per_two * cols), F32),
+            pltpu.VMEM(((a_count - 1) * rows, 2 * cols), F32),
+            pltpu.VMEM((per_two, rows * nodes, cols), F32),
+        ],
+        flops=6 * rows * nodes * full * per_two * cols,
+    )
+
+    low = (a_count - 1) * rows
+    groups = [tuple(range(nodes))]
+    sends = {}
+    state = ()
+    for ks in groups:
+        arrived = []
+        for k in ks:
+            arrived += [got_cross[k], cross_side[k], got_top[k], top_side[k]]
+        operands = (
+            tables
+            + [panel_two, beside_two, across_two, corner_two, lower, inner, diag_two]
+            + arrived
+            + list(state)
+        )
+        n = len(operands)
+        out = call(
+            functools.partial(parent_two_kernel, nodes, per_one, ks, bool(state)),
+            [S(*panel_two.shape), S(*diag_two.shape)] + [S(2, rows, cols)] * len(ks),
+            operands,
+            len(tables),
+            [
+                pltpu.VMEM((low, 2 * cols), F32),
+                pltpu.VMEM((rows, 2 * cols), F32),
+                pltpu.VMEM((2 * rows, cols), F32),
+                pltpu.VMEM((low, cols), F32),
+                pltpu.VMEM((low + 2 * rows, 2 * cols), F32),
+                pltpu.VMEM((low + 2 * rows, cols), F32),
+                pltpu.VMEM((2 * rows, cols), F32),
+            ],
+            aliases={n - 2: 0, n - 1: 1} if state else None,
+            flops=6 * len(ks) * 6 * low * cols * 2 * cols,
+        )
+        state = out[:2]
+        for k, x in zip(ks, out[2:]):
+            sends[k] = x
+    got = [shift(sends[k], "row", 1) for k in range(nodes)]
+    cov_panel_two, cov_diag_two = finish(nodes, place, owners, got, *state)
+    return (cov_panel_one, cov_diag_one, cov_panel_two, cov_diag_two)
+
+
+def finish(nodes, place, owners, got, panel, diag):
+    per_two, _, rows, cols = panel.shape
+    firsts = pl.BlockSpec((per_two, 1, rows, cols), lambda i: (0, 0, 0, 0))
+    whole = pl.BlockSpec(diag.shape, lambda i: (0, 0, 0))
+    n = 2 + nodes
+    return pl.pallas_call(
+        functools.partial(finish_kernel, nodes),
+        grid=(1,),
+        out_shape=(
+            jax.ShapeDtypeStruct(panel.shape, F32),
+            jax.ShapeDtypeStruct(diag.shape, F32),
+        ),
+        in_specs=[SMEM] * 2 + [VMEM] * nodes + [firsts, whole],
+        out_specs=(firsts, whole),
+        input_output_aliases={n: 0, n + 1: 1},
+        compiler_params=pltpu.CompilerParams(vmem_limit_bytes=16 * 1024 * 1024),
+        cost_estimate=pl.CostEstimate(flops=0, bytes_accessed=3 * 8 * diag.size, transcendentals=0),
+    )(place, owners, *got, panel, diag)
 
 
 def pick_blocks(gathered, block_ids):
@@ -33,7 +354,7 @@
     return diagonal - jnp.transpose(summed, (1, 0, 2))
 
 
-def shards(
+def general_shards(
     root_inverse,
     panel_one,
     diag_one,
@@ -114,6 +435,14 @@
     return (cov_panel_one, cov_diag_one, cov_panel_two, cov_diag_two)
 
 
+def shards(*args):
+    sizes = lax.axis_size("node"), lax.axis_size("row"), lax.axis_size("sub")
+    root, panel_one, panel_two = args[0], args[1], args[3]
+    if panel_two.shape[0] == sizes[0] == root.shape[2] and sizes[1:] == (2, 2) and root.shape[0] == 1 and panel_one.shape[1] == A:
+        return paired_shards(*args)
+    return general_shards(*args)
+
+
 def solution(mesh):
     return jax.shard_map(
         shards,

time: 221 us -> 112 us (0.51)
  waiting for transfers between devices: 129 us -> 61.9 us
  matrix products: 28.9 us -> 0 us
  Pallas kernels: 0 us -> 17 us
  between operations: 14.2 us -> 0.84 us
  other arithmetic: 9.65 us -> 0.08 us
  local copies, waits for them, and re-layouts: 22.3 us -> 12.9 us
  starting transfers between devices: 12.4 us -> 18 us
    all_gather x6 -> x0, waiting for transfers between devices: 72.5 us -> none  [the longest x1 41 us: shards(): gathered = lax.all_gather(root_inverse, 'node', axis=0, tiled=True)]
    ppermute x0 -> x30, waiting for transfers between devices: none -> 61.9 us  [shift(): return lax.ppermute(x, axis, [(i, (i + k) % n) for i in range(n)])]
    all_to_all x2 -> x0, waiting for transfers between devices: 40.2 us -> none  [the longest x1 32.8 us: shards(): lax.all_to_all(cross_pick, 'node', split_axis=0, concat_axis=0, tiled=True)]
    dot_general x5 -> x0, matrix products: 28.9 us -> none  [the longest x2 17.6 us: apply_panel(): jnp.einsum('kabic,kbcj->kaij', matrix, lax.all_gather(masked, 'row', axis...]
    ppermute x0 -> x30, starting transfers between devices: none -> 18 us  [shift(): return lax.ppermute(x, axis, [(i, (i + k) % n) for i in range(n)])]
    pallas_call x0 -> x5, Pallas kernels: none -> 17 us  [the longest x4 15.1 us: call(): pl.pallas_call(body, out_shape=tuple(out_shapes), in_specs=[SMEM] * n_sme...]
    gather x13 -> x0, local copies, waits for them, and re-layouts: 16 us -> none  [the longest x2 7.61 us: pick_blocks(): return gathered[block_ids[:, :, None], :, block_ids[:, None, :]]]
    reduce_scatter x3 -> x0, waiting for transfers between devices: 14.7 us -> none  [the longest x2 14.7 us: diag_update(): lax.psum_scatter(jnp.einsum('kaij,kail->jkl', full_cols, column, precisio...]
  transfers between devices with their start and end apart: 11 -> 30, of which waited for: 7 -> 11; matrix products, arithmetic and copies ran while one was open for 24% -> 5% of each run, Pallas kernels for 0% -> 9%
where the time goes in v1:
time: 112 us; the launch traced here: 111 us
  waiting for transfers between devices  61.9 us (55%)
  starting transfers between devices  18 us (16%)
  Pallas kernels  17 us (15%)
  local copies, waits for them, and re-layouts  12.9 us (12%)
    ppermute x30, waiting for transfers between devices, shift(): return lax.ppermute(x, axis, [(i, (i + k) % n) for i in range(n)])  61.9 us
    ppermute x30, starting transfers between devices, shift(): return lax.ppermute(x, axis, [(i, (i + k) % n) for i in range(n)])  18 us
    pallas_call x4, Pallas kernels, call(): pl.pallas_call(body, out_shape=tuple(out_shapes), in_specs=[SMEM] * n_sme...  15.1 us
    unnamed x35, local copies, waits for them, and re-layouts  9.48 us
  transfers between devices with their start and end apart: 30, of which 11 were waited for; matrix products, arithmetic and copies ran while one was open for 5% of the time, Pallas kernels for 9%

profile of v1, /device:TPU:18, one launch (start us, length us, event | category | flops | bytes accessed | tf_op | source)
XLA Modules:
  0.0 110.7 jit_solution(15921307894928931764)
XLA Ops:
  0.6 0.0 copy-start
  0.7 1.1 %dynamic-slice_bitcast_fusion = f32[64,4,256]{2,1,0:T(4,128)S(1)} fusion(f32[1,128,4,256]{3,2,1,0:T(4,128)} %param.10, s32[]{:T(128)S(6)} %select_n.3), kind=kLoop, calls=%fused_computation.1 | loop fusion | bytes 524292 | tf_op jit(solution)/shard_map/dynamic_slice | solution.py:220
  1.8 1.6 %collective-permute-start = (f32[64,4,256]{2,1,0:T(4,128)S(1)}, f32[64,4,256]{2,1,0:T(4,128)S(1)}, u32[]{:S(2)}, u32[]{:S(2)}) collective-permute-start(f32[64,4,256]{2,1,0:T(4,128)S(1)} %dynamic-slice_bitcast_fusion), channel_id=1, source_target_pairs={{0,4},{4,8},{8,12},{12,0},{1,5},{5,9},{9,13},{13,1},{2,6},{6,10},{... | collective-permute-start | bytes 786440 | tf_op jit(solution)/shard_map/ppermute | solution.py:208
  3.4 0.3 collective-permute-start.1
  3.8 1.3 %collective-permute-start.2 = (f32[64,4,256]{2,1,0:T(4,128)S(1)}, f32[64,4,256]{2,1,0:T(4,128)}, u32[]{:S(2)}, u32[]{:S(2)}) collective-permute-start(f32[64,4,256]{2,1,0:T(4,128)S(1)} %dynamic-slice_bitcast_fusion), channel_id=1, source_target_pairs={{0,12},{4,0},{8,4},{12,8},{1,13},{5,1},{9,5},{13,9},{2,14},{6,2},{... | collective-permute-start | bytes 786440 | tf_op jit(solution)/shard_map/ppermute | solution.py:208
  5.1 2.3 %copy.18 = f32[4,4,128,128]{3,2,0,1:T(8,128)} copy(f32[4,4,128,128]{3,2,1,0:T(8,128)} %own.3) | data formatting | bytes 2097152 | tf_op args[3]
  7.4 0.4 collective-permute-start.9
  7.8 14.4 %collective-permute-done.refs_1_ = f32[64,4,256]{2,1,0:T(4,128)S(1)} collective-permute-done((f32[64,4,256]{2,1,0:T(4,128)S(1)}, f32[64,4,256]{2,1,0:T(4,128)S(1)}, u32[]{:S(2)}, u32[]{:S(2)}) %collective-permute-start) | collective-permute-done | bytes 262176 | tf_op jit(solution)/shard_map/ppermute | solution.py:208
  22.3 0.0 collective-permute-start.3
  22.3 0.0 collective-permute-done.1.refs_2_
  22.3 0.5 collective-permute-start.4
  22.8 0.7 copy-done.4
  23.5 0.5 collective-permute-start.6
  24.0 1.6 %collective-permute-done.2.refs_3_ = f32[64,4,256]{2,1,0:T(4,128)} collective-permute-done((f32[64,4,256]{2,1,0:T(4,128)S(1)}, f32[64,4,256]{2,1,0:T(4,128)}, u32[]{:S(2)}, u32[]{:S(2)}) %collective-permute-start.2) | collective-permute-done | bytes 262176 | tf_op jit(solution)/shard_map/ppermute | solution.py:208
  25.6 0.0 collective-permute-start.7
  25.6 0.0 collective-permute-done.3.refs_4_
  25.6 0.7 copy-done.6
  26.3 0.5 collective-permute-start.10
  26.8 0.7 copy-done.8
  27.6 0.0 collective-permute-start.5
  27.6 0.1 copy.16.ids
  27.7 0.8 copy.17.offsets
  28.4 0.1 pad_add_fusion.place
  28.5 1.3 %collective-permute-done.5.refs_6_ = f32[64,4,256]{2,1,0:T(4,128)} collective-permute-done((f32[64,4,256]{2,1,0:T(4,128)}, f32[64,4,256]{2,1,0:T(4,128)}, u32[]{:S(2)}, u32[]{:S(2)}) %collective-permute-start.5) | collective-permute-done | bytes 262176 | tf_op jit(solution)/shard_map/ppermute | solution.py:208
  29.8 13.4 %collective-permute-done.6.refs_8_ = f32[2,4,128,128]{3,2,1,0:T(8,128)} collective-permute-done((f32[2,4,128,128]{3,2,1,0:T(8,128)S(1)}, f32[2,4,128,128]{3,2,1,0:T(8,128)}, u32[]{:S(2)}, u32[]{:S(2)}) %collective-permute-start.6) | collective-permute-done | bytes 524320 | tf_op jit(solution)/shard_map/ppermute | solution.py:208
  43.2 0.0 collective-permute-done.7.refs_9_
  43.2 0.0 copy-start.5
  43.2 0.9 copy-done.5
  44.2 0.9 copy-done.7
  45.1 0.9 copy-done.9
  46.1 0.7 copy-done.12
  46.7 0.7 copy-done.13
  47.4 4.5 %shard_map.129 = (f32[512,1024]{1,0:T(8,128)S(1)}, f32[2,4,128,128]{3,2,1,0:T(8,128)}, f32[2,128,128]{2,1,0:T(8,128)S(1)}, f32[2,128,128]{2,1,0:T(8,128)S(1)}, f...) custom-call(s32[3]{0:T(128)S(1)} %pad_add_fusion.place, ...), custom_call_target="tpu_custom_call" | custom-call | flops 805306368 | bytes 7340524 | tf_op jit(solution)/shard_map/pallas_call | solution.py:32
  51.9 0.0 copy-start.14
  51.9 0.6 collective-permute-start.8
  52.5 0.0 collective-permute-start.12
  52.5 0.5 collective-permute-start.14
  53.0 3.9 %collective-permute-done.8.got = f32[2,128,128]{2,1,0:T(8,128)S(1)} collective-permute-done((f32[2,128,128]{2,1,0:T(8,128)S(1)}, f32[2,128,128]{2,1,0:T(8,128)S(1)}, u32[]{:S(2)}, u32[]{:S(2)}) %collective-permute-start.8) | collective-permute-done | bytes 131104 | tf_op jit(solution)/shard_map/ppermute | solution.py:208
  56.9 1.2 %shard_map.130 = (f32[2,128,128]{2,1,0:T(8,128)}, f32[128,128]{1,0:T(8,128)S(1)}, f32[128,128]{1,0:T(8,128)S(1)}, f32[128,128]{1,0:T(8,128)S(1)}, f32[128,128]{1,0:T(8,128)S(1)}) custom-call(s32[3]{0:T(128)S(1)} %pad_add_fusion.place, s32[16]{0:T(128)S(1)} %copy-done.11, s32[16]{0:T(128)S(1)} %copy-done.12, f32[2,128,128]{2,1,0:T(8,128)S(1)} %copy-done.10, ...), custom_call_target="tpu_custom_call" | custom-call | bytes 786572 | tf_op jit(solution)/shard_map/pallas_call | solution.py:32
  58.2 2.5 %collective-permute-start.18 = (f32[3,128,128]{2,1,0:T(8,128)S(1)}, f32[3,128,128]{2,1,0:T(8,128)S(1)}, u32[]{:S(2)}, u32[]{:S(2)}) collective-permute-start(f32[3,128,128]{2,1,0:T(8,128)S(1)} %get-tuple-element.38), channel_id=1, source_target_pairs={{0,8},{4,12},{8,0},{12,4},{1,9},{5,13},{9,1},{13,5},{2,10},{6,14},... | collective-permute-start | bytes 589832 | tf_op jit(solution)/shard_map/ppermute | solution.py:208
  60.6 0.5 collective-permute-start.22
  61.1 1.6 %collective-permute-start.16 = (f32[128,128]{1,0:T(8,128)S(1)}, f32[128,128]{1,0:T(8,128)S(1)}, u32[]{:S(2)}, u32[]{:S(2)}) collective-permute-start(f32[128,128]{1,0:T(8,128)S(1)} %get-tuple-element.37), channel_id=1, source_target_pairs={{0,4},{4,8},{8,12},{12,0},{1,5},{5,9},{9,13},{13,1},{2,6},{6,10},{... | collective-permute-start | bytes 196616 | tf_op jit(solution)/shard_map/ppermute | solution.py:208
  62.7 1.4 %collective-permute-start.20 = (f32[128,128]{1,0:T(8,128)S(1)}, f32[128,128]{1,0:T(8,128)S(1)}, u32[]{:S(2)}, u32[]{:S(2)}) collective-permute-start(f32[128,128]{1,0:T(8,128)S(1)} %get-tuple-element.39), channel_id=1, source_target_pairs={{0,8},{4,12},{8,0},{12,4},{1,9},{5,13},{9,1},{13,5},{2,10},{6,14},... | collective-permute-start | bytes 196616 | tf_op jit(solution)/shard_map/ppermute | solution.py:208
  64.1 1.0 slice_bitcast_fusion
  65.0 13.7 %collective-permute-done.16.refs_6_ = f32[128,128]{1,0:T(8,128)S(1)} collective-permute-done((f32[128,128]{1,0:T(8,128)S(1)}, f32[128,128]{1,0:T(8,128)S(1)}, u32[]{:S(2)}, u32[]{:S(2)}) %collective-permute-start.16) | collective-permute-done | bytes 65568 | tf_op jit(solution)/shard_map/ppermute | solution.py:208
  78.7 0.0 collective-permute-start.24
  78.8 0.5 collective-permute-start.21
  79.3 0.1 collective-permute-start.11
  79.3 3.7 %collective-permute-done.24.refs_14_ = f32[128,128]{1,0:T(8,128)S(1)} collective-permute-done((f32[128,128]{1,0:T(8,128)S(1)}, f32[128,128]{1,0:T(8,128)S(1)}, u32[]{:S(2)}, u32[]{:S(2)}) %collective-permute-start.24) | collective-permute-done | bytes 65568 | tf_op jit(solution)/shard_map/ppermute | solution.py:208
  83.0 0.5 collective-permute-start.19
  83.5 0.1 collective-permute-start.23
  83.6 1.3 %copy.24.beside = f32[4,4,128,128]{3,2,1,0:T(8,128)S(1)} copy(f32[4,4,128,128]{3,2,0,1:T(8,128)} %collective-permute-done.9) | data formatting | bytes 2097152 | tf_op jit(solution)/shard_map/ppermute | solution.py:208
  84.9 0.5 collective-permute-start.25
  85.4 3.9 %shard_map.131 = (f32[4,3,128,128]{3,2,1,0:T(8,128)S(1)}, f32[4,256,128]{2,1,0:T(8,128)S(1)}) custom-call(s32[3]{0:T(128)S(1)} %pad_add_fusion.place, s32[8,4]{1,0:T(8,128)S(1)} %copy.16.ids, s32[8]{0:T(128)S(1)} %copy-done.14, s32[16]{0:T(128)S(1)} %copy-done.11, s32[16]{0:T(128)S(1)} %copy-done.12, s32[16,3]{1,0:T(8,128)S(1)} %copy.17.offsets, ...), custom_call_target="tpu_custom_call" | custom-call | flops 1610612736 | bytes 6554092 | tf_op jit(solution)/shard_map/pallas_call | solution.py:32
  89.3 5.5 %shard_map.132 = (f32[4,4,128,128]{3,2,1,0:T(8,128)}, f32[4,128,128]{2,1,0:T(8,128)}, f32[2,128,128]{2,1,0:T(8,128)S(1)}, f32[2,128,128]{2,1,0:T(8,128)S(1)}, f3...) custom-call(s32[3]{0:T(128)S(1)} %pad_add_fusion.place, s32[8,4]{1,0:T(8,128)S(1)} %copy.16.ids, s32[8]{0:T(128)S(1)} %copy-done.14, ...), custom_call_target="tpu_custom_call" | custom-call | flops 1811939328 | bytes 8913388 | tf_op jit(solution)/shard_map/pallas_call | solution.py:32
  94.9 0.5 collective-permute-start.26
  95.4 1.5 %collective-permute-start.27 = (f32[2,128,128]{2,1,0:T(8,128)S(1)}, f32[2,128,128]{2,1,0:T(8,128)S(1)}, u32[]{:S(2)}, u32[]{:S(2)}) collective-permute-start(f32[2,128,128]{2,1,0:T(8,128)S(1)} %get-tuple-element.43), channel_id=1, source_target_pairs={{0,2},{2,0},{1,3},{3,1},{4,6},{6,4},{5,7},{7,5},{8,10},{10,8},{9,1... | collective-permute-start | bytes 393224 | tf_op jit(solution)/shard_map/ppermute | solution.py:208
  96.9 0.5 collective-permute-start.28
  97.4 1.5 %collective-permute-start.29 = (f32[2,128,128]{2,1,0:T(8,128)S(1)}, f32[2,128,128]{2,1,0:T(8,128)S(1)}, u32[]{:S(2)}, u32[]{:S(2)}) collective-permute-start(f32[2,128,128]{2,1,0:T(8,128)S(1)} %get-tuple-element.45), channel_id=1, source_target_pairs={{0,2},{2,0},{1,3},{3,1},{4,6},{6,4},{5,7},{7,5},{8,10},{10,8},{9,1... | collective-permute-start | bytes 393224 | tf_op jit(solution)/shard_map/ppermute | solution.py:208
  98.9 2.3 %collective-permute-done.26.refs_0_ = f32[2,128,128]{2,1,0:T(8,128)S(1)} collective-permute-done((f32[2,128,128]{2,1,0:T(8,128)S(1)}, f32[2,128,128]{2,1,0:T(8,128)S(1)}, u32[]{:S(2)}, u32[]{:S(2)}) %collective-permute-start.26) | collective-permute-done | bytes 131104 | tf_op jit(solution)/shard_map/ppermute | solution.py:208
  101.2 2.8 %collective-permute-done.27.refs_1_ = f32[2,128,128]{2,1,0:T(8,128)S(1)} collective-permute-done((f32[2,128,128]{2,1,0:T(8,128)S(1)}, f32[2,128,128]{2,1,0:T(8,128)S(1)}, u32[]{:S(2)}, u32[]{:S(2)}) %collective-permute-start.27) | collective-permute-done | bytes 131104 | tf_op jit(solution)/shard_map/ppermute | solution.py:208
  104.0 2.8 %collective-permute-done.28.refs_2_ = f32[2,128,128]{2,1,0:T(8,128)S(1)} collective-permute-done((f32[2,128,128]{2,1,0:T(8,128)S(1)}, f32[2,128,128]{2,1,0:T(8,128)S(1)}, u32[]{:S(2)}, u32[]{:S(2)}) %collective-permute-start.28) | collective-permute-done | bytes 131104 | tf_op jit(solution)/shard_map/ppermute | solution.py:208
  106.8 1.9 %collective-permute-done.29.refs_3_ = f32[2,128,128]{2,1,0:T(8,128)S(1)} collective-permute-done((f32[2,128,128]{2,1,0:T(8,128)S(1)}, f32[2,128,128]{2,1,0:T(8,128)S(1)}, u32[]{:S(2)}, u32[]{:S(2)}) %collective-permute-start.29) | collective-permute-done | bytes 131104 | tf_op jit(solution)/shard_map/ppermute | solution.py:208
  108.8 1.9 %shard_map.133 = (f32[4,4,128,128]{3,2,1,0:T(8,128)}, f32[4,128,128]{2,1,0:T(8,128)}) custom-call(s32[3]{0:T(128)S(1)} %pad_add_fusion.place, s32[16]{0:T(128)S(1)} %copy-done.11, f32[2,128,128]{2,1,0:T(8,128)S(1)} %collective-permute-done.26.refs_0_, ...), custom_call_target="tpu_custom_call", output_to_operand_aliasing={{0}: (6, {}), {1}: (7, {})} | custom-call | bytes 1572864 | tf_op jit(solution)/shard_map/pallas_call | solution.py:318
  (40 shorter events, 0.1 us)
Async XLA Ops:
  0.6 42.6 %copy-start.1 = (f32[1,128,4,256]{3,2,1,0:T(4,128)S(1)}, f32[1,128,4,256]{3,2,1,0:T(4,128)}, u32[]{:S(2)}) copy-start(f32[1,128,4,256]{3,2,1,0:T(4,128)} %param.10) | copy-start | bytes 1572868
  0.6 25.7 %copy-start = (f32[4,4,128,128]{3,2,1,0:T(8,128)S(1)}, f32[4,4,128,128]{3,2,1,0:T(8,128)}, u32[]{:S(2)}) copy-start(f32[4,4,128,128]{3,2,1,0:T(8,128)} %own.3) | copy-start | bytes 3145732
  0.7 22.8 %copy-start.2 = (f32[2,4,128,128]{3,2,1,0:T(8,128)S(1)}, f32[2,4,128,128]{3,2,1,0:T(8,128)}, u32[]{:S(2)}) copy-start(f32[2,4,128,128]{3,2,1,0:T(8,128)} %refs_7_.1) | copy-start | bytes 1572868
  0.7 26.9 %copy-start.15 = (s32[8,4]{0,1:T(4,128)S(1)}, s32[8,4]{0,1:T(4,128)}, u32[]{:S(2)}) copy-start(s32[8,4]{0,1:T(4,128)} %param.15) | copy-start | bytes 388
  0.7 42.5 %copy-start.11 = (s32[16]{0:T(128)S(1)}, s32[16]{0:T(128)}, u32[]{:S(2)}) copy-start(s32[16]{0:T(128)} %owners.9) | copy-start | bytes 196
  1.8 20.5 %collective-permute-start = (f32[64,4,256]{2,1,0:T(4,128)S(1)}, f32[64,4,256]{2,1,0:T(4,128)S(1)}, u32[]{:S(2)}, u32[]{:S(2)}) collective-permute-start(f32[64,4,256]{2,1,0:T(4,128)S(1)} %dynamic-slice_bitcast_fusion), channel_id=1, source_target_pairs={{0,4},{4,8},{8,12},{12,0},{1,5},{5,9},{9,13},{13,1},{2,6},{6,10},{... | collective-permute-start | bytes 786440 | tf_op jit(solution)/shard_map/ppermute | solution.py:208
  3.4 18.9 %collective-permute-start.1 = (f32[64,4,256]{2,1,0:T(4,128)S(1)}, f32[64,4,256]{2,1,0:T(4,128)S(1)}, u32[]{:S(2)}, u32[]{:S(2)}) collective-permute-start(f32[64,4,256]{2,1,0:T(4,128)S(1)} %dynamic-slice_bitcast_fusion), channel_id=1, source_target_pairs={{0,8},{4,12},{8,0},{12,4},{1,9},{5,13},{9,1},{13,5},{2,10},{6,14},... | collective-permute-start | bytes 786440 | tf_op jit(solution)/shard_map/ppermute | solution.py:208
  3.8 21.8 %collective-permute-start.2 = (f32[64,4,256]{2,1,0:T(4,128)S(1)}, f32[64,4,256]{2,1,0:T(4,128)}, u32[]{:S(2)}, u32[]{:S(2)}) collective-permute-start(f32[64,4,256]{2,1,0:T(4,128)S(1)} %dynamic-slice_bitcast_fusion), channel_id=1, source_target_pairs={{0,12},{4,0},{8,4},{12,8},{1,13},{5,1},{9,5},{13,9},{2,14},{6,2},{... | collective-permute-start | bytes 786440 | tf_op jit(solution)/shard_map/ppermute | solution.py:208
  5.1 51.8 %copy-start.10 = (f32[2,128,128]{2,1,0:T(8,128)S(1)}, f32[2,128,128]{2,1,0:T(8,128)}, u32[]{:S(2)}) copy-start(f32[2,128,128]{2,1,0:T(8,128)} %diagonal.2) | copy-start | bytes 393220
  7.4 55.2 %collective-permute-start.9 = (f32[4,4,128,128]{3,2,0,1:T(8,128)}, f32[4,4,128,128]{3,2,0,1:T(8,128)}, u32[]{:S(2)}, u32[]{:S(2)}) collective-permute-start(f32[4,4,128,128]{3,2,0,1:T(8,128)} %copy.18), channel_id=1, source_target_pairs={{0,2},{2,0},{1,3},{3,1},{4,6},{6,4},{5,7},{7,5},{8,10},{10,8},{9,1... | collective-permute-start | bytes 3145736 | tf_op jit(solution)/shard_map/ppermute | solution.py:208
  22.3 3.4 %collective-permute-start.3 = (f32[64,4,256]{2,1,0:T(4,128)S(1)}, f32[64,4,256]{2,1,0:T(4,128)S(1)}, u32[]{:S(2)}, u32[]{:S(2)}) collective-permute-start(f32[64,4,256]{2,1,0:T(4,128)S(1)} %collective-permute-done.refs_1_), channel_id=1, source_target_pairs={{0,1},{1,0},{2,3},{3,2},{4,5},{5,4},{6,7},{7,6},{8,9},{9,8},{10,11... | collective-permute-start | bytes 786440 | tf_op jit(solution)/shard_map/ppermute | solution.py:208
  22.3 4.5 %collective-permute-start.4 = (f32[64,4,256]{2,1,0:T(4,128)S(1)}, f32[64,4,256]{2,1,0:T(4,128)S(1)}, u32[]{:S(2)}, u32[]{:S(2)}) collective-permute-start(f32[64,4,256]{2,1,0:T(4,128)S(1)} %collective-permute-done.1.refs_2_), channel_id=1, source_target_pairs={{0,1},{1,0},{2,3},{3,2},{4,5},{5,4},{6,7},{7,6},{8,9},{9,8},{10,11... | collective-permute-start | bytes 786440 | tf_op jit(solution)/shard_map/ppermute | solution.py:208
  22.8 0.7 copy-start.4
  23.5 19.7 %collective-permute-start.6 = (f32[2,4,128,128]{3,2,1,0:T(8,128)S(1)}, f32[2,4,128,128]{3,2,1,0:T(8,128)}, u32[]{:S(2)}, u32[]{:S(2)}) collective-permute-start(f32[2,4,128,128]{3,2,1,0:T(8,128)S(1)} %copy-done.2), channel_id=1, source_target_pairs={{0,2},{2,0},{1,3},{3,1},{4,6},{6,4},{5,7},{7,5},{8,10},{10,8},{9,1... | collective-permute-start | bytes 1572872 | tf_op jit(solution)/shard_map/ppermute | solution.py:208
  25.6 17.6 %collective-permute-start.7 = (f32[2,4,128,128]{3,2,1,0:T(8,128)S(1)}, f32[2,4,128,128]{3,2,1,0:T(8,128)}, u32[]{:S(2)}, u32[]{:S(2)}) collective-permute-start(f32[2,4,128,128]{3,2,1,0:T(8,128)S(1)} %copy-done.2), channel_id=1, source_target_pairs={{0,1},{1,0},{2,3},{3,2},{4,5},{5,4},{6,7},{7,6},{8,9},{9,8},{10,11... | collective-permute-start | bytes 1572872 | tf_op jit(solution)/shard_map/ppermute | solution.py:208
  25.6 0.7 copy-start.6
  26.3 58.6 %collective-permute-start.10 = (f32[4,4,128,128]{3,2,1,0:T(8,128)S(1)}, f32[4,4,128,128]{3,2,1,0:T(8,128)S(1)}, u32[]{:S(2)}, u32[]{:S(2)}) collective-permute-start(f32[4,4,128,128]{3,2,1,0:T(8,128)S(1)} %copy-done), channel_id=1, source_target_pairs={{0,1},{1,0},{2,3},{3,2},{4,5},{5,4},{6,7},{7,6},{8,9},{9,8},{10,11... | collective-permute-start | bytes 3145736 | tf_op jit(solution)/shard_map/ppermute | solution.py:208
  26.8 0.7 copy-start.8
  27.6 2.3 %collective-permute-start.5 = (f32[64,4,256]{2,1,0:T(4,128)}, f32[64,4,256]{2,1,0:T(4,128)}, u32[]{:S(2)}, u32[]{:S(2)}) collective-permute-start(f32[64,4,256]{2,1,0:T(4,128)} %collective-permute-done.2.refs_3_), channel_id=1, source_target_pairs={{0,1},{1,0},{2,3},{3,2},{4,5},{5,4},{6,7},{7,6},{8,9},{9,8},{10,11... | collective-permute-start | bytes 786440 | tf_op jit(solution)/shard_map/ppermute | solution.py:208
  43.2 1.0 copy-start.5
  44.2 0.9 copy-start.7
  45.1 0.9 copy-start.9
  46.1 0.7 copy-start.12
  46.7 0.7 copy-start.13
  51.9 33.5 %copy-start.14 = (s32[8]{0:T(128)S(1)}, s32[8]{0:T(128)}, u32[]{:S(2)}) copy-start(s32[8]{0:T(128)} %counts.5) | copy-start | bytes 100
  51.9 5.0 %collective-permute-start.8 = (f32[2,128,128]{2,1,0:T(8,128)S(1)}, f32[2,128,128]{2,1,0:T(8,128)S(1)}, u32[]{:S(2)}, u32[]{:S(2)}) collective-permute-start(f32[2,128,128]{2,1,0:T(8,128)S(1)} %get-tuple-element.29), channel_id=1, source_target_pairs={{0,2},{2,0},{1,3},{3,1},{4,6},{6,4},{5,7},{7,5},{8,10},{10,8},{9,1... | collective-permute-start | bytes 393224 | tf_op jit(solution)/shard_map/ppermute | solution.py:208
  52.5 5.7 %collective-permute-start.12 = (f32[3,128,128]{2,1,0:T(8,128)S(1)}, f32[3,128,128]{2,1,0:T(8,128)S(1)}, u32[]{:S(2)}, u32[]{:S(2)}) collective-permute-start(f32[3,128,128]{2,1,0:T(8,128)S(1)} %get-tuple-element.34.refs_0_), channel_id=1, source_target_pairs={{0,1},{1,0},{2,3},{3,2},{4,5},{5,4},{6,7},{7,6},{8,9},{9,8},{10,11... | collective-permute-start | bytes 589832 | tf_op jit(solution)/shard_map/ppermute | solution.py:208
  52.5 8.6 %collective-permute-start.14 = (f32[3,128,128]{2,1,0:T(8,128)S(1)}, f32[3,128,128]{2,1,0:T(8,128)S(1)}, u32[]{:S(2)}, u32[]{:S(2)}) collective-permute-start(f32[3,128,128]{2,1,0:T(8,128)S(1)} %get-tuple-element.36), channel_id=1, source_target_pairs={{0,4},{4,8},{8,12},{12,0},{1,5},{5,9},{9,13},{13,1},{2,6},{6,10},{... | collective-permute-start | bytes 589832 | tf_op jit(solution)/shard_map/ppermute | solution.py:208
  58.2 2.5 %collective-permute-start.13 = (f32[128,128]{1,0:T(8,128)S(1)}, f32[128,128]{1,0:T(8,128)S(1)}, u32[]{:S(2)}, u32[]{:S(2)}) collective-permute-start(f32[128,128]{1,0:T(8,128)S(1)} %get-tuple-element.35.refs_2_), channel_id=1, source_target_pairs={{0,1},{1,0},{2,3},{3,2},{4,5},{5,4},{6,7},{7,6},{8,9},{9,8},{10,11... | collective-permute-start | bytes 196616 | tf_op jit(solution)/shard_map/ppermute | solution.py:208
  58.2 20.6 %collective-permute-start.18 = (f32[3,128,128]{2,1,0:T(8,128)S(1)}, f32[3,128,128]{2,1,0:T(8,128)S(1)}, u32[]{:S(2)}, u32[]{:S(2)}) collective-permute-start(f32[3,128,128]{2,1,0:T(8,128)S(1)} %get-tuple-element.38), channel_id=1, source_target_pairs={{0,8},{4,12},{8,0},{12,4},{1,9},{5,13},{9,1},{13,5},{2,10},{6,14},... | collective-permute-start | bytes 589832 | tf_op jit(solution)/shard_map/ppermute | solution.py:208
  60.6 18.6 %collective-permute-start.22 = (f32[3,128,128]{2,1,0:T(8,128)S(1)}, f32[3,128,128]{2,1,0:T(8,128)S(1)}, u32[]{:S(2)}, u32[]{:S(2)}) collective-permute-start(f32[3,128,128]{2,1,0:T(8,128)S(1)} %get-tuple-element.40), channel_id=1, source_target_pairs={{0,12},{4,0},{8,4},{12,8},{1,13},{5,1},{9,5},{13,9},{2,14},{6,2},{... | collective-permute-start | bytes 589832 | tf_op jit(solution)/shard_map/ppermute | solution.py:208
  61.1 17.6 %collective-permute-start.16 = (f32[128,128]{1,0:T(8,128)S(1)}, f32[128,128]{1,0:T(8,128)S(1)}, u32[]{:S(2)}, u32[]{:S(2)}) collective-permute-start(f32[128,128]{1,0:T(8,128)S(1)} %get-tuple-element.37), channel_id=1, source_target_pairs={{0,4},{4,8},{8,12},{12,0},{1,5},{5,9},{9,13},{13,1},{2,6},{6,10},{... | collective-permute-start | bytes 196616 | tf_op jit(solution)/shard_map/ppermute | solution.py:208
  62.7 16.1 %collective-permute-start.20 = (f32[128,128]{1,0:T(8,128)S(1)}, f32[128,128]{1,0:T(8,128)S(1)}, u32[]{:S(2)}, u32[]{:S(2)}) collective-permute-start(f32[128,128]{1,0:T(8,128)S(1)} %get-tuple-element.39), channel_id=1, source_target_pairs={{0,8},{4,12},{8,0},{12,4},{1,9},{5,13},{9,1},{13,5},{2,10},{6,14},... | collective-permute-start | bytes 196616 | tf_op jit(solution)/shard_map/ppermute | solution.py:208
  78.7 4.3 %collective-permute-start.24 = (f32[128,128]{1,0:T(8,128)S(1)}, f32[128,128]{1,0:T(8,128)S(1)}, u32[]{:S(2)}, u32[]{:S(2)}) collective-permute-start(f32[128,128]{1,0:T(8,128)S(1)} %get-tuple-element.41), channel_id=1, source_target_pairs={{0,12},{4,0},{8,4},{12,8},{1,13},{5,1},{9,5},{13,9},{2,14},{6,2},{... | collective-permute-start | bytes 196616 | tf_op jit(solution)/shard_map/ppermute | solution.py:208
  78.7 4.3 %collective-permute-start.17 = (f32[128,128]{1,0:T(8,128)S(1)}, f32[128,128]{1,0:T(8,128)S(1)}, u32[]{:S(2)}, u32[]{:S(2)}) collective-permute-start(f32[128,128]{1,0:T(8,128)S(1)} %collective-permute-done.16.refs_6_), channel_id=1, source_target_pairs={{0,1},{1,0},{2,3},{3,2},{4,5},{5,4},{6,7},{7,6},{8,9},{9,8},{10,11... | collective-permute-start | bytes 196616 | tf_op jit(solution)/shard_map/ppermute | solution.py:208
  78.8 4.8 %collective-permute-start.21 = (f32[128,128]{1,0:T(8,128)S(1)}, f32[128,128]{1,0:T(8,128)S(1)}, u32[]{:S(2)}, u32[]{:S(2)}) collective-permute-start(f32[128,128]{1,0:T(8,128)S(1)} %collective-permute-done.20.refs_10_), channel_id=1, source_target_pairs={{0,1},{1,0},{2,3},{3,2},{4,5},{5,4},{6,7},{7,6},{8,9},{9,8},{10,11... | collective-permute-start | bytes 196616 | tf_op jit(solution)/shard_map/ppermute | solution.py:208
  79.3 10.1 %collective-permute-start.11 = (f32[4,128,128]{2,1,0:T(8,128)S(1)}, f32[4,128,128]{2,1,0:T(8,128)S(1)}, u32[]{:S(2)}, u32[]{:S(2)}) collective-permute-start(f32[4,128,128]{2,1,0:T(8,128)S(1)} %slice_bitcast_fusion), channel_id=1, source_target_pairs={{0,1},{1,0},{2,3},{3,2},{4,5},{5,4},{6,7},{7,6},{8,9},{9,8},{10,11... | collective-permute-start | bytes 786440 | tf_op jit(solution)/shard_map/ppermute | solution.py:208
  83.0 6.3 %collective-permute-start.15 = (f32[3,128,128]{2,1,0:T(8,128)S(1)}, f32[3,128,128]{2,1,0:T(8,128)S(1)}, u32[]{:S(2)}, u32[]{:S(2)}) collective-permute-start(f32[3,128,128]{2,1,0:T(8,128)S(1)} %collective-permute-done.14.refs_4_), channel_id=1, source_target_pairs={{0,1},{1,0},{2,3},{3,2},{4,5},{5,4},{6,7},{7,6},{8,9},{9,8},{10,11... | collective-permute-start | bytes 589832 | tf_op jit(solution)/shard_map/ppermute | solution.py:208
  83.0 6.3 %collective-permute-start.19 = (f32[3,128,128]{2,1,0:T(8,128)S(1)}, f32[3,128,128]{2,1,0:T(8,128)S(1)}, u32[]{:S(2)}, u32[]{:S(2)}) collective-permute-start(f32[3,128,128]{2,1,0:T(8,128)S(1)} %collective-permute-done.18.refs_8_), channel_id=1, source_target_pairs={{0,1},{1,0},{2,3},{3,2},{4,5},{5,4},{6,7},{7,6},{8,9},{9,8},{10,11... | collective-permute-start | bytes 589832 | tf_op jit(solution)/shard_map/ppermute | solution.py:208
  83.5 5.8 %collective-permute-start.23 = (f32[3,128,128]{2,1,0:T(8,128)S(1)}, f32[3,128,128]{2,1,0:T(8,128)S(1)}, u32[]{:S(2)}, u32[]{:S(2)}) collective-permute-start(f32[3,128,128]{2,1,0:T(8,128)S(1)} %collective-permute-done.22.refs_12_), channel_id=1, source_target_pairs={{0,1},{1,0},{2,3},{3,2},{4,5},{5,4},{6,7},{7,6},{8,9},{9,8},{10,11... | collective-permute-start | bytes 589832 | tf_op jit(solution)/shard_map/ppermute | solution.py:208
  84.9 4.4 %collective-permute-start.25 = (f32[128,128]{1,0:T(8,128)S(1)}, f32[128,128]{1,0:T(8,128)S(1)}, u32[]{:S(2)}, u32[]{:S(2)}) collective-permute-start(f32[128,128]{1,0:T(8,128)S(1)} %collective-permute-done.24.refs_14_), channel_id=1, source_target_pairs={{0,1},{1,0},{2,3},{3,2},{4,5},{5,4},{6,7},{7,6},{8,9},{9,8},{10,11... | collective-permute-start | bytes 196616 | tf_op jit(solution)/shard_map/ppermute | solution.py:208
  85.4 3.9 %copy-start.3 = (f32[4,128,128]{2,1,0:T(8,128)S(1)}, f32[4,128,128]{2,1,0:T(8,128)}, u32[]{:S(2)}) copy-start(f32[4,128,128]{2,1,0:T(8,128)} %diagonal.3) | copy-start | bytes 786436
  94.9 6.4 %collective-permute-start.26 = (f32[2,128,128]{2,1,0:T(8,128)S(1)}, f32[2,128,128]{2,1,0:T(8,128)S(1)}, u32[]{:S(2)}, u32[]{:S(2)}) collective-permute-start(f32[2,128,128]{2,1,0:T(8,128)S(1)} %get-tuple-element.42), channel_id=1, source_target_pairs={{0,2},{2,0},{1,3},{3,1},{4,6},{6,4},{5,7},{7,5},{8,10},{10,8},{9,1... | collective-permute-start | bytes 393224 | tf_op jit(solution)/shard_map/ppermute | solution.py:208
  95.4 8.6 %collective-permute-start.27 = (f32[2,128,128]{2,1,0:T(8,128)S(1)}, f32[2,128,128]{2,1,0:T(8,128)S(1)}, u32[]{:S(2)}, u32[]{:S(2)}) collective-permute-start(f32[2,128,128]{2,1,0:T(8,128)S(1)} %get-tuple-element.43), channel_id=1, source_target_pairs={{0,2},{2,0},{1,3},{3,1},{4,6},{6,4},{5,7},{7,5},{8,10},{10,8},{9,1... | collective-permute-start | bytes 393224 | tf_op jit(solution)/shard_map/ppermute | solution.py:208
  96.9 9.9 %collective-permute-start.28 = (f32[2,128,128]{2,1,0:T(8,128)S(1)}, f32[2,128,128]{2,1,0:T(8,128)S(1)}, u32[]{:S(2)}, u32[]{:S(2)}) collective-permute-start(f32[2,128,128]{2,1,0:T(8,128)S(1)} %get-tuple-element.44), channel_id=1, source_target_pairs={{0,2},{2,0},{1,3},{3,1},{4,6},{6,4},{5,7},{7,5},{8,10},{10,8},{9,1... | collective-permute-start | bytes 393224 | tf_op jit(solution)/shard_map/ppermute | solution.py:208
  97.4 11.3 %collective-permute-start.29 = (f32[2,128,128]{2,1,0:T(8,128)S(1)}, f32[2,128,128]{2,1,0:T(8,128)S(1)}, u32[]{:S(2)}, u32[]{:S(2)}) collective-permute-start(f32[2,128,128]{2,1,0:T(8,128)S(1)} %get-tuple-element.45), channel_id=1, source_target_pairs={{0,2},{2,0},{1,3},{3,1},{4,6},{6,4},{5,7},{7,5},{8,10},{10,8},{9,1... | collective-permute-start | bytes 393224 | tf_op jit(solution)/shard_map/ppermute | solution.py:208

commit v2 on v0

--- a/solution.py
+++ b/solution.py
@@ -1,12 +1,378 @@
+import functools
+
 import jax
 import jax.numpy as jnp
 from jax import lax
+from jax.experimental import pallas as pl
+from jax.experimental.pallas import tpu as pltpu
 from jax.sharding import PartitionSpec as P
 
 A = 4
 
 
 PRECISE = lax.Precision.HIGHEST
+THREE_PASS = lax.Precision.HIGH
+F32 = jnp.float32
+SMEM = pl.BlockSpec(memory_space=pltpu.SMEM)
+VMEM = pl.BlockSpec(memory_space=pltpu.VMEM)
+
+
+def mm(a, b):
+    return jnp.dot(a, b, precision=THREE_PASS, preferred_element_type=F32)
+
+
+def mm_t(a, b):
+    return lax.dot_general(
+        a, b, (((0,), (0,)), ((), ())), precision=THREE_PASS, preferred_element_type=F32
+    )
+
+
+def array(*shape):
+    return jax.ShapeDtypeStruct(shape, F32)
+
+
+def call(body, out_shapes, table, operands, scratch=(), flops=0):
+    size = sum(4 * o.size for o in operands) + sum(4 * o.size for o in out_shapes)
+    return pl.pallas_call(
+        body,
+        out_shape=tuple(out_shapes),
+        in_specs=[SMEM] + [VMEM] * len(operands),
+        out_specs=tuple([VMEM] * len(out_shapes)),
+        scratch_shapes=[pltpu.VMEM(s, F32) for s in scratch],
+        compiler_params=pltpu.CompilerParams(vmem_limit_bytes=40 * 1024 * 1024),
+        cost_estimate=pl.CostEstimate(flops=0, bytes_accessed=0, transcendentals=0),
+    )(table, *operands)
+
+
+def spot(index, size):
+    return pl.ds(pl.multiple_of(index * size, size), size)
+
+
+class Tree:
+    def __init__(self, table, nodes, per_one, per_two):
+        self.table, self.nodes, self.per_one, self.per_two = table, nodes, per_one, per_two
+        self.ones, self.twos = nodes * per_one, nodes * per_two
+        self.me, self.row, self.sub = table[0], table[1], table[2]
+
+    def count(self, g):
+        return self.table[3 + g]
+
+    def owner(self, h):
+        return self.table[3 + self.ones + h]
+
+    def slot(self, h):
+        return self.table[3 + self.ones + self.twos + h]
+
+    def ancestor(self, g, a):
+        return self.table[3 + self.ones + 2 * self.twos + a * self.ones + g]
+
+    def offset(self, h, t):
+        return self.table[3 + (1 + A) * self.ones + (2 + t) * self.twos + h]
+
+    def node(self, k):
+        return lax.rem(self.me + k + self.nodes, self.nodes)
+
+    def child(self, node, owner):
+        found = jnp.int32(0)
+        for c in range(self.per_two):
+            found = jnp.where(self.owner(node * self.per_two + c) == owner, c, found)
+        return found
+
+    def back(self, block):
+        return lax.rem(self.me - block + self.nodes, self.nodes)
+
+    def live(self, g, a):
+        return (a < self.count(g)).astype(F32)
+
+    def level_two(self, h):
+        h = self.me * self.per_two + h
+        parent = self.owner(h) * self.per_one + self.slot(h)
+        valid = [(t < 1 + self.count(parent)).astype(F32) for t in range(A)]
+        return valid, [self.ancestor(parent, self.offset(h, t)) for t in range(A - 1)]
+
+
+def fill_rows(out, at, rows, parts):
+    for first, part in parts:
+        width = part.shape[2]
+        for b in range(part.shape[1]):
+            out[pl.ds(pl.multiple_of(at + first, rows // 2), part.shape[0]), b * width : (b + 1) * width] = part[:, b, :]
+
+
+EARLY, LATE = (1, 3), 2
+
+
+def early_kernel(sizes, table, root, *refs):
+    tree = Tree(table, *sizes)
+    n = len(EARLY)
+    far, near = refs[:n], refs[n : 2 * n]
+    own, beside, whole, spread, total = refs[2 * n :]
+    beside = beside.at[1 - tree.row]
+    per_one, blocks, rows, cols = own.shape
+    half = rows // 2
+    fill_rows(whole, 0, rows, [(0, root)])
+    for i in range(n):
+        fill_rows(whole, (i + 1) * rows, rows, [(tree.sub * half, far[i]), ((1 - tree.sub) * half, near[i])])
+    for g in range(per_one):
+        for a in range(blocks):
+            one = tree.me * per_one + g
+            at, valid = tree.ancestor(one, a), tree.live(one, a)
+            lanes = slice(g * cols, (g + 1) * cols)
+            spread[spot(at * 2 + tree.row, rows), lanes] = own[g, a] * valid
+            spread[spot(at * 2 + 1 - tree.row, rows), lanes] = beside[g, a] * valid
+    total[...] = mm(whole[...], spread[...])
+
+
+def late_kernel(sizes, table, far, near, spread, total, own, across, rest, cov, keep, send, *refs):
+    tree = Tree(table, *sizes)
+    picks = refs[: tree.nodes]
+    wide, tall, part = refs[tree.nodes :]
+    per_one, blocks, rows, cols = own.shape
+    half = rows // 2
+    fill_rows(rest, 0, rows, [(tree.sub * half, far), ((1 - tree.sub) * half, near)])
+    last = mm(rest[...], spread[...])
+    for g in range(per_one):
+        lanes = slice(g * cols, (g + 1) * cols)
+        for i, k in enumerate((0,) + EARLY):
+            tall[g, k] = total[i * rows : (i + 1) * rows, lanes]
+        tall[g, LATE] = last[:, lanes]
+    for g in range(per_one):
+        one = tree.me * per_one + g
+        for a in range(blocks):
+            cov[g, a] = tall[g, tree.back(tree.ancestor(one, a))] * (-tree.live(one, a))
+    for k in range(tree.nodes):
+        target = tree.node(k)
+        h = target * tree.per_two + tree.child(target, tree.me)
+        for t in range(blocks - 1):
+            picks[k][t] = cov[tree.slot(h), tree.offset(h, t)]
+    for g in range(per_one):
+        one = tree.me * per_one + g
+        for a in range(blocks):
+            valid = tree.live(one, a)
+            wide[a * rows : (a + 1) * rows, spot(tree.sub, cols)] = own[g, a] * valid
+            wide[a * rows : (a + 1) * rows, spot(1 - tree.sub, cols)] = across[g, a] * valid
+        part[...] = -mm_t(wide[...], cov[g].reshape(blocks * rows, cols))
+        keep[g] = part[spot(tree.row, rows), :]
+        send[g] = part[spot(1 - tree.row, rows), :]
+
+
+def diag_one_kernel(sizes, table, diagonal, keep, got, cross, out, *tops):
+    tree = Tree(table, *sizes)
+    out[...] = diagonal[...] + (keep[...] + got[...])
+    for k in range(tree.nodes):
+        target = tree.node(k)
+        slot = tree.slot(target * tree.per_two + tree.child(target, tree.me))
+        if k == LATE:
+            tops[k][: A - 1] = cross[...]
+            tops[k][A - 1] = out[slot]
+        else:
+            tops[k][...] = out[slot]
+
+
+def first_blocks_kernel(sizes, table, panel, out):
+    tree = Tree(table, *sizes)
+    out[...] = panel[1 - tree.row, :, 0]
+
+
+def root_two_kernel(sizes, table, whole, rest, own, beside, across, lower, inner, spread, wide, tall):
+    tree = Tree(table, *sizes)
+    per_two, blocks, rows, cols = own.shape
+    beside = beside.at[1 - tree.row]
+    spread[...] = jnp.zeros_like(spread)
+    for h in range(per_two):
+        valid, at = tree.level_two(h)
+        lanes = slice(h * cols, (h + 1) * cols)
+        for t in range(1, blocks):
+            spread[spot(at[t - 1] * 2 + tree.row, rows), lanes] = own[h, t] * valid[t]
+            spread[spot(at[t - 1] * 2 + 1 - tree.row, rows), lanes] = beside[h, t] * valid[t]
+    most = mm(whole[...], spread[...])
+    last = mm(rest[...], spread[...])
+    for h in range(per_two):
+        lanes = slice(h * cols, (h + 1) * cols)
+        for i, k in enumerate((0,) + EARLY):
+            tall[h, k] = most[i * rows : (i + 1) * rows, lanes]
+        tall[h, LATE] = last[:, lanes]
+    for h in range(per_two):
+        valid, at = tree.level_two(h)
+        for t in range(1, blocks):
+            lower[h, t - 1] = tall[h, tree.back(at[t - 1])] * valid[t]
+            wide[(t - 1) * rows : t * rows, spot(tree.sub, cols)] = own[h, t] * valid[t]
+            wide[(t - 1) * rows : t * rows, spot(1 - tree.sub, cols)] = across[h, t] * valid[t]
+        inner[h] = mm_t(wide[...], lower[h].reshape((blocks - 1) * rows, cols))
+
+
+def parent_two_kernel(sizes, shifts, table, own, beside, across, corner, lower, inner, diagonal, *refs):
+    tree = Tree(table, *sizes)
+    row, sub = tree.row, tree.sub
+    blocks, rows, cols = own.shape[1:]
+    beside = beside.at[1 - row]
+    refs = list(refs)
+    ins = []
+    for k in shifts:
+        if k == LATE:
+            mine, side = refs[:2]
+            del refs[:2]
+            ins.append((mine, side, mine.at[A - 1], side.at[A - 1]))
+        else:
+            ins.append(refs[:4])
+            del refs[:4]
+    panel, diag, sends, cross, top, first, local, wide, part, more = refs
+    low = (blocks - 1) * rows
+    for i, k in enumerate(shifts):
+        cross_own, cross_side, top_own, top_side = ins[i]
+        h = tree.child(tree.me, tree.node(-k))
+        valid, _ = tree.level_two(h)
+        for t in range(1, blocks):
+            span = slice((t - 1) * rows, t * rows)
+            cross[span, spot(sub, cols)] = cross_own[t - 1]
+            cross[span, spot(1 - sub, cols)] = cross_side[t - 1]
+            local[span, :] = own[h, t] * valid[t]
+            wide[span, spot(sub, cols)] = own[h, t] * valid[t]
+            wide[span, spot(1 - sub, cols)] = across[h, t] * valid[t]
+        top[:, spot(sub, cols)] = top_own[...]
+        top[:, spot(1 - sub, cols)] = top_side[...]
+        first[spot(row, rows), :] = own[h, 0]
+        first[spot(1 - row, rows), :] = beside[h, 0]
+        mine = spot(blocks - 1 + row, rows)
+        other = spot(blocks - row, rows)
+        wide[mine, spot(sub, cols)] = own[h, 0]
+        wide[mine, spot(1 - sub, cols)] = across[h, 0]
+        wide[other, spot(sub, cols)] = beside[h, 0]
+        wide[other, spot(1 - sub, cols)] = corner[h]
+        below = mm(cross[...], first[...])
+        for t in range(1, blocks):
+            span = slice((t - 1) * rows, t * rows)
+            part[span, :] = below[span, :] * valid[t]
+            panel[i, t] = -(lower[h, t - 1] + part[span, :])
+        part[low:, :] = mm_t(cross[...], local[...])
+        part[mine, :] += mm(top[...], first[...])
+        more[...] = inner[h] + mm_t(wide[...], part[...])
+        panel[i, 0] = -part[mine, :]
+        sends[i, 0] = part[other, :]
+        diag[i] = diagonal[h] + more[spot(row, rows), :]
+        sends[i, 1] = more[spot(1 - row, rows), :]
+
+
+def finish_kernel(sizes, groups, table, *refs):
+    tree = Tree(table, *sizes)
+    n = len(groups)
+    panels, diags, gots = refs[:n], refs[n : 2 * n], refs[2 * n : 3 * n]
+    panel_out, diag_out = refs[3 * n :]
+    for j, shifts in enumerate(groups):
+        for i, k in enumerate(shifts):
+            h = tree.child(tree.me, tree.node(-k))
+            panel_out[h, 1:] = panels[j][i, 1:]
+            panel_out[h, 0] = panels[j][i, 0] - gots[j][i, 0]
+            diag_out[h] = diags[j][i] + gots[j][i, 1]
+
+
+def shift(x, axis, k):
+    n = lax.axis_size(axis)
+    return lax.ppermute(x, axis, [(i, (i + k) % n) for i in range(n)])
+
+
+def after(x, *others):
+    return lax.optimization_barrier((x,) + others)[0]
+
+
+def paired_shards(root_inverse, panel_one, diag_one, panel_two, diag_two, ancestors, counts, owners, slots, offsets):
+    nodes = lax.axis_size("node")
+    me, row, sub = lax.axis_index("node"), lax.axis_index("row"), lax.axis_index("sub")
+    per_one, blocks, rows, cols = panel_one.shape
+    per_two = panel_two.shape[0]
+    sizes = nodes, per_one, per_two
+    full = root_inverse.shape[2] * root_inverse.shape[3]
+    low = (blocks - 1) * rows
+    table = jnp.concatenate(
+        [jnp.stack([me, row, sub]).astype(jnp.int32), counts, owners, slots, ancestors.T.reshape(-1), offsets.T.reshape(-1)]
+    )
+    bind = lambda kernel, *more: functools.partial(kernel, sizes, *more)
+
+    root = root_inverse[0]
+    half = lax.dynamic_slice_in_dim(root, sub * (rows // 2), rows // 2, 0)
+    far = {k: shift(half, "node", k) for k in EARLY + (LATE,)}
+    beside_one = lax.all_gather(panel_one, "row")
+    beside_two = lax.all_gather(panel_two, "row")
+    across_one = shift(after(panel_one, *[far[k] for k in EARLY]), "sub", 1)
+    across_two = shift(after(panel_two, *[far[k] for k in EARLY]), "sub", 1)
+    near = {k: shift(far[k], "sub", 1) for k in EARLY}
+    near[LATE] = shift(after(far[LATE], across_two), "sub", 1)
+
+    n = len(EARLY) + 1
+    whole, spread, total = call(
+        bind(early_kernel),
+        [array(n * rows, full), array(full, per_one * cols), array(n * rows, per_one * cols)],
+        table,
+        [root] + [far[k] for k in EARLY] + [near[k] for k in EARLY] + [panel_one, beside_one],
+        flops=6 * n * rows * full * per_one * cols,
+    )
+    out = call(
+        bind(late_kernel),
+        [array(rows, full), array(*panel_one.shape), array(per_one, rows, cols), array(per_one, rows, cols)]
+        + [array(blocks - 1, rows, cols)] * nodes,
+        table,
+        [far[LATE], near[LATE], spread, total, panel_one, across_one],
+        [(blocks * rows, 2 * cols), (per_one, nodes, rows, cols), (2 * rows, cols)],
+        flops=6 * rows * full * per_one * cols,
+    )
+    rest, cov_panel_one, keep, send = out[:4]
+    picks = out[4:]
+    cross = {k: shift(picks[k], "node", k) for k in EARLY}
+    out = call(
+        bind(diag_one_kernel),
+        [array(*diag_one.shape)] + [array(blocks, rows, cols) if k == LATE else array(rows, cols) for k in range(nodes)],
+        table,
+        [diag_one, keep, shift(send, "row", 1), picks[LATE]],
+    )
+    cov_diag_one = out[0]
+    arrived = {k: [cross[k], shift(out[1 + k], "node", k)] for k in EARLY}
+    arrived[0] = [after(x, cross[EARLY[0]]) for x in (picks[0], out[1])]
+    arrived[LATE] = [shift(out[1 + LATE], "node", LATE)]
+
+    corner_two = shift(call(bind(first_blocks_kernel), [array(per_two, rows, cols)], table, [after(beside_two, cross[EARLY[0]])])[0], "sub", 1)
+    lower, inner = call(
+        bind(root_two_kernel),
+        [array(per_two, blocks - 1, rows, cols), array(per_two, 2 * rows, cols)],
+        table,
+        [whole, rest, panel_two, beside_two, across_two],
+        [(full, per_two * cols), (low, 2 * cols), (per_two, nodes, rows, cols)],
+        flops=6 * rows * nodes * full * per_two * cols,
+    )
+    groups = ((0,) + EARLY, (LATE,))
+    panels, diags, gots = [], [], []
+    for shifts in groups:
+        extra = []
+        for k in shifts:
+            for x in arrived[k]:
+                if gots:
+                    x = after(x, sends)
+                extra += [x, shift(x, "sub", 1)]
+        panel, diag, sends = call(
+            bind(parent_two_kernel, shifts),
+            [array(len(shifts), blocks, rows, cols), array(len(shifts), rows, cols), array(len(shifts), 2, rows, cols)],
+            table,
+            [panel_two, beside_two, across_two, corner_two, lower, inner, diag_two]
+            + extra,
+            [
+                (low, 2 * cols),
+                (rows, 2 * cols),
+                (2 * rows, cols),
+                (low, cols),
+                (low + 2 * rows, 2 * cols),
+                (low + 2 * rows, cols),
+                (2 * rows, cols),
+            ],
+            flops=len(shifts) * 36 * low * cols * 2 * cols,
+        )
+        panels.append(panel)
+        diags.append(diag)
+        gots.append(shift(sends, "row", 1))
+    cov_panel_two, cov_diag_two = call(
+        bind(finish_kernel, groups),
+        [array(*panel_two.shape), array(*diag_two.shape)],
+        table,
+        panels + diags + gots,
+    )
+    return (cov_panel_one, cov_diag_one, cov_panel_two, cov_diag_two)
 
 
 def pick_blocks(gathered, block_ids):
@@ -33,7 +399,7 @@
     return diagonal - jnp.transpose(summed, (1, 0, 2))
 
 
-def shards(
+def general_shards(
     root_inverse,
     panel_one,
     diag_one,
@@ -114,6 +480,14 @@
     return (cov_panel_one, cov_diag_one, cov_panel_two, cov_diag_two)
 
 
+def shards(*args):
+    sizes = lax.axis_size("node"), lax.axis_size("row"), lax.axis_size("sub")
+    root, panel_one, panel_two = args[0], args[1], args[3]
+    if sizes == (4, 2, 2) and panel_two.shape[0] == root.shape[2] == panel_one.shape[1] == A and root.shape[0] == 1:
+        return paired_shards(*args)
+    return general_shards(*args)
+
+
 def solution(mesh):
     return jax.shard_map(
         shards,

time: 221 us -> 112 us (0.51)
  the two profiles are of different devices: /device:TPU:18 before, /device:TPU:0 now
where the time goes in v2:
time: 112 us
  waiting for transfers between devices  49.9 us (45%)
  starting transfers between devices  21 us (19%)
  Pallas kernels  19.1 us (17%)
  between operations  14.3 us (13%)
  local copies, waits for them, and re-layouts  7.45 us (7%)
    ppermute x24, waiting for transfers between devices, shift(): return lax.ppermute(x, axis, [(i, (i + k) % n) for i in range(n)])  45.3 us
    ppermute x24, starting transfers between devices, shift(): return lax.ppermute(x, axis, [(i, (i + k) % n) for i in range(n)])  20.9 us
    pallas_call x8, Pallas kernels, call(): pl.pallas_call(body, out_shape=tuple(out_shapes), in_specs=[SMEM] + [VMEM...  19.1 us
    unnamed x36, local copies, waits for them, and re-layouts  6.24 us
    all_gather x1, waiting for transfers between devices, paired_shards(): beside_two = lax.all_gather(panel_two, 'row')  3.18 us
  transfers between devices with their start and end apart: 26, of which 10 were waited for; matrix products, arithmetic and copies ran while one was open for 1% of the time, Pallas kernels for 16%

profile of v2, /device:TPU:0, one launch (start us, length us, event | category | flops | bytes accessed | tf_op | source)
XLA Modules:
  0.0 111.7 jit_solution(18302032169376632210)
XLA Ops:
  7.2 0.0 all-gather.5.cloned.1.call-start
  7.3 0.7 all-gather.5.cloned.1.call-update
  8.0 0.0 all-gather.7.cloned.1.call-start
  8.0 0.7 all-gather.7.cloned.1.call-update
  8.7 1.0 dynamic-slice_bitcast_fusion
  9.7 3.1 %collective-permute-start.1 = (f32[64,4,256]{2,1,0:T(4,128)S(1)}, f32[64,4,256]{2,1,0:T(4,128)}, u32[]{:S(2)}, u32[]{:S(2)}) collective-permute-start(f32[64,4,256]{2,1,0:T(4,128)S(1)} %dynamic-slice_bitcast_fusion), channel_id=1, source_target_pairs={{0,4},{4,8},{8,12},{12,0},{1,5},{5,9},{9,13},{13,1},{2,6},{6,10},{... | collective-permute-start | bytes 786440 | tf_op jit(solution)/shard_map/ppermute | solution.py:270
  12.8 2.1 %collective-permute-start.2 = (f32[64,4,256]{2,1,0:T(4,128)S(1)}, f32[64,4,256]{2,1,0:T(4,128)}, u32[]{:S(2)}, u32[]{:S(2)}) collective-permute-start(f32[64,4,256]{2,1,0:T(4,128)S(1)} %dynamic-slice_bitcast_fusion), channel_id=1, source_target_pairs={{0,12},{4,0},{8,4},{12,8},{1,13},{5,1},{9,5},{13,9},{2,14},{6,2},{... | collective-permute-start | bytes 786440 | tf_op jit(solution)/shard_map/ppermute | solution.py:270
  14.9 7.2 %collective-permute-done.1.refs_0_ = f32[64,4,256]{2,1,0:T(4,128)} collective-permute-done((f32[64,4,256]{2,1,0:T(4,128)S(1)}, f32[64,4,256]{2,1,0:T(4,128)}, u32[]{:S(2)}, u32[]{:S(2)}) %collective-permute-start.1) | collective-permute-done | bytes 262176 | tf_op jit(solution)/shard_map/ppermute | solution.py:270
  22.1 4.2 %collective-permute-done.2.refs_1_ = f32[64,4,256]{2,1,0:T(4,128)} collective-permute-done((f32[64,4,256]{2,1,0:T(4,128)S(1)}, f32[64,4,256]{2,1,0:T(4,128)}, u32[]{:S(2)}, u32[]{:S(2)}) %collective-permute-start.2) | collective-permute-done | bytes 262176 | tf_op jit(solution)/shard_map/ppermute | solution.py:270
  26.3 0.0 collective-permute-start.3
  26.3 1.4 %collective-permute-start = (f32[64,4,256]{2,1,0:T(4,128)S(1)}, f32[64,4,256]{2,1,0:T(4,128)S(1)}, u32[]{:S(2)}, u32[]{:S(2)}) collective-permute-start(f32[64,4,256]{2,1,0:T(4,128)S(1)} %dynamic-slice_bitcast_fusion), channel_id=1, source_target_pairs={{0,8},{4,12},{8,0},{12,4},{1,9},{5,13},{9,1},{13,5},{2,10},{6,14},... | collective-permute-start | bytes 786440 | tf_op jit(solution)/shard_map/ppermute | solution.py:270
  27.7 0.2 collective-permute-start.7
  27.8 0.4 collective-permute-start.5
  28.2 0.2 collective-permute-start.6
  28.3 13.2 %collective-permute-done.far = f32[64,4,256]{2,1,0:T(4,128)S(1)} collective-permute-done((f32[64,4,256]{2,1,0:T(4,128)S(1)}, f32[64,4,256]{2,1,0:T(4,128)S(1)}, u32[]{:S(2)}, u32[]{:S(2)}) %collective-permute-start) | collective-permute-done | bytes 262176 | tf_op jit(solution)/shard_map/ppermute | solution.py:270
  41.5 0.0 collective-permute-done.3.across
  41.5 0.0 collective-permute-start.4
  41.5 0.1 reshape.15
  41.6 0.1 reshape.16
  41.7 0.1 concatenate.3.table
  41.8 0.0 collective-permute-done.5.refs_2_
  41.8 0.0 collective-permute-done.6.refs_3_
  41.8 0.0 all-gather.5.cloned.1.call-done
  41.9 1.3 %copy-done.7 = f32[4,4,128,128]{3,2,1,0:T(8,128)S(1)} copy-done((f32[4,4,128,128]{3,2,1,0:T(8,128)S(1)}, f32[4,4,128,128]{3,2,1,0:T(8,128)}, u32[]{:S(2)}) %copy-start.7) | copy-done | bytes 1048600
  43.2 2.7 %shard_map.129 = (f32[384,1024]{1,0:T(8,128)S(1)}, f32[1024,256]{1,0:T(8,128)S(1)}, f32[384,256]{1,0:T(8,128)S(1)}) custom-call(s32[123]{0:T(128)S(1)} %concatenate.3.table, f32[128,4,256]{2,1,0:T(4,128)S(1)} %bitcast.14, f32[64,4,256]{2,1,0:T(4,128)} %collective-permute-done.1.refs_0_, f32[64,4,256]{2,1,0:T(4,128)} %collective-permute-done.2.refs_1_, ...), custom_call_target="tpu_custom_call" | custom-call | tf_op jit(solution)/shard_map/pallas_call | solution.py:36
  45.9 1.1 %copy-done.4 = f32[384,1024]{1,0:T(8,128)} copy-done((f32[384,1024]{1,0:T(8,128)}, f32[384,1024]{1,0:T(8,128)S(1)}, u32[]{:S(2)}) %copy-start.4) | copy-done | bytes 1572888
  47.0 0.0 collective-permute-done.7.across
  47.1 3.0 %shard_map.130 = (f32[128,1024]{1,0:T(8,128)S(1)}, f32[2,4,128,128]{3,2,1,0:T(8,128)}, f32[2,128,128]{2,1,0:T(8,128)S(1)}, f32[2,128,128]{2,1,0:T(8,128)S(1)}, f...) custom-call(s32[123]{0:T(128)S(1)} %concatenate.3.table, ...), custom_call_target="tpu_custom_call" | custom-call | tf_op jit(solution)/shard_map/pallas_call | solution.py:36
  50.1 1.5 %collective-permute-start.8 = (f32[2,128,128]{2,1,0:T(8,128)S(1)}, f32[2,128,128]{2,1,0:T(8,128)S(1)}, u32[]{:S(2)}, u32[]{:S(2)}) collective-permute-start(f32[2,128,128]{2,1,0:T(8,128)S(1)} %get-tuple-element.44), channel_id=1, source_target_pairs={{0,2},{2,0},{1,3},{3,1},{4,6},{6,4},{5,7},{7,5},{8,10},{10,8},{9,1... | collective-permute-start | bytes 393224 | tf_op jit(solution)/shard_map/ppermute | solution.py:270
  51.6 3.8 %collective-permute-start.16 = (f32[3,128,128]{2,1,0:T(8,128)}, f32[3,128,128]{2,1,0:T(8,128)S(1)}, u32[]{:S(2)}, u32[]{:S(2)}) collective-permute-start(f32[3,128,128]{2,1,0:T(8,128)} %get-tuple-element.58), channel_id=1, source_target_pairs={{0,12},{4,0},{8,4},{12,8},{1,13},{5,1},{9,5},{13,9},{2,14},{6,2},{... | collective-permute-start | bytes 589832 | tf_op jit(solution)/shard_map/ppermute | solution.py:270
  55.4 3.7 %collective-permute-done.8.got = f32[2,128,128]{2,1,0:T(8,128)S(1)} collective-permute-done((f32[2,128,128]{2,1,0:T(8,128)S(1)}, f32[2,128,128]{2,1,0:T(8,128)S(1)}, u32[]{:S(2)}, u32[]{:S(2)}) %collective-permute-start.8) | collective-permute-done | bytes 131104 | tf_op jit(solution)/shard_map/ppermute | solution.py:270
  59.1 1.2 %shard_map.131 = (f32[2,128,128]{2,1,0:T(8,128)}, f32[128,128]{1,0:T(8,128)}, f32[128,128]{1,0:T(8,128)S(1)}, f32[4,128,128]{2,1,0:T(8,128)S(1)}, f32[128,128]{1,0:T(8,128)S(1)}) custom-call(s32[123]{0:T(128)S(1)} %concatenate.3.table, f32[2,128,128]{2,1,0:T(8,128)S(1)} %copy-done.11, f32[2,128,128]{2,1,0:T(8,128)S(1)} %get-tuple-element.43.keep, ...), custom_call_target="tpu_custom_call" | custom-call | tf_op jit(solution)/shard_map/pallas_call | solution.py:36
  60.3 0.7 copy-done.12
  61.0 0.0 collective-permute-start.14
  61.0 3.8 %collective-permute-start.18 = (f32[128,128]{1,0:T(8,128)S(1)}, f32[128,128]{1,0:T(8,128)}, u32[]{:S(2)}, u32[]{:S(2)}) collective-permute-start(f32[128,128]{1,0:T(8,128)S(1)} %get-tuple-element.59), channel_id=1, source_target_pairs={{0,12},{4,0},{8,4},{12,8},{1,13},{5,1},{9,5},{13,9},{2,14},{6,2},{... | collective-permute-start | bytes 196616 | tf_op jit(solution)/shard_map/ppermute | solution.py:270
  64.9 0.0 collective-permute-done.9.refs_4_
  64.9 0.0 collective-permute-start.12
  64.9 2.6 %collective-permute-done.14.refs_6_ = f32[128,128]{1,0:T(8,128)} collective-permute-done((f32[128,128]{1,0:T(8,128)S(1)}, f32[128,128]{1,0:T(8,128)}, u32[]{:S(2)}, u32[]{:S(2)}) %collective-permute-start.14) | collective-permute-done | bytes 65568 | tf_op jit(solution)/shard_map/ppermute | solution.py:270
  67.5 0.0 collective-permute-start.15
  67.5 0.0 collective-permute-done.18.refs_10_
  67.5 0.5 collective-permute-start.19
  68.0 3.2 %all-gather.7.cloned.1.call-done = f32[8,4,128,128]{3,2,1,0:T(8,128)} async-done(((f32[4,4,128,128]{3,2,1,0:T(8,128)}), f32[8,4,128,128]{3,2,1,0:T(8,128)}) %all-gather.7.cloned.1.call-update) | async-done | bytes 2097168 | tf_op jit(solution)/shard_map/all_gather | solution.py:294
  71.2 1.6 %copy-done = f32[8,4,128,128]{3,2,1,0:T(8,128)S(1)} copy-done((f32[8,4,128,128]{3,2,1,0:T(8,128)S(1)}, f32[8,4,128,128]{3,2,1,0:T(8,128)}, u32[]{:S(2)}) %copy-start) | copy-done | bytes 2097176
  72.8 0.6 shard_map.132
  73.3 0.1 collective-permute-start.10
  73.4 2.5 %collective-permute-start.20 = (f32[4,128,128]{2,1,0:T(8,128)}, f32[4,128,128]{2,1,0:T(8,128)S(1)}, u32[]{:S(2)}, u32[]{:S(2)}) collective-permute-start(f32[4,128,128]{2,1,0:T(8,128)} %copy-done.12), channel_id=1, source_target_pairs={{0,8},{4,12},{8,0},{12,4},{1,9},{5,13},{9,1},{13,5},{2,10},{6,14},... | collective-permute-start | bytes 786440 | tf_op jit(solution)/shard_map/ppermute | solution.py:270
  75.9 0.0 collective-permute-done.12.refs_3_
  75.9 0.2 collective-permute-start.11
  76.1 0.4 collective-permute-start.13
  76.4 0.0 collective-permute-done.19.refs_11_
  76.4 0.2 collective-permute-start.17
  76.6 1.4 %copy-done.5 = f32[384,1024]{1,0:T(8,128)S(1)} copy-done((f32[384,1024]{1,0:T(8,128)S(1)}, f32[384,1024]{1,0:T(8,128)}, u32[]{:S(2)}) %copy-start.5) | copy-done | bytes 1572888
  78.0 3.8 %shard_map.133 = (f32[4,3,128,128]{3,2,1,0:T(8,128)S(1)}, f32[4,256,128]{2,1,0:T(8,128)S(1)}) custom-call(s32[123]{0:T(128)S(1)} %concatenate.3.table, f32[384,1024]{1,0:T(8,128)S(1)} %copy-done.5, f32[128,1024]{1,0:T(8,128)S(1)} %get-tuple-element.50.rest, f32[4,4,128,128]{3,2,1,0:T(8,128)S(1)} %copy-done.2, f32[2,4,4,128,128]{4,3,2,1,0:T(8,128)S(1)} %bitcast.11, ...), custom_call_target="tpu_custom_call" | custom-call | tf_op jit(solution)/shard_map/pallas_call | solution.py:36
  81.8 0.0 collective-permute-done.11.refs_1_
  81.8 0.0 collective-permute-done.10.corner
  81.8 4.2 %shard_map.134 = (f32[3,4,128,128]{3,2,1,0:T(8,128)S(1)}, f32[3,128,128]{2,1,0:T(8,128)S(1)}, f32[3,2,128,128]{3,2,1,0:T(8,128)S(1)}) custom-call(s32[123]{0:T(128)S(1)} %concatenate.3.table, f32[4,4,128,128]{3,2,1,0:T(8,128)S(1)} %copy-done.2, f32[2,4,4,128,128]{4,3,2,1,0:T(8,128)S(1)} %bitcast.12, f32[4,4,128,128]{3,2,1,0:T(8,128)S(1)} %collective-permute-done.3.across, ...), custom_call_target="tpu_custom_call" | custom-call | tf_op jit(solution)/shard_map/pallas_call | solution.py:36
  86.0 2.9 %collective-permute-done.20.refs_0_ = f32[4,128,128]{2,1,0:T(8,128)S(1)} collective-permute-done((f32[4,128,128]{2,1,0:T(8,128)}, f32[4,128,128]{2,1,0:T(8,128)S(1)}, u32[]{:S(2)}, u32[]{:S(2)}) %collective-permute-start.20) | collective-permute-done | bytes 262176 | tf_op jit(solution)/shard_map/ppermute | solution.py:270
  88.9 0.3 collective-permute-start.22
  89.2 1.2 %collective-permute-done.21.refs_1_ = f32[4,128,128]{2,1,0:T(8,128)S(1)} collective-permute-done((f32[4,128,128]{2,1,0:T(8,128)S(1)}, f32[4,128,128]{2,1,0:T(8,128)S(1)}, u32[]{:S(2)}, u32[]{:S(2)}) %collective-permute-start.21) | collective-permute-done | bytes 262176 | tf_op jit(solution)/shard_map/ppermute | solution.py:270
  90.4 1.9 %shard_map.135 = (f32[1,4,128,128]{3,2,1,0:T(8,128)S(1)}, f32[1,128,128]{2,1,0:T(8,128)S(1)}, f32[1,2,128,128]{3,2,1,0:T(8,128)S(1)}) custom-call(s32[123]{0:T(128)S(1)} %concatenate.3.table, f32[4,4,128,128]{3,2,1,0:T(8,128)S(1)} %copy-done.2, f32[2,4,4,128,128]{4,3,2,1,0:T(8,128)S(1)} %bitcast.13, f32[4,4,128,128]{3,2,1,0:T(8,128)S(1)} %collective-permute-done.3.across, ...), custom_call_target="tpu_custom_call" | custom-call | tf_op jit(solution)/shard_map/pallas_call | solution.py:36
  92.3 0.6 collective-permute-start.23
  92.9 7.9 %collective-permute-done.22.refs_4_ = f32[3,2,128,128]{3,2,1,0:T(8,128)S(1)} collective-permute-done((f32[3,2,128,128]{3,2,1,0:T(8,128)S(1)}, f32[3,2,128,128]{3,2,1,0:T(8,128)S(1)}, u32[]{:S(2)}, u32[]{:S(2)}) %collective-permute-start.22) | collective-permute-done | bytes 393248 | tf_op jit(solution)/shard_map/ppermute | solution.py:270
  100.8 2.4 %collective-permute-done.23.refs_5_ = f32[1,2,128,128]{3,2,1,0:T(8,128)S(1)} collective-permute-done((f32[1,2,128,128]{3,2,1,0:T(8,128)S(1)}, f32[1,2,128,128]{3,2,1,0:T(8,128)S(1)}, u32[]{:S(2)}, u32[]{:S(2)}) %collective-permute-start.23) | collective-permute-done | bytes 131104 | tf_op jit(solution)/shard_map/ppermute | solution.py:270
  103.2 1.7 %shard_map.136 = (f32[4,4,128,128]{3,2,1,0:T(8,128)}, f32[4,128,128]{2,1,0:T(8,128)}) custom-call(s32[123]{0:T(128)S(1)} %concatenate.3.table, f32[3,4,128,128]{3,2,1,0:T(8,128)S(1)} %get-tuple-element.60.refs_0_, f32[1,4,128,128]{3,2,1,0:T(8,128)S(1)} %get-tuple-element.64.refs_1_, f32[3,128,128]{2,1,0:T(8,128)S(1)} %get-tuple-element.65.refs_2_, ...), custom_call_target="tpu_custom_call" | custom-call | tf_op jit(solution)/shard_map/pallas_call | solution.py:36
  (38 shorter events, 0.1 us)
Async XLA Ops:
  7.2 20.5 %copy-start.3 = (f32[2,4,128,128]{3,2,1,0:T(8,128)S(1)}, f32[2,4,128,128]{3,2,1,0:T(8,128)}, u32[]{:S(2)}) copy-start(f32[2,4,128,128]{3,2,1,0:T(8,128)} %own.4) | copy-start | bytes 1572868
  7.2 19.1 %copy-start.2 = (f32[4,4,128,128]{3,2,1,0:T(8,128)S(1)}, f32[4,4,128,128]{3,2,1,0:T(8,128)}, u32[]{:S(2)}) copy-start(f32[4,4,128,128]{3,2,1,0:T(8,128)} %own.7) | copy-start | bytes 3145732
  7.2 34.7 %copy-start.6 = (f32[1,128,4,256]{3,2,1,0:T(4,128)S(1)}, f32[1,128,4,256]{3,2,1,0:T(4,128)}, u32[]{:S(2)}) copy-start(f32[1,128,4,256]{3,2,1,0:T(4,128)} %param.10) | copy-start | bytes 1572868
  7.2 34.3 %copy-start.13 = (s32[8,4]{0,1:T(4,128)S(1)}, s32[8,4]{0,1:T(4,128)}, u32[]{:S(2)}) copy-start(s32[8,4]{0,1:T(4,128)} %param.15) | copy-start | bytes 388
  7.2 34.4 %copy-start.14 = (s32[16,3]{0,1:T(4,128)S(1)}, s32[16,3]{0,1:T(4,128)}, u32[]{:S(2)}) copy-start(s32[16,3]{0,1:T(4,128)} %param.19) | copy-start | bytes 580
  7.2 34.5 %copy-start.15 = (s32[8]{0:T(128)S(1)}, s32[8]{0:T(128)}, u32[]{:S(2)}) copy-start(s32[8]{0:T(128)} %param.16) | copy-start | bytes 100
  7.2 34.5 %copy-start.16 = (s32[16]{0:T(128)S(1)}, s32[16]{0:T(128)}, u32[]{:S(2)}) copy-start(s32[16]{0:T(128)} %param.17) | copy-start | bytes 196
  7.2 34.5 %copy-start.17 = (s32[16]{0:T(128)S(1)}, s32[16]{0:T(128)}, u32[]{:S(2)}) copy-start(s32[16]{0:T(128)} %param.18) | copy-start | bytes 196
  7.2 34.6 %all-gather.5.cloned.1.call-start = ((), (), s32[]{:S(2)}) async-start(), calls=%async_computation | async-start | bytes 1572864 | tf_op jit(solution)/shard_map/all_gather | solution.py:293
  8.0 63.2 %all-gather.7.cloned.1.call-start = ((), (), s32[]{:S(2)}) async-start(), calls=%async_computation.1 | async-start | bytes 3145728 | tf_op jit(solution)/shard_map/all_gather | solution.py:294
  9.7 12.4 %collective-permute-start.1 = (f32[64,4,256]{2,1,0:T(4,128)S(1)}, f32[64,4,256]{2,1,0:T(4,128)}, u32[]{:S(2)}, u32[]{:S(2)}) collective-permute-start(f32[64,4,256]{2,1,0:T(4,128)S(1)} %dynamic-slice_bitcast_fusion), channel_id=1, source_target_pairs={{0,4},{4,8},{8,12},{12,0},{1,5},{5,9},{9,13},{13,1},{2,6},{6,10},{... | collective-permute-start | bytes 786440 | tf_op jit(solution)/shard_map/ppermute | solution.py:270
  12.8 13.5 %collective-permute-start.2 = (f32[64,4,256]{2,1,0:T(4,128)S(1)}, f32[64,4,256]{2,1,0:T(4,128)}, u32[]{:S(2)}, u32[]{:S(2)}) collective-permute-start(f32[64,4,256]{2,1,0:T(4,128)S(1)} %dynamic-slice_bitcast_fusion), channel_id=1, source_target_pairs={{0,12},{4,0},{8,4},{12,8},{1,13},{5,1},{9,5},{13,9},{2,14},{6,2},{... | collective-permute-start | bytes 786440 | tf_op jit(solution)/shard_map/ppermute | solution.py:270
  26.3 15.2 %collective-permute-start.3 = (f32[4,4,128,128]{3,2,1,0:T(8,128)S(1)}, f32[4,4,128,128]{3,2,1,0:T(8,128)S(1)}, u32[]{:S(2)}, u32[]{:S(2)}) collective-permute-start(f32[4,4,128,128]{3,2,1,0:T(8,128)S(1)} %copy-done.2), channel_id=1, source_target_pairs={{0,1},{1,0},{2,3},{3,2},{4,5},{5,4},{6,7},{7,6},{8,9},{9,8},{10,11... | collective-permute-start | bytes 3145736 | tf_op jit(solution)/shard_map/ppermute | solution.py:270
  26.3 15.2 %collective-permute-start = (f32[64,4,256]{2,1,0:T(4,128)S(1)}, f32[64,4,256]{2,1,0:T(4,128)S(1)}, u32[]{:S(2)}, u32[]{:S(2)}) collective-permute-start(f32[64,4,256]{2,1,0:T(4,128)S(1)} %dynamic-slice_bitcast_fusion), channel_id=1, source_target_pairs={{0,8},{4,12},{8,0},{12,4},{1,9},{5,13},{9,1},{13,5},{2,10},{6,14},... | collective-permute-start | bytes 786440 | tf_op jit(solution)/shard_map/ppermute | solution.py:270
  27.7 19.4 %collective-permute-start.7 = (f32[2,4,128,128]{3,2,1,0:T(8,128)S(1)}, f32[2,4,128,128]{3,2,1,0:T(8,128)}, u32[]{:S(2)}, u32[]{:S(2)}) collective-permute-start(f32[2,4,128,128]{3,2,1,0:T(8,128)S(1)} %copy-done.3), channel_id=1, source_target_pairs={{0,1},{1,0},{2,3},{3,2},{4,5},{5,4},{6,7},{7,6},{8,9},{9,8},{10,11... | collective-permute-start | bytes 1572872 | tf_op jit(solution)/shard_map/ppermute | solution.py:270
  27.8 14.0 %collective-permute-start.5 = (f32[64,4,256]{2,1,0:T(4,128)}, f32[64,4,256]{2,1,0:T(4,128)}, u32[]{:S(2)}, u32[]{:S(2)}) collective-permute-start(f32[64,4,256]{2,1,0:T(4,128)} %collective-permute-done.1.refs_0_), channel_id=1, source_target_pairs={{0,1},{1,0},{2,3},{3,2},{4,5},{5,4},{6,7},{7,6},{8,9},{9,8},{10,11... | collective-permute-start | bytes 786440 | tf_op jit(solution)/shard_map/ppermute | solution.py:270
  28.2 13.6 %collective-permute-start.6 = (f32[64,4,256]{2,1,0:T(4,128)}, f32[64,4,256]{2,1,0:T(4,128)}, u32[]{:S(2)}, u32[]{:S(2)}) collective-permute-start(f32[64,4,256]{2,1,0:T(4,128)} %collective-permute-done.2.refs_1_), channel_id=1, source_target_pairs={{0,1},{1,0},{2,3},{3,2},{4,5},{5,4},{6,7},{7,6},{8,9},{9,8},{10,11... | collective-permute-start | bytes 786440 | tf_op jit(solution)/shard_map/ppermute | solution.py:270
  41.5 5.5 %collective-permute-start.4 = (f32[64,4,256]{2,1,0:T(4,128)S(1)}, f32[64,4,256]{2,1,0:T(4,128)}, u32[]{:S(2)}, u32[]{:S(2)}) collective-permute-start(f32[64,4,256]{2,1,0:T(4,128)S(1)} %collective-permute-done.far), channel_id=1, source_target_pairs={{0,1},{1,0},{2,3},{3,2},{4,5},{5,4},{6,7},{7,6},{8,9},{9,8},{10,11... | collective-permute-start | bytes 786440 | tf_op jit(solution)/shard_map/ppermute | solution.py:270
  41.9 1.4 %copy-start.7 = (f32[4,4,128,128]{3,2,1,0:T(8,128)S(1)}, f32[4,4,128,128]{3,2,1,0:T(8,128)}, u32[]{:S(2)}) copy-start(f32[4,4,128,128]{3,2,1,0:T(8,128)} %all-gather.5.cloned.1.call-done) | copy-start | bytes 3145732
  45.9 1.1 %copy-start.4 = (f32[384,1024]{1,0:T(8,128)}, f32[384,1024]{1,0:T(8,128)S(1)}, u32[]{:S(2)}) copy-start(f32[384,1024]{1,0:T(8,128)S(1)} %get-tuple-element.49.whole) | copy-start | bytes 4718596
  47.0 12.0 %copy-start.11 = (f32[2,128,128]{2,1,0:T(8,128)S(1)}, f32[2,128,128]{2,1,0:T(8,128)}, u32[]{:S(2)}) copy-start(f32[2,128,128]{2,1,0:T(8,128)} %diagonal.3) | copy-start | bytes 393220
  50.1 10.3 %copy-start.9 = (f32[3,128,128]{2,1,0:T(8,128)}, f32[3,128,128]{2,1,0:T(8,128)S(1)}, u32[]{:S(2)}) copy-start(f32[3,128,128]{2,1,0:T(8,128)S(1)} %get-tuple-element.54.refs_0_) | copy-start | bytes 589828
  50.1 9.0 %collective-permute-start.8 = (f32[2,128,128]{2,1,0:T(8,128)S(1)}, f32[2,128,128]{2,1,0:T(8,128)S(1)}, u32[]{:S(2)}, u32[]{:S(2)}) collective-permute-start(f32[2,128,128]{2,1,0:T(8,128)S(1)} %get-tuple-element.44), channel_id=1, source_target_pairs={{0,2},{2,0},{1,3},{3,1},{4,6},{6,4},{5,7},{7,5},{8,10},{10,8},{9,1... | collective-permute-start | bytes 393224 | tf_op jit(solution)/shard_map/ppermute | solution.py:270
  51.6 13.3 %collective-permute-start.9 = (f32[3,128,128]{2,1,0:T(8,128)S(1)}, f32[3,128,128]{2,1,0:T(8,128)S(1)}, u32[]{:S(2)}, u32[]{:S(2)}) collective-permute-start(f32[3,128,128]{2,1,0:T(8,128)S(1)} %get-tuple-element.47), channel_id=1, source_target_pairs={{0,4},{4,8},{8,12},{12,0},{1,5},{5,9},{9,13},{13,1},{2,6},{6,10},{... | collective-permute-start | bytes 589832 | tf_op jit(solution)/shard_map/ppermute | solution.py:270
  51.6 21.8 %collective-permute-start.16 = (f32[3,128,128]{2,1,0:T(8,128)}, f32[3,128,128]{2,1,0:T(8,128)S(1)}, u32[]{:S(2)}, u32[]{:S(2)}) collective-permute-start(f32[3,128,128]{2,1,0:T(8,128)} %get-tuple-element.58), channel_id=1, source_target_pairs={{0,12},{4,0},{8,4},{12,8},{1,13},{5,1},{9,5},{13,9},{2,14},{6,2},{... | collective-permute-start | bytes 589832 | tf_op jit(solution)/shard_map/ppermute | solution.py:270
  60.3 0.7 copy-start.12
  61.0 6.4 %collective-permute-start.14 = (f32[128,128]{1,0:T(8,128)S(1)}, f32[128,128]{1,0:T(8,128)}, u32[]{:S(2)}, u32[]{:S(2)}) collective-permute-start(f32[128,128]{1,0:T(8,128)S(1)} %get-tuple-element.57), channel_id=1, source_target_pairs={{0,4},{4,8},{8,12},{12,0},{1,5},{5,9},{9,13},{13,1},{2,6},{6,10},{... | collective-permute-start | bytes 196616 | tf_op jit(solution)/shard_map/ppermute | solution.py:270
  61.0 6.4 %collective-permute-start.18 = (f32[128,128]{1,0:T(8,128)S(1)}, f32[128,128]{1,0:T(8,128)}, u32[]{:S(2)}, u32[]{:S(2)}) collective-permute-start(f32[128,128]{1,0:T(8,128)S(1)} %get-tuple-element.59), channel_id=1, source_target_pairs={{0,12},{4,0},{8,4},{12,8},{1,13},{5,1},{9,5},{13,9},{2,14},{6,2},{... | collective-permute-start | bytes 196616 | tf_op jit(solution)/shard_map/ppermute | solution.py:270
  64.9 11.0 %collective-permute-start.12 = (f32[128,128]{1,0:T(8,128)}, f32[128,128]{1,0:T(8,128)}, u32[]{:S(2)}, u32[]{:S(2)}) collective-permute-start(f32[128,128]{1,0:T(8,128)} %get-tuple-element.56.refs_2_), channel_id=1, source_target_pairs={{0,1},{1,0},{2,3},{3,2},{4,5},{5,4},{6,7},{7,6},{8,9},{9,8},{10,11... | collective-permute-start | bytes 196616 | tf_op jit(solution)/shard_map/ppermute | solution.py:270
  67.5 8.6 %collective-permute-start.15 = (f32[128,128]{1,0:T(8,128)}, f32[128,128]{1,0:T(8,128)}, u32[]{:S(2)}, u32[]{:S(2)}) collective-permute-start(f32[128,128]{1,0:T(8,128)} %collective-permute-done.14.refs_6_), channel_id=1, source_target_pairs={{0,1},{1,0},{2,3},{3,2},{4,5},{5,4},{6,7},{7,6},{8,9},{9,8},{10,11... | collective-permute-start | bytes 196616 | tf_op jit(solution)/shard_map/ppermute | solution.py:270
  67.5 8.9 %collective-permute-start.19 = (f32[128,128]{1,0:T(8,128)}, f32[128,128]{1,0:T(8,128)}, u32[]{:S(2)}, u32[]{:S(2)}) collective-permute-start(f32[128,128]{1,0:T(8,128)} %collective-permute-done.18.refs_10_), channel_id=1, source_target_pairs={{0,1},{1,0},{2,3},{3,2},{4,5},{5,4},{6,7},{7,6},{8,9},{9,8},{10,11... | collective-permute-start | bytes 196616 | tf_op jit(solution)/shard_map/ppermute | solution.py:270
  71.2 1.6 %copy-start = (f32[8,4,128,128]{3,2,1,0:T(8,128)S(1)}, f32[8,4,128,128]{3,2,1,0:T(8,128)}, u32[]{:S(2)}) copy-start(f32[8,4,128,128]{3,2,1,0:T(8,128)} %all-gather.7.cloned.1.call-done) | copy-start | bytes 6291460
  72.8 3.1 %copy-start.10 = (f32[3,128,128]{2,1,0:T(8,128)S(1)}, f32[3,128,128]{2,1,0:T(8,128)}, u32[]{:S(2)}) copy-start(f32[3,128,128]{2,1,0:T(8,128)} %copy-done.9) | copy-start | bytes 589828
  72.8 3.8 %copy-start.1 = (f32[8,4,128,128]{3,2,1,0:T(8,128)S(1)}, f32[8,4,128,128]{3,2,1,0:T(8,128)}, u32[]{:S(2)}) copy-start(f32[8,4,128,128]{3,2,1,0:T(8,128)} %all-gather.7.cloned.1.call-done) | copy-start | bytes 6291460
  73.3 8.5 %collective-permute-start.10 = (f32[4,128,128]{2,1,0:T(8,128)S(1)}, f32[4,128,128]{2,1,0:T(8,128)S(1)}, u32[]{:S(2)}, u32[]{:S(2)}) collective-permute-start(f32[4,128,128]{2,1,0:T(8,128)S(1)} %shard_map.132), channel_id=1, source_target_pairs={{0,1},{1,0},{2,3},{3,2},{4,5},{5,4},{6,7},{7,6},{8,9},{9,8},{10,11... | collective-permute-start | bytes 786440 | tf_op jit(solution)/shard_map/ppermute | solution.py:270
  73.4 15.4 %collective-permute-start.20 = (f32[4,128,128]{2,1,0:T(8,128)}, f32[4,128,128]{2,1,0:T(8,128)S(1)}, u32[]{:S(2)}, u32[]{:S(2)}) collective-permute-start(f32[4,128,128]{2,1,0:T(8,128)} %copy-done.12), channel_id=1, source_target_pairs={{0,8},{4,12},{8,0},{12,4},{1,9},{5,13},{9,1},{13,5},{2,10},{6,14},... | collective-permute-start | bytes 786440 | tf_op jit(solution)/shard_map/ppermute | solution.py:270
  75.9 5.9 %collective-permute-start.11 = (f32[3,128,128]{2,1,0:T(8,128)S(1)}, f32[3,128,128]{2,1,0:T(8,128)S(1)}, u32[]{:S(2)}, u32[]{:S(2)}) collective-permute-start(f32[3,128,128]{2,1,0:T(8,128)S(1)} %copy-done.10), channel_id=1, source_target_pairs={{0,1},{1,0},{2,3},{3,2},{4,5},{5,4},{6,7},{7,6},{8,9},{9,8},{10,11... | collective-permute-start | bytes 589832 | tf_op jit(solution)/shard_map/ppermute | solution.py:270
  76.1 5.7 %collective-permute-start.13 = (f32[3,128,128]{2,1,0:T(8,128)S(1)}, f32[3,128,128]{2,1,0:T(8,128)S(1)}, u32[]{:S(2)}, u32[]{:S(2)}) collective-permute-start(f32[3,128,128]{2,1,0:T(8,128)S(1)} %collective-permute-done.9.refs_4_), channel_id=1, source_target_pairs={{0,1},{1,0},{2,3},{3,2},{4,5},{5,4},{6,7},{7,6},{8,9},{9,8},{10,11... | collective-permute-start | bytes 589832 | tf_op jit(solution)/shard_map/ppermute | solution.py:270
  76.4 5.4 %collective-permute-start.17 = (f32[3,128,128]{2,1,0:T(8,128)S(1)}, f32[3,128,128]{2,1,0:T(8,128)S(1)}, u32[]{:S(2)}, u32[]{:S(2)}) collective-permute-start(f32[3,128,128]{2,1,0:T(8,128)S(1)} %collective-permute-done.16.refs_8_), channel_id=1, source_target_pairs={{0,1},{1,0},{2,3},{3,2},{4,5},{5,4},{6,7},{7,6},{8,9},{9,8},{10,11... | collective-permute-start | bytes 589832 | tf_op jit(solution)/shard_map/ppermute | solution.py:270
  76.6 1.4 %copy-start.5 = (f32[384,1024]{1,0:T(8,128)S(1)}, f32[384,1024]{1,0:T(8,128)}, u32[]{:S(2)}) copy-start(f32[384,1024]{1,0:T(8,128)} %copy-done.4) | copy-start | bytes 4718596
  78.0 3.8 %copy-start.8 = (f32[4,128,128]{2,1,0:T(8,128)S(1)}, f32[4,128,128]{2,1,0:T(8,128)}, u32[]{:S(2)}) copy-start(f32[4,128,128]{2,1,0:T(8,128)} %diagonal.5) | copy-start | bytes 786436
  88.9 1.5 %collective-permute-start.21 = (f32[4,128,128]{2,1,0:T(8,128)S(1)}, f32[4,128,128]{2,1,0:T(8,128)S(1)}, u32[]{:S(2)}, u32[]{:S(2)}) collective-permute-start(f32[4,128,128]{2,1,0:T(8,128)S(1)} %collective-permute-done.20.refs_0_), channel_id=1, source_target_pairs={{0,1},{1,0},{2,3},{3,2},{4,5},{5,4},{6,7},{7,6},{8,9},{9,8},{10,11... | collective-permute-start | bytes 786440 | tf_op jit(solution)/shard_map/ppermute | solution.py:270
  88.9 11.9 %collective-permute-start.22 = (f32[3,2,128,128]{3,2,1,0:T(8,128)S(1)}, f32[3,2,128,128]{3,2,1,0:T(8,128)S(1)}, u32[]{:S(2)}, u32[]{:S(2)}) collective-permute-start(f32[3,2,128,128]{3,2,1,0:T(8,128)S(1)} %get-tuple-element.62), channel_id=1, source_target_pairs={{0,2},{2,0},{1,3},{3,1},{4,6},{6,4},{5,7},{7,5},{8,10},{10,8},{9,1... | collective-permute-start | bytes 1179656 | tf_op jit(solution)/shard_map/ppermute | solution.py:270
  92.3 10.9 %collective-permute-start.23 = (f32[1,2,128,128]{3,2,1,0:T(8,128)S(1)}, f32[1,2,128,128]{3,2,1,0:T(8,128)S(1)}, u32[]{:S(2)}, u32[]{:S(2)}) collective-permute-start(f32[1,2,128,128]{3,2,1,0:T(8,128)S(1)} %get-tuple-element.67), channel_id=1, source_target_pairs={{0,2},{2,0},{1,3},{3,1},{4,6},{6,4},{5,7},{7,5},{8,10},{10,8},{9,1... | collective-permute-start | bytes 393224 | tf_op jit(solution)/shard_map/ppermute | solution.py:270
Sparse Core Ops, SparseCore 0:
  9.6 23.9 all-gather.4
  35.2 35.9 all-gather.6

commit v3 on v2

--- a/solution.py
+++ b/solution.py
@@ -40,7 +40,7 @@
         out_specs=tuple([VMEM] * len(out_shapes)),
         scratch_shapes=[pltpu.VMEM(s, F32) for s in scratch],
         compiler_params=pltpu.CompilerParams(vmem_limit_bytes=40 * 1024 * 1024),
-        cost_estimate=pl.CostEstimate(flops=0, bytes_accessed=0, transcendentals=0),
+        cost_estimate=pl.CostEstimate(flops=flops, bytes_accessed=0, transcendentals=0),
     )(table, *operands)
 
 
@@ -98,20 +98,15 @@
             out[pl.ds(pl.multiple_of(at + first, rows // 2), part.shape[0]), b * width : (b + 1) * width] = part[:, b, :]
 
 
-EARLY, LATE = (1, 3), 2
-
-
-def early_kernel(sizes, table, root, *refs):
+SINGLE, LATE = (1, 3), 2
+GROUPS = ((0,), SINGLE, (LATE,))
+LONG = 20_000_000_000
+
+
+def early_kernel(sizes, table, root, own, beside, first, spread, total):
     tree = Tree(table, *sizes)
-    n = len(EARLY)
-    far, near = refs[:n], refs[n : 2 * n]
-    own, beside, whole, spread, total = refs[2 * n :]
-    beside = beside.at[1 - tree.row]
     per_one, blocks, rows, cols = own.shape
-    half = rows // 2
-    fill_rows(whole, 0, rows, [(0, root)])
-    for i in range(n):
-        fill_rows(whole, (i + 1) * rows, rows, [(tree.sub * half, far[i]), ((1 - tree.sub) * half, near[i])])
+    fill_rows(first, 0, rows, [(0, root)])
     for g in range(per_one):
         for a in range(blocks):
             one = tree.me * per_one + g
@@ -119,22 +114,25 @@
             lanes = slice(g * cols, (g + 1) * cols)
             spread[spot(at * 2 + tree.row, rows), lanes] = own[g, a] * valid
             spread[spot(at * 2 + 1 - tree.row, rows), lanes] = beside[g, a] * valid
-    total[...] = mm(whole[...], spread[...])
-
-
-def late_kernel(sizes, table, far, near, spread, total, own, across, rest, cov, keep, send, *refs):
+    total[...] = mm(first[...], spread[...])
+
+
+def late_kernel(sizes, table, spread, total, own, across, *refs):
     tree = Tree(table, *sizes)
-    picks = refs[: tree.nodes]
-    wide, tall, part = refs[tree.nodes :]
+    shifts = tree.nodes - 1
+    far, near = refs[:shifts], refs[shifts : 2 * shifts]
+    rest, cov, keep, send, *picks = refs[2 * shifts : 2 * shifts + 4 + tree.nodes]
+    wide, tall, part = refs[2 * shifts + 4 + tree.nodes :]
     per_one, blocks, rows, cols = own.shape
     half = rows // 2
-    fill_rows(rest, 0, rows, [(tree.sub * half, far), ((1 - tree.sub) * half, near)])
-    last = mm(rest[...], spread[...])
+    for i in range(shifts):
+        fill_rows(rest, i * rows, rows, [(tree.sub * half, far[i]), ((1 - tree.sub) * half, near[i])])
+    others = mm(rest[...], spread[...])
     for g in range(per_one):
         lanes = slice(g * cols, (g + 1) * cols)
-        for i, k in enumerate((0,) + EARLY):
-            tall[g, k] = total[i * rows : (i + 1) * rows, lanes]
-        tall[g, LATE] = last[:, lanes]
+        tall[g, 0] = total[:, lanes]
+        for i in range(shifts):
+            tall[g, i + 1] = others[i * rows : (i + 1) * rows, lanes]
     for g in range(per_one):
         one = tree.me * per_one + g
         for a in range(blocks):
@@ -155,42 +153,43 @@
         send[g] = part[spot(1 - tree.row, rows), :]
 
 
-def diag_one_kernel(sizes, table, diagonal, keep, got, cross, out, *tops):
+def diag_one_kernel(sizes, table, diagonal, keep, got, pick, out, *tops):
     tree = Tree(table, *sizes)
     out[...] = diagonal[...] + (keep[...] + got[...])
     for k in range(tree.nodes):
         target = tree.node(k)
         slot = tree.slot(target * tree.per_two + tree.child(target, tree.me))
         if k == LATE:
-            tops[k][: A - 1] = cross[...]
+            tops[k][: A - 1] = pick[...]
             tops[k][A - 1] = out[slot]
         else:
             tops[k][...] = out[slot]
 
 
-def first_blocks_kernel(sizes, table, panel, out):
-    tree = Tree(table, *sizes)
-    out[...] = panel[1 - tree.row, :, 0]
-
-
-def root_two_kernel(sizes, table, whole, rest, own, beside, across, lower, inner, spread, wide, tall):
+def first_blocks_kernel(sizes, table, panel, later, out):
+    soon = panel.shape[0]
+    out[:soon] = panel[:, 0]
+    out[soon:] = later[:, 0]
+
+
+def root_two_kernel(sizes, table, first, rest, own, beside, later, across, lower, inner, spread, wide, tall):
     tree = Tree(table, *sizes)
     per_two, blocks, rows, cols = own.shape
-    beside = beside.at[1 - tree.row]
+    soon = beside.shape[0]
     spread[...] = jnp.zeros_like(spread)
     for h in range(per_two):
         valid, at = tree.level_two(h)
         lanes = slice(h * cols, (h + 1) * cols)
         for t in range(1, blocks):
             spread[spot(at[t - 1] * 2 + tree.row, rows), lanes] = own[h, t] * valid[t]
-            spread[spot(at[t - 1] * 2 + 1 - tree.row, rows), lanes] = beside[h, t] * valid[t]
-    most = mm(whole[...], spread[...])
-    last = mm(rest[...], spread[...])
+            spread[spot(at[t - 1] * 2 + 1 - tree.row, rows), lanes] = (beside[h, t] if h < soon else later[h - soon, t]) * valid[t]
+    mine = mm(first[...], spread[...])
+    others = mm(rest[...], spread[...])
     for h in range(per_two):
         lanes = slice(h * cols, (h + 1) * cols)
-        for i, k in enumerate((0,) + EARLY):
-            tall[h, k] = most[i * rows : (i + 1) * rows, lanes]
-        tall[h, LATE] = last[:, lanes]
+        tall[h, 0] = mine[:, lanes]
+        for k in range(1, tree.nodes):
+            tall[h, k] = others[(k - 1) * rows : k * rows, lanes]
     for h in range(per_two):
         valid, at = tree.level_two(h)
         for t in range(1, blocks):
@@ -200,11 +199,10 @@
         inner[h] = mm_t(wide[...], lower[h].reshape((blocks - 1) * rows, cols))
 
 
-def parent_two_kernel(sizes, shifts, table, own, beside, across, corner, lower, inner, diagonal, *refs):
+def parent_two_kernel(sizes, shifts, table, own, first_beside, across, corner, lower, inner, diagonal, *refs):
     tree = Tree(table, *sizes)
     row, sub = tree.row, tree.sub
     blocks, rows, cols = own.shape[1:]
-    beside = beside.at[1 - row]
     refs = list(refs)
     ins = []
     for k in shifts:
@@ -231,12 +229,12 @@
         top[:, spot(sub, cols)] = top_own[...]
         top[:, spot(1 - sub, cols)] = top_side[...]
         first[spot(row, rows), :] = own[h, 0]
-        first[spot(1 - row, rows), :] = beside[h, 0]
+        first[spot(1 - row, rows), :] = first_beside[h]
         mine = spot(blocks - 1 + row, rows)
         other = spot(blocks - row, rows)
         wide[mine, spot(sub, cols)] = own[h, 0]
         wide[mine, spot(1 - sub, cols)] = across[h, 0]
-        wide[other, spot(sub, cols)] = beside[h, 0]
+        wide[other, spot(sub, cols)] = first_beside[h]
         wide[other, spot(1 - sub, cols)] = corner[h]
         below = mm(cross[...], first[...])
         for t in range(1, blocks):
@@ -289,69 +287,69 @@
 
     root = root_inverse[0]
     half = lax.dynamic_slice_in_dim(root, sub * (rows // 2), rows // 2, 0)
-    far = {k: shift(half, "node", k) for k in EARLY + (LATE,)}
-    beside_one = lax.all_gather(panel_one, "row")
-    beside_two = lax.all_gather(panel_two, "row")
-    across_one = shift(after(panel_one, *[far[k] for k in EARLY]), "sub", 1)
-    across_two = shift(after(panel_two, *[far[k] for k in EARLY]), "sub", 1)
-    near = {k: shift(far[k], "sub", 1) for k in EARLY}
-    near[LATE] = shift(after(far[LATE], across_two), "sub", 1)
-
-    n = len(EARLY) + 1
-    whole, spread, total = call(
+    far = [shift(half, "node", k) for k in range(1, nodes)]
+    beside_one = shift(panel_one, "row", 1)
+    soon = per_two // 2
+    beside_soon = shift(panel_two[:soon], "row", 1)
+    first, spread, total = call(
         bind(early_kernel),
-        [array(n * rows, full), array(full, per_one * cols), array(n * rows, per_one * cols)],
+        [array(rows, full), array(full, per_one * cols), array(rows, per_one * cols)],
         table,
-        [root] + [far[k] for k in EARLY] + [near[k] for k in EARLY] + [panel_one, beside_one],
-        flops=6 * n * rows * full * per_one * cols,
-    )
+        [root, panel_one, beside_one],
+    )
+    *far, beside_soon, total = lax.optimization_barrier((*far, beside_soon, total))
+    near = [shift(x, "sub", 1) for x in far]
+    across_one = shift(after(panel_one, total), "sub", 1)
     out = call(
         bind(late_kernel),
-        [array(rows, full), array(*panel_one.shape), array(per_one, rows, cols), array(per_one, rows, cols)]
+        [array((nodes - 1) * rows, full), array(*panel_one.shape), array(per_one, rows, cols), array(per_one, rows, cols)]
         + [array(blocks - 1, rows, cols)] * nodes,
         table,
-        [far[LATE], near[LATE], spread, total, panel_one, across_one],
+        [spread, total, panel_one, across_one] + far + near,
         [(blocks * rows, 2 * cols), (per_one, nodes, rows, cols), (2 * rows, cols)],
-        flops=6 * rows * full * per_one * cols,
     )
     rest, cov_panel_one, keep, send = out[:4]
     picks = out[4:]
-    cross = {k: shift(picks[k], "node", k) for k in EARLY}
+    got = shift(send, "row", 1)
+    beside_later = shift(after(panel_two[soon:], got), "row", 1)
+    cross = {k: shift(picks[k], "node", k) for k in SINGLE}
+    across_two = shift(after(panel_two, send), "sub", 1)
     out = call(
         bind(diag_one_kernel),
         [array(*diag_one.shape)] + [array(blocks, rows, cols) if k == LATE else array(rows, cols) for k in range(nodes)],
         table,
-        [diag_one, keep, shift(send, "row", 1), picks[LATE]],
+        [diag_one, keep, got, picks[LATE]],
     )
     cov_diag_one = out[0]
-    arrived = {k: [cross[k], shift(out[1 + k], "node", k)] for k in EARLY}
-    arrived[0] = [after(x, cross[EARLY[0]]) for x in (picks[0], out[1])]
-    arrived[LATE] = [shift(out[1 + LATE], "node", LATE)]
-
-    corner_two = shift(call(bind(first_blocks_kernel), [array(per_two, rows, cols)], table, [after(beside_two, cross[EARLY[0]])])[0], "sub", 1)
+    tops = {k: out[1 + k] if k == 0 else shift(out[1 + k], "node", k) for k in range(nodes)}
+    (first_beside,) = call(bind(first_blocks_kernel), [array(per_two, rows, cols)], table, [beside_soon, beside_later])
+    corner_two = shift(first_beside, "sub", 1)
+    *arrived, panel_early = lax.optimization_barrier((*cross.values(), picks[0], tops[0], panel_two))
+    cross_side = [shift(x, "sub", 1) for x in arrived]
     lower, inner = call(
         bind(root_two_kernel),
         [array(per_two, blocks - 1, rows, cols), array(per_two, 2 * rows, cols)],
         table,
-        [whole, rest, panel_two, beside_two, across_two],
+        [first, rest, panel_early, beside_soon, beside_later, across_two],
         [(full, per_two * cols), (low, 2 * cols), (per_two, nodes, rows, cols)],
-        flops=6 * rows * nodes * full * per_two * cols,
-    )
-    groups = ((0,) + EARLY, (LATE,))
+        flops=LONG,
+    )
+    parent = {0: [arrived[-2], cross_side[-2], arrived[-1], cross_side[-1]]}
+    for i, k in enumerate(SINGLE):
+        top = after(tops[k], lower)
+        parent[k] = [arrived[i], cross_side[i], top, shift(top, "sub", 1)]
+    groups = GROUPS
     panels, diags, gots = [], [], []
     for shifts in groups:
-        extra = []
-        for k in shifts:
-            for x in arrived[k]:
-                if gots:
-                    x = after(x, sends)
-                extra += [x, shift(x, "sub", 1)]
+        if shifts == (LATE,):
+            both = after(tops[LATE], sends)
+            parent[LATE] = [both, shift(both, "sub", 1)]
         panel, diag, sends = call(
             bind(parent_two_kernel, shifts),
             [array(len(shifts), blocks, rows, cols), array(len(shifts), rows, cols), array(len(shifts), 2, rows, cols)],
             table,
-            [panel_two, beside_two, across_two, corner_two, lower, inner, diag_two]
-            + extra,
+            [panel_two, first_beside, across_two, corner_two, lower, inner, diag_two]
+            + [x for k in shifts for x in parent[k]],
             [
                 (low, 2 * cols),
                 (rows, 2 * cols),
@@ -361,7 +359,6 @@
                 (low + 2 * rows, cols),
                 (2 * rows, cols),
             ],
-            flops=len(shifts) * 36 * low * cols * 2 * cols,
         )
         panels.append(panel)
         diags.append(diag)

time: 112 us -> 88.4 us (0.79)
  waiting for transfers between devices: 49.9 us -> 36.2 us
  between operations: 14.3 us -> 0.81 us
  starting transfers between devices: 21 us -> 29.5 us
  local copies, waits for them, and re-layouts: 7.45 us -> 3.07 us
    ppermute x24 -> x28, waiting for transfers between devices: 45.3 us -> 36.2 us  [shift(): return lax.ppermute(x, axis, [(i, (i + k) % n) for i in range(n)])]
    ppermute x24 -> x28, starting transfers between devices: 20.9 us -> 29.5 us  [shift(): return lax.ppermute(x, axis, [(i, (i + k) % n) for i in range(n)])]
    unnamed x36 -> x20, local copies, waits for them, and re-layouts: 6.24 us -> 0.04 us
    all_gather x2 -> x0, waiting for transfers between devices: 3.2 us -> none  [the longest x1 3.18 us: paired_shards(): beside_two = lax.all_gather(panel_two, 'row')]
    slice x0 -> x1, local copies, waits for them, and re-layouts: none -> 2.06 us  [paired_shards(): beside_later = shift(after(panel_two[soon:], got), 'row', 1)]
    unnamed x2 -> x0, waiting for transfers between devices: 1.38 us -> none
    pallas_call x8 -> x9, Pallas kernels: 19.1 us -> 18.7 us  [call(): pl.pallas_call(body, out_shape=tuple(out_shapes), in_specs=[SMEM] + [VMEM...]
  transfers between devices with their start and end apart: 26 -> 28, of which waited for: 10 -> 15; matrix products, arithmetic and copies ran while one was open for 1% -> 3% of each run, Pallas kernels for 16% -> 15%
where the time goes in v3:
time: 88.4 us; the launch traced here: 88.3 us
  waiting for transfers between devices  36.2 us (41%)
  starting transfers between devices  29.5 us (33%)
  Pallas kernels  18.7 us (21%)
  local copies, waits for them, and re-layouts  3.07 us (3%)
    ppermute x28, waiting for transfers between devices, shift(): return lax.ppermute(x, axis, [(i, (i + k) % n) for i in range(n)])  36.2 us
    ppermute x28, starting transfers between devices, shift(): return lax.ppermute(x, axis, [(i, (i + k) % n) for i in range(n)])  29.5 us
    pallas_call x9, Pallas kernels, call(): pl.pallas_call(body, out_shape=tuple(out_shapes), in_specs=[SMEM] + [VMEM...  18.7 us
    slice x1, local copies, waits for them, and re-layouts, paired_shards(): beside_later = shift(after(panel_two[soon:], got), 'row', 1)  2.06 us
  transfers between devices with their start and end apart: 28, of which 15 were waited for; matrix products, arithmetic and copies ran while one was open for 3% of the time, Pallas kernels for 15%

profile of v3, /device:TPU:0, one launch (start us, length us, event | category | flops | bytes accessed | tf_op | source)
XLA Modules:
  0.0 88.3 jit_solution(15332310267027639023)
XLA Ops:
  0.7 3.0 %collective-permute-start = (f32[2,4,128,128]{3,2,1,0:T(8,128)}, f32[2,4,128,128]{3,2,1,0:T(8,128)S(1)}, u32[]{:S(2)}, u32[]{:S(2)}) collective-permute-start(f32[2,4,128,128]{3,2,1,0:T(8,128)} %own.6), channel_id=1, source_target_pairs={{0,2},{2,0},{1,3},{3,1},{4,6},{6,4},{5,7},{7,5},{8,10},{10,8},{9,1... | collective-permute-start | bytes 1572872 | tf_op jit(solution)/shard_map/ppermute | solution.py:268
  3.7 2.1 %fusion = (f32[2,4,128,128]{3,2,1,0:T(8,128)S(1)}, f32[2,4,128,128]{3,2,1,0:T(8,128)}) fusion(f32[4,4,128,128]{3,2,1,0:T(8,128)} %own.10), kind=kLoop, calls=%fused_computation.1 | loop fusion | bytes 2097152 | tf_op jit(solution)/shard_map/slice | solution.py:314
  5.8 0.2 collective-permute-start.4
  5.9 0.7 dynamic-slice_bitcast_fusion
  6.7 1.9 %collective-permute-start.1 = (f32[64,4,256]{2,1,0:T(4,128)}, f32[64,4,256]{2,1,0:T(4,128)S(1)}, u32[]{:S(2)}, u32[]{:S(2)}) collective-permute-start(f32[64,4,256]{2,1,0:T(4,128)} %dynamic-slice_bitcast_fusion), channel_id=1, source_target_pairs={{0,4},{4,8},{8,12},{12,0},{1,5},{5,9},{9,13},{13,1},{2,6},{6,10},{... | collective-permute-start | bytes 786440 | tf_op jit(solution)/shard_map/ppermute | solution.py:268
  8.6 2.6 %collective-permute-start.2 = (f32[64,4,256]{2,1,0:T(4,128)}, f32[64,4,256]{2,1,0:T(4,128)S(1)}, u32[]{:S(2)}, u32[]{:S(2)}) collective-permute-start(f32[64,4,256]{2,1,0:T(4,128)} %dynamic-slice_bitcast_fusion), channel_id=1, source_target_pairs={{0,8},{4,12},{8,0},{12,4},{1,9},{5,13},{9,1},{13,5},{2,10},{6,14},... | collective-permute-start | bytes 786440 | tf_op jit(solution)/shard_map/ppermute | solution.py:268
  11.2 1.3 %collective-permute-start.3 = (f32[64,4,256]{2,1,0:T(4,128)}, f32[64,4,256]{2,1,0:T(4,128)S(1)}, u32[]{:S(2)}, u32[]{:S(2)}) collective-permute-start(f32[64,4,256]{2,1,0:T(4,128)} %dynamic-slice_bitcast_fusion), channel_id=1, source_target_pairs={{0,12},{4,0},{8,4},{12,8},{1,13},{5,1},{9,5},{13,9},{2,14},{6,2},{... | collective-permute-start | bytes 786440 | tf_op jit(solution)/shard_map/ppermute | solution.py:268
  12.5 0.1 reshape.15
  12.6 0.1 reshape.16
  12.7 0.1 concatenate.3.table
  12.8 3.9 %collective-permute-done.beside = f32[2,4,128,128]{3,2,1,0:T(8,128)S(1)} collective-permute-done((f32[2,4,128,128]{3,2,1,0:T(8,128)}, f32[2,4,128,128]{3,2,1,0:T(8,128)S(1)}, u32[]{:S(2)}, u32[]{:S(2)}) %collective-permute-start) | collective-permute-done | bytes 524320 | tf_op jit(solution)/shard_map/ppermute | solution.py:268
  16.7 1.3 %shard_map.129 = (f32[128,1024]{1,0:T(8,128)S(1)}, f32[1024,256]{1,0:T(8,128)S(1)}, f32[128,256]{1,0:T(8,128)S(1)}) custom-call(s32[123]{0:T(128)S(1)} %concatenate.3.table, f32[128,4,256]{2,1,0:T(4,128)S(1)} %bitcast.8, f32[2,4,128,128]{3,2,1,0:T(8,128)S(1)} %copy-done.2, f32[2,4,128,128]{3,2,1,0:T(8,128)S(1)} %collective-permute-done.beside), custom_call_target="tpu_custom_call" | custom-call | tf_op jit(solution)/shard_map/pallas_call | solution.py:36
  17.9 0.2 collective-permute-done.1.refs_0_
  18.2 9.8 %collective-permute-done.2.refs_1_ = f32[64,4,256]{2,1,0:T(4,128)S(1)} collective-permute-done((f32[64,4,256]{2,1,0:T(4,128)}, f32[64,4,256]{2,1,0:T(4,128)S(1)}, u32[]{:S(2)}, u32[]{:S(2)}) %collective-permute-start.2) | collective-permute-done | bytes 262176 | tf_op jit(solution)/shard_map/ppermute | solution.py:268
  28.0 0.0 collective-permute-done.3.refs_2_
  28.0 0.5 collective-permute-start.6
  28.5 0.1 collective-permute-start.7
  28.5 0.4 collective-permute-start.8
  29.0 1.3 %collective-permute-done.6.refs_3_ = f32[64,4,256]{2,1,0:T(4,128)S(1)} collective-permute-done((f32[64,4,256]{2,1,0:T(4,128)S(1)}, f32[64,4,256]{2,1,0:T(4,128)S(1)}, u32[]{:S(2)}, u32[]{:S(2)}) %collective-permute-start.6) | collective-permute-done | bytes 262176 | tf_op jit(solution)/shard_map/ppermute | solution.py:268
  30.2 0.4 collective-permute-done.7.refs_4_
  30.6 0.4 collective-permute-done.8.refs_5_
  31.0 0.0 collective-permute-done.5.across
  31.0 3.4 %shard_map.130 = (f32[384,1024]{1,0:T(8,128)S(1)}, f32[2,4,128,128]{3,2,1,0:T(8,128)}, f32[2,128,128]{2,1,0:T(8,128)S(1)}, f32[2,128,128]{2,1,0:T(8,128)S(1)}, f...) custom-call(s32[123]{0:T(128)S(1)} %concatenate.3.table, ...), custom_call_target="tpu_custom_call" | custom-call | tf_op jit(solution)/shard_map/pallas_call | solution.py:36
  34.4 0.2 collective-permute-start.11
  34.6 1.5 %collective-permute-start.9 = (f32[2,128,128]{2,1,0:T(8,128)S(1)}, f32[2,128,128]{2,1,0:T(8,128)S(1)}, u32[]{:S(2)}, u32[]{:S(2)}) collective-permute-start(f32[2,128,128]{2,1,0:T(8,128)S(1)} %get-tuple-element.58), channel_id=1, source_target_pairs={{0,2},{2,0},{1,3},{3,1},{4,6},{6,4},{5,7},{7,5},{8,10},{10,8},{9,1... | collective-permute-start | bytes 393224 | tf_op jit(solution)/shard_map/ppermute | solution.py:268
  36.1 4.3 %collective-permute-done.9.got = f32[2,128,128]{2,1,0:T(8,128)S(1)} collective-permute-done((f32[2,128,128]{2,1,0:T(8,128)S(1)}, f32[2,128,128]{2,1,0:T(8,128)S(1)}, u32[]{:S(2)}, u32[]{:S(2)}) %collective-permute-start.9) | collective-permute-done | bytes 131104 | tf_op jit(solution)/shard_map/ppermute | solution.py:268
  40.4 1.5 %collective-permute-start.10 = (f32[2,4,128,128]{3,2,1,0:T(8,128)S(1)}, f32[2,4,128,128]{3,2,1,0:T(8,128)S(1)}, u32[]{:S(2)}, u32[]{:S(2)}) collective-permute-start(f32[2,4,128,128]{3,2,1,0:T(8,128)S(1)} %get-tuple-element.62), channel_id=1, source_target_pairs={{0,2},{2,0},{1,3},{3,1},{4,6},{6,4},{5,7},{7,5},{8,10},{10,8},{9,1... | collective-permute-start | bytes 1572872 | tf_op jit(solution)/shard_map/ppermute | solution.py:268
  41.9 6.1 %collective-permute-start.13 = (f32[3,128,128]{2,1,0:T(8,128)S(1)}, f32[3,128,128]{2,1,0:T(8,128)S(1)}, u32[]{:S(2)}, u32[]{:S(2)}) collective-permute-start(f32[3,128,128]{2,1,0:T(8,128)S(1)} %get-tuple-element.66), channel_id=1, source_target_pairs={{0,4},{4,8},{8,12},{12,0},{1,5},{5,9},{9,13},{13,1},{2,6},{6,10},{... | collective-permute-start | bytes 589832 | tf_op jit(solution)/shard_map/ppermute | solution.py:268
  48.0 1.0 %collective-permute-start.14 = (f32[3,128,128]{2,1,0:T(8,128)S(1)}, f32[3,128,128]{2,1,0:T(8,128)S(1)}, u32[]{:S(2)}, u32[]{:S(2)}) collective-permute-start(f32[3,128,128]{2,1,0:T(8,128)S(1)} %get-tuple-element.67), channel_id=1, source_target_pairs={{0,12},{4,0},{8,4},{12,8},{1,13},{5,1},{9,5},{13,9},{2,14},{6,2},{... | collective-permute-start | bytes 589832 | tf_op jit(solution)/shard_map/ppermute | solution.py:268
  49.0 1.2 %shard_map.131 = (f32[2,128,128]{2,1,0:T(8,128)}, f32[128,128]{1,0:T(8,128)S(1)}, f32[128,128]{1,0:T(8,128)S(1)}, f32[4,128,128]{2,1,0:T(8,128)S(1)}, f32[128,128]{1,0:T(8,128)S(1)}) custom-call(s32[123]{0:T(128)S(1)} %concatenate.3.table, f32[2,128,128]{2,1,0:T(8,128)S(1)} %copy-done.4, f32[2,128,128]{2,1,0:T(8,128)S(1)} %get-tuple-element.57.keep, ...), custom_call_target="tpu_custom_call" | custom-call | tf_op jit(solution)/shard_map/pallas_call | solution.py:36
  50.2 2.0 %collective-permute-start.21 = (f32[128,128]{1,0:T(8,128)S(1)}, f32[128,128]{1,0:T(8,128)S(1)}, u32[]{:S(2)}, u32[]{:S(2)}) collective-permute-start(f32[128,128]{1,0:T(8,128)S(1)} %get-tuple-element.80), channel_id=1, source_target_pairs={{0,12},{4,0},{8,4},{12,8},{1,13},{5,1},{9,5},{13,9},{2,14},{6,2},{... | collective-permute-start | bytes 196616 | tf_op jit(solution)/shard_map/ppermute | solution.py:268
  52.2 2.6 %collective-permute-done.13.refs_0_ = f32[3,128,128]{2,1,0:T(8,128)S(1)} collective-permute-done((f32[3,128,128]{2,1,0:T(8,128)S(1)}, f32[3,128,128]{2,1,0:T(8,128)S(1)}, u32[]{:S(2)}, u32[]{:S(2)}) %collective-permute-start.13) | collective-permute-done | bytes 196640 | tf_op jit(solution)/shard_map/ppermute | solution.py:268
  54.8 1.0 %collective-permute-start.18 = (f32[128,128]{1,0:T(8,128)S(1)}, f32[128,128]{1,0:T(8,128)S(1)}, u32[]{:S(2)}, u32[]{:S(2)}) collective-permute-start(f32[128,128]{1,0:T(8,128)S(1)} %get-tuple-element.77), channel_id=1, source_target_pairs={{0,4},{4,8},{8,12},{12,0},{1,5},{5,9},{9,13},{13,1},{2,6},{6,10},{... | collective-permute-start | bytes 196616 | tf_op jit(solution)/shard_map/ppermute | solution.py:268
  55.8 2.1 %collective-permute-done.14.refs_4_ = f32[3,128,128]{2,1,0:T(8,128)S(1)} collective-permute-done((f32[3,128,128]{2,1,0:T(8,128)S(1)}, f32[3,128,128]{2,1,0:T(8,128)S(1)}, u32[]{:S(2)}, u32[]{:S(2)}) %collective-permute-start.14) | collective-permute-done | bytes 196640 | tf_op jit(solution)/shard_map/ppermute | solution.py:268
  57.8 1.7 %collective-permute-start.23 = (f32[4,128,128]{2,1,0:T(8,128)S(1)}, f32[4,128,128]{2,1,0:T(8,128)S(1)}, u32[]{:S(2)}, u32[]{:S(2)}) collective-permute-start(f32[4,128,128]{2,1,0:T(8,128)S(1)} %get-tuple-element.83), channel_id=1, source_target_pairs={{0,8},{4,12},{8,0},{12,4},{1,9},{5,13},{9,1},{13,5},{2,10},{6,14},... | collective-permute-start | bytes 786440 | tf_op jit(solution)/shard_map/ppermute | solution.py:268
  59.6 0.0 collective-permute-done.10.later
  59.6 0.0 collective-permute-start.17
  59.6 0.6 shard_map.132.first_beside
  60.1 0.6 collective-permute-start.20
  60.7 0.0 collective-permute-done.11.across
  60.7 0.1 collective-permute-start.12
  60.8 3.8 %shard_map.133 = (f32[4,3,128,128]{3,2,1,0:T(8,128)S(1)}, f32[4,256,128]{2,1,0:T(8,128)S(1)}) custom-call(s32[123]{0:T(128)S(1)} %concatenate.3.table, f32[128,1024]{1,0:T(8,128)S(1)} %get-tuple-element.64.first, f32[384,1024]{1,0:T(8,128)S(1)} %get-tuple-element.65.rest, f32[4,4,128,128]{3,2,1,0:T(8,128)S(1)} %copy-done, ...), custom_call_target="tpu_custom_call" | custom-call | flops 20000000000 | tf_op jit(solution)/shard_map/pallas_call | solution.py:36
  64.6 0.5 collective-permute-start.22
  65.1 0.0 collective-permute-done.17.refs_1_
  65.1 0.1 collective-permute-start.19
  65.2 0.0 collective-permute-done.20.refs_5_
  65.2 0.0 collective-permute-done.12.corner
  65.2 0.8 collective-permute-done.22.refs_7_
  66.0 0.4 collective-permute-done.19.refs_3_
  66.4 2.9 %shard_map.135 = (f32[2,4,128,128]{3,2,1,0:T(8,128)S(1)}, f32[2,128,128]{2,1,0:T(8,128)S(1)}, f32[2,2,128,128]{3,2,1,0:T(8,128)S(1)}) custom-call(s32[123]{0:T(128)S(1)} %concatenate.3.table, f32[4,4,128,128]{3,2,1,0:T(8,128)S(1)} %copy-done, f32[4,128,128]{2,1,0:T(8,128)S(1)} %shard_map.132.first_beside, ...), custom_call_target="tpu_custom_call" | custom-call | tf_op jit(solution)/shard_map/pallas_call | solution.py:36
  69.3 3.0 %collective-permute-done.23.refs_0_ = f32[4,128,128]{2,1,0:T(8,128)S(1)} collective-permute-done((f32[4,128,128]{2,1,0:T(8,128)S(1)}, f32[4,128,128]{2,1,0:T(8,128)S(1)}, u32[]{:S(2)}, u32[]{:S(2)}) %collective-permute-start.23) | collective-permute-done | bytes 262176 | tf_op jit(solution)/shard_map/ppermute | solution.py:268
  72.3 0.0 collective-permute-start.24
  72.3 0.5 collective-permute-start.15
  72.8 0.5 collective-permute-start.26
  73.3 1.3 %collective-permute-done.16.refs_3_ = f32[128,128]{1,0:T(8,128)S(1)} collective-permute-done((f32[128,128]{1,0:T(8,128)S(1)}, f32[128,128]{1,0:T(8,128)S(1)}, u32[]{:S(2)}, u32[]{:S(2)}) %collective-permute-start.16) | collective-permute-done | bytes 65568 | tf_op jit(solution)/shard_map/ppermute | solution.py:268
  74.6 1.9 %shard_map.134 = (f32[1,4,128,128]{3,2,1,0:T(8,128)S(1)}, f32[1,128,128]{2,1,0:T(8,128)S(1)}, f32[1,2,128,128]{3,2,1,0:T(8,128)S(1)}) custom-call(s32[123]{0:T(128)S(1)} %concatenate.3.table, f32[4,4,128,128]{3,2,1,0:T(8,128)S(1)} %copy-done, f32[4,128,128]{2,1,0:T(8,128)S(1)} %shard_map.132.first_beside, ...), custom_call_target="tpu_custom_call" | custom-call | tf_op jit(solution)/shard_map/pallas_call | solution.py:36
  76.5 1.6 %collective-permute-start.25 = (f32[1,2,128,128]{3,2,1,0:T(8,128)S(1)}, f32[1,2,128,128]{3,2,1,0:T(8,128)S(1)}, u32[]{:S(2)}, u32[]{:S(2)}) collective-permute-start(f32[1,2,128,128]{3,2,1,0:T(8,128)S(1)} %get-tuple-element.90), channel_id=1, source_target_pairs={{0,2},{2,0},{1,3},{3,1},{4,6},{6,4},{5,7},{7,5},{8,10},{10,8},{9,1... | collective-permute-start | bytes 393224 | tf_op jit(solution)/shard_map/ppermute | solution.py:268
  78.1 0.0 collective-permute-done.24.refs_1_
  78.1 1.9 %shard_map.136 = (f32[1,4,128,128]{3,2,1,0:T(8,128)S(1)}, f32[1,128,128]{2,1,0:T(8,128)S(1)}, f32[1,2,128,128]{3,2,1,0:T(8,128)S(1)}) custom-call(s32[123]{0:T(128)S(1)} %concatenate.3.table, f32[4,4,128,128]{3,2,1,0:T(8,128)S(1)} %copy-done, f32[4,128,128]{2,1,0:T(8,128)S(1)} %shard_map.132.first_beside, ...), custom_call_target="tpu_custom_call" | custom-call | tf_op jit(solution)/shard_map/pallas_call | solution.py:36
  80.0 0.6 collective-permute-start.27
  80.6 4.2 %collective-permute-done.25.refs_6_ = f32[1,2,128,128]{3,2,1,0:T(8,128)S(1)} collective-permute-done((f32[1,2,128,128]{3,2,1,0:T(8,128)S(1)}, f32[1,2,128,128]{3,2,1,0:T(8,128)S(1)}, u32[]{:S(2)}, u32[]{:S(2)}) %collective-permute-start.25) | collective-permute-done | bytes 131104 | tf_op jit(solution)/shard_map/ppermute | solution.py:268
  84.7 0.0 collective-permute-done.26.refs_7_
  84.8 1.8 %collective-permute-done.27.refs_8_ = f32[1,2,128,128]{3,2,1,0:T(8,128)S(1)} collective-permute-done((f32[1,2,128,128]{3,2,1,0:T(8,128)S(1)}, f32[1,2,128,128]{3,2,1,0:T(8,128)S(1)}, u32[]{:S(2)}, u32[]{:S(2)}) %collective-permute-start.27) | collective-permute-done | bytes 131104 | tf_op jit(solution)/shard_map/ppermute | solution.py:268
  86.6 1.7 %shard_map.137 = (f32[4,4,128,128]{3,2,1,0:T(8,128)}, f32[4,128,128]{2,1,0:T(8,128)}) custom-call(s32[123]{0:T(128)S(1)} %concatenate.3.table, f32[1,4,128,128]{3,2,1,0:T(8,128)S(1)} %get-tuple-element.75.refs_0_, f32[2,4,128,128]{3,2,1,0:T(8,128)S(1)} %get-tuple-element.82.refs_1_, f32[1,4,128,128]{3,2,1,0:T(8,128)S(1)} %get-tuple-element.86.refs_2_, ...), custom_call_target="tpu_custom_call" | custom-call | tf_op jit(solution)/shard_map/pallas_call | solution.py:36
  (26 shorter events, 0.1 us)
Async XLA Ops:
  0.6 16.0 %copy-start.2 = (f32[2,4,128,128]{3,2,1,0:T(8,128)S(1)}, f32[2,4,128,128]{3,2,1,0:T(8,128)}, u32[]{:S(2)}) copy-start(f32[2,4,128,128]{3,2,1,0:T(8,128)} %own.6) | copy-start | bytes 1572868
  0.6 5.3 %copy-start.3 = (f32[1,128,4,256]{3,2,1,0:T(4,128)S(1)}, f32[1,128,4,256]{3,2,1,0:T(4,128)}, u32[]{:S(2)}) copy-start(f32[1,128,4,256]{3,2,1,0:T(4,128)} %param.10) | copy-start | bytes 1572868
  0.7 11.9 %copy-start.5 = (s32[8,4]{0,1:T(4,128)S(1)}, s32[8,4]{0,1:T(4,128)}, u32[]{:S(2)}) copy-start(s32[8,4]{0,1:T(4,128)} %param.15) | copy-start | bytes 388
  0.7 12.0 %copy-start.6 = (s32[16,3]{0,1:T(4,128)S(1)}, s32[16,3]{0,1:T(4,128)}, u32[]{:S(2)}) copy-start(s32[16,3]{0,1:T(4,128)} %param.19) | copy-start | bytes 580
  0.7 12.0 %copy-start.7 = (s32[8]{0:T(128)S(1)}, s32[8]{0:T(128)}, u32[]{:S(2)}) copy-start(s32[8]{0:T(128)} %param.16) | copy-start | bytes 100
  0.7 12.0 %copy-start.8 = (s32[16]{0:T(128)S(1)}, s32[16]{0:T(128)}, u32[]{:S(2)}) copy-start(s32[16]{0:T(128)} %param.17) | copy-start | bytes 196
  0.7 12.0 %copy-start.9 = (s32[16]{0:T(128)S(1)}, s32[16]{0:T(128)}, u32[]{:S(2)}) copy-start(s32[16]{0:T(128)} %param.18) | copy-start | bytes 196
  0.7 16.0 %collective-permute-start = (f32[2,4,128,128]{3,2,1,0:T(8,128)}, f32[2,4,128,128]{3,2,1,0:T(8,128)S(1)}, u32[]{:S(2)}, u32[]{:S(2)}) collective-permute-start(f32[2,4,128,128]{3,2,1,0:T(8,128)} %own.6), channel_id=1, source_target_pairs={{0,2},{2,0},{1,3},{3,1},{4,6},{6,4},{5,7},{7,5},{8,10},{10,8},{9,1... | collective-permute-start | bytes 1572872 | tf_op jit(solution)/shard_map/ppermute | solution.py:268
  5.8 22.2 %collective-permute-start.4 = (f32[2,4,128,128]{3,2,1,0:T(8,128)}, f32[2,4,128,128]{3,2,1,0:T(8,128)S(1)}, u32[]{:S(2)}, u32[]{:S(2)}) collective-permute-start(f32[2,4,128,128]{3,2,1,0:T(8,128)} %get-tuple-element.95), channel_id=1, source_target_pairs={{0,2},{2,0},{1,3},{3,1},{4,6},{6,4},{5,7},{7,5},{8,10},{10,8},{9,1... | collective-permute-start | bytes 1572872 | tf_op jit(solution)/shard_map/ppermute | solution.py:268
  6.7 11.5 %collective-permute-start.1 = (f32[64,4,256]{2,1,0:T(4,128)}, f32[64,4,256]{2,1,0:T(4,128)S(1)}, u32[]{:S(2)}, u32[]{:S(2)}) collective-permute-start(f32[64,4,256]{2,1,0:T(4,128)} %dynamic-slice_bitcast_fusion), channel_id=1, source_target_pairs={{0,4},{4,8},{8,12},{12,0},{1,5},{5,9},{9,13},{13,1},{2,6},{6,10},{... | collective-permute-start | bytes 786440 | tf_op jit(solution)/shard_map/ppermute | solution.py:268
  8.6 19.3 %collective-permute-start.2 = (f32[64,4,256]{2,1,0:T(4,128)}, f32[64,4,256]{2,1,0:T(4,128)S(1)}, u32[]{:S(2)}, u32[]{:S(2)}) collective-permute-start(f32[64,4,256]{2,1,0:T(4,128)} %dynamic-slice_bitcast_fusion), channel_id=1, source_target_pairs={{0,8},{4,12},{8,0},{12,4},{1,9},{5,13},{9,1},{13,5},{2,10},{6,14},... | collective-permute-start | bytes 786440 | tf_op jit(solution)/shard_map/ppermute | solution.py:268
  11.2 16.8 %collective-permute-start.3 = (f32[64,4,256]{2,1,0:T(4,128)}, f32[64,4,256]{2,1,0:T(4,128)S(1)}, u32[]{:S(2)}, u32[]{:S(2)}) collective-permute-start(f32[64,4,256]{2,1,0:T(4,128)} %dynamic-slice_bitcast_fusion), channel_id=1, source_target_pairs={{0,12},{4,0},{8,4},{12,8},{1,13},{5,1},{9,5},{13,9},{2,14},{6,2},{... | collective-permute-start | bytes 786440 | tf_op jit(solution)/shard_map/ppermute | solution.py:268
  28.0 3.0 %collective-permute-start.5 = (f32[2,4,128,128]{3,2,1,0:T(8,128)S(1)}, f32[2,4,128,128]{3,2,1,0:T(8,128)S(1)}, u32[]{:S(2)}, u32[]{:S(2)}) collective-permute-start(f32[2,4,128,128]{3,2,1,0:T(8,128)S(1)} %copy-done.2), channel_id=1, source_target_pairs={{0,1},{1,0},{2,3},{3,2},{4,5},{5,4},{6,7},{7,6},{8,9},{9,8},{10,11... | collective-permute-start | bytes 1572872 | tf_op jit(solution)/shard_map/ppermute | solution.py:268
  28.0 2.3 %collective-permute-start.6 = (f32[64,4,256]{2,1,0:T(4,128)S(1)}, f32[64,4,256]{2,1,0:T(4,128)S(1)}, u32[]{:S(2)}, u32[]{:S(2)}) collective-permute-start(f32[64,4,256]{2,1,0:T(4,128)S(1)} %collective-permute-done.1.refs_0_), channel_id=1, source_target_pairs={{0,1},{1,0},{2,3},{3,2},{4,5},{5,4},{6,7},{7,6},{8,9},{9,8},{10,11... | collective-permute-start | bytes 786440 | tf_op jit(solution)/shard_map/ppermute | solution.py:268
  28.5 2.1 %collective-permute-start.7 = (f32[64,4,256]{2,1,0:T(4,128)S(1)}, f32[64,4,256]{2,1,0:T(4,128)S(1)}, u32[]{:S(2)}, u32[]{:S(2)}) collective-permute-start(f32[64,4,256]{2,1,0:T(4,128)S(1)} %collective-permute-done.2.refs_1_), channel_id=1, source_target_pairs={{0,1},{1,0},{2,3},{3,2},{4,5},{5,4},{6,7},{7,6},{8,9},{9,8},{10,11... | collective-permute-start | bytes 786440 | tf_op jit(solution)/shard_map/ppermute | solution.py:268
  28.5 2.5 %collective-permute-start.8 = (f32[64,4,256]{2,1,0:T(4,128)S(1)}, f32[64,4,256]{2,1,0:T(4,128)S(1)}, u32[]{:S(2)}, u32[]{:S(2)}) collective-permute-start(f32[64,4,256]{2,1,0:T(4,128)S(1)} %collective-permute-done.3.refs_2_), channel_id=1, source_target_pairs={{0,1},{1,0},{2,3},{3,2},{4,5},{5,4},{6,7},{7,6},{8,9},{9,8},{10,11... | collective-permute-start | bytes 786440 | tf_op jit(solution)/shard_map/ppermute | solution.py:268
  31.0 3.4 %copy-start = (f32[4,4,128,128]{3,2,1,0:T(8,128)S(1)}, f32[4,4,128,128]{3,2,1,0:T(8,128)}, u32[]{:S(2)}) copy-start(f32[4,4,128,128]{3,2,1,0:T(8,128)} %own.10) | copy-start | bytes 3145732
  31.0 18.0 %copy-start.4 = (f32[2,128,128]{2,1,0:T(8,128)S(1)}, f32[2,128,128]{2,1,0:T(8,128)}, u32[]{:S(2)}) copy-start(f32[2,128,128]{2,1,0:T(8,128)} %diagonal.4) | copy-start | bytes 393220
  34.4 26.3 %collective-permute-start.11 = (f32[4,4,128,128]{3,2,1,0:T(8,128)S(1)}, f32[4,4,128,128]{3,2,1,0:T(8,128)S(1)}, u32[]{:S(2)}, u32[]{:S(2)}) collective-permute-start(f32[4,4,128,128]{3,2,1,0:T(8,128)S(1)} %copy-done), channel_id=1, source_target_pairs={{0,1},{1,0},{2,3},{3,2},{4,5},{5,4},{6,7},{7,6},{8,9},{9,8},{10,11... | collective-permute-start | bytes 3145736 | tf_op jit(solution)/shard_map/ppermute | solution.py:268
  34.6 5.8 %collective-permute-start.9 = (f32[2,128,128]{2,1,0:T(8,128)S(1)}, f32[2,128,128]{2,1,0:T(8,128)S(1)}, u32[]{:S(2)}, u32[]{:S(2)}) collective-permute-start(f32[2,128,128]{2,1,0:T(8,128)S(1)} %get-tuple-element.58), channel_id=1, source_target_pairs={{0,2},{2,0},{1,3},{3,1},{4,6},{6,4},{5,7},{7,5},{8,10},{10,8},{9,1... | collective-permute-start | bytes 393224 | tf_op jit(solution)/shard_map/ppermute | solution.py:268
  40.4 19.2 %collective-permute-start.10 = (f32[2,4,128,128]{3,2,1,0:T(8,128)S(1)}, f32[2,4,128,128]{3,2,1,0:T(8,128)S(1)}, u32[]{:S(2)}, u32[]{:S(2)}) collective-permute-start(f32[2,4,128,128]{3,2,1,0:T(8,128)S(1)} %get-tuple-element.62), channel_id=1, source_target_pairs={{0,2},{2,0},{1,3},{3,1},{4,6},{6,4},{5,7},{7,5},{8,10},{10,8},{9,1... | collective-permute-start | bytes 1572872 | tf_op jit(solution)/shard_map/ppermute | solution.py:268
  41.9 13.0 %collective-permute-start.13 = (f32[3,128,128]{2,1,0:T(8,128)S(1)}, f32[3,128,128]{2,1,0:T(8,128)S(1)}, u32[]{:S(2)}, u32[]{:S(2)}) collective-permute-start(f32[3,128,128]{2,1,0:T(8,128)S(1)} %get-tuple-element.66), channel_id=1, source_target_pairs={{0,4},{4,8},{8,12},{12,0},{1,5},{5,9},{9,13},{13,1},{2,6},{6,10},{... | collective-permute-start | bytes 589832 | tf_op jit(solution)/shard_map/ppermute | solution.py:268
  48.0 9.9 %collective-permute-start.14 = (f32[3,128,128]{2,1,0:T(8,128)S(1)}, f32[3,128,128]{2,1,0:T(8,128)S(1)}, u32[]{:S(2)}, u32[]{:S(2)}) collective-permute-start(f32[3,128,128]{2,1,0:T(8,128)S(1)} %get-tuple-element.67), channel_id=1, source_target_pairs={{0,12},{4,0},{8,4},{12,8},{1,13},{5,1},{9,5},{13,9},{2,14},{6,2},{... | collective-permute-start | bytes 589832 | tf_op jit(solution)/shard_map/ppermute | solution.py:268
  50.2 9.9 %collective-permute-start.21 = (f32[128,128]{1,0:T(8,128)S(1)}, f32[128,128]{1,0:T(8,128)S(1)}, u32[]{:S(2)}, u32[]{:S(2)}) collective-permute-start(f32[128,128]{1,0:T(8,128)S(1)} %get-tuple-element.80), channel_id=1, source_target_pairs={{0,12},{4,0},{8,4},{12,8},{1,13},{5,1},{9,5},{13,9},{2,14},{6,2},{... | collective-permute-start | bytes 196616 | tf_op jit(solution)/shard_map/ppermute | solution.py:268
  54.8 9.8 %collective-permute-start.18 = (f32[128,128]{1,0:T(8,128)S(1)}, f32[128,128]{1,0:T(8,128)S(1)}, u32[]{:S(2)}, u32[]{:S(2)}) collective-permute-start(f32[128,128]{1,0:T(8,128)S(1)} %get-tuple-element.77), channel_id=1, source_target_pairs={{0,4},{4,8},{8,12},{12,0},{1,5},{5,9},{9,13},{13,1},{2,6},{6,10},{... | collective-permute-start | bytes 196616 | tf_op jit(solution)/shard_map/ppermute | solution.py:268
  57.8 14.4 %collective-permute-start.23 = (f32[4,128,128]{2,1,0:T(8,128)S(1)}, f32[4,128,128]{2,1,0:T(8,128)S(1)}, u32[]{:S(2)}, u32[]{:S(2)}) collective-permute-start(f32[4,128,128]{2,1,0:T(8,128)S(1)} %get-tuple-element.83), channel_id=1, source_target_pairs={{0,8},{4,12},{8,0},{12,4},{1,9},{5,13},{9,1},{13,5},{2,10},{6,14},... | collective-permute-start | bytes 786440 | tf_op jit(solution)/shard_map/ppermute | solution.py:268
  59.6 5.6 %collective-permute-start.17 = (f32[3,128,128]{2,1,0:T(8,128)S(1)}, f32[3,128,128]{2,1,0:T(8,128)S(1)}, u32[]{:S(2)}, u32[]{:S(2)}) collective-permute-start(f32[3,128,128]{2,1,0:T(8,128)S(1)} %collective-permute-done.13.refs_0_), channel_id=1, source_target_pairs={{0,1},{1,0},{2,3},{3,2},{4,5},{5,4},{6,7},{7,6},{8,9},{9,8},{10,11... | collective-permute-start | bytes 589832 | tf_op jit(solution)/shard_map/ppermute | solution.py:268
  60.1 5.1 %collective-permute-start.20 = (f32[3,128,128]{2,1,0:T(8,128)S(1)}, f32[3,128,128]{2,1,0:T(8,128)S(1)}, u32[]{:S(2)}, u32[]{:S(2)}) collective-permute-start(f32[3,128,128]{2,1,0:T(8,128)S(1)} %collective-permute-done.14.refs_4_), channel_id=1, source_target_pairs={{0,1},{1,0},{2,3},{3,2},{4,5},{5,4},{6,7},{7,6},{8,9},{9,8},{10,11... | collective-permute-start | bytes 589832 | tf_op jit(solution)/shard_map/ppermute | solution.py:268
  60.7 4.5 %collective-permute-start.12 = (f32[4,128,128]{2,1,0:T(8,128)S(1)}, f32[4,128,128]{2,1,0:T(8,128)S(1)}, u32[]{:S(2)}, u32[]{:S(2)}) collective-permute-start(f32[4,128,128]{2,1,0:T(8,128)S(1)} %shard_map.132.first_beside), channel_id=1, source_target_pairs={{0,1},{1,0},{2,3},{3,2},{4,5},{5,4},{6,7},{7,6},{8,9},{9,8},{10,11... | collective-permute-start | bytes 786440 | tf_op jit(solution)/shard_map/ppermute | solution.py:268
  60.8 5.6 %copy-start.1 = (f32[4,128,128]{2,1,0:T(8,128)S(1)}, f32[4,128,128]{2,1,0:T(8,128)}, u32[]{:S(2)}) copy-start(f32[4,128,128]{2,1,0:T(8,128)} %diagonal.7) | copy-start | bytes 786436
  64.6 1.4 %collective-permute-start.22 = (f32[128,128]{1,0:T(8,128)S(1)}, f32[128,128]{1,0:T(8,128)S(1)}, u32[]{:S(2)}, u32[]{:S(2)}) collective-permute-start(f32[128,128]{1,0:T(8,128)S(1)} %collective-permute-done.21.refs_6_), channel_id=1, source_target_pairs={{0,1},{1,0},{2,3},{3,2},{4,5},{5,4},{6,7},{7,6},{8,9},{9,8},{10,11... | collective-permute-start | bytes 196616 | tf_op jit(solution)/shard_map/ppermute | solution.py:268
  65.1 1.3 %collective-permute-start.19 = (f32[128,128]{1,0:T(8,128)S(1)}, f32[128,128]{1,0:T(8,128)S(1)}, u32[]{:S(2)}, u32[]{:S(2)}) collective-permute-start(f32[128,128]{1,0:T(8,128)S(1)} %collective-permute-done.18.refs_2_), channel_id=1, source_target_pairs={{0,1},{1,0},{2,3},{3,2},{4,5},{5,4},{6,7},{7,6},{8,9},{9,8},{10,11... | collective-permute-start | bytes 196616 | tf_op jit(solution)/shard_map/ppermute | solution.py:268
  72.3 5.8 %collective-permute-start.24 = (f32[4,128,128]{2,1,0:T(8,128)S(1)}, f32[4,128,128]{2,1,0:T(8,128)S(1)}, u32[]{:S(2)}, u32[]{:S(2)}) collective-permute-start(f32[4,128,128]{2,1,0:T(8,128)S(1)} %collective-permute-done.23.refs_0_), channel_id=1, source_target_pairs={{0,1},{1,0},{2,3},{3,2},{4,5},{5,4},{6,7},{7,6},{8,9},{9,8},{10,11... | collective-permute-start | bytes 786440 | tf_op jit(solution)/shard_map/ppermute | solution.py:268
  72.3 2.3 %collective-permute-start.15 = (f32[3,128,128]{2,1,0:T(8,128)S(1)}, f32[3,128,128]{2,1,0:T(8,128)S(1)}, u32[]{:S(2)}, u32[]{:S(2)}) collective-permute-start(f32[3,128,128]{2,1,0:T(8,128)S(1)} %get-tuple-element.73.refs_0_), channel_id=1, source_target_pairs={{0,1},{1,0},{2,3},{3,2},{4,5},{5,4},{6,7},{7,6},{8,9},{9,8},{10,11... | collective-permute-start | bytes 589832 | tf_op jit(solution)/shard_map/ppermute | solution.py:268
  72.8 12.0 %collective-permute-start.26 = (f32[2,2,128,128]{3,2,1,0:T(8,128)S(1)}, f32[2,2,128,128]{3,2,1,0:T(8,128)S(1)}, u32[]{:S(2)}, u32[]{:S(2)}) collective-permute-start(f32[2,2,128,128]{3,2,1,0:T(8,128)S(1)} %get-tuple-element.84), channel_id=1, source_target_pairs={{0,2},{2,0},{1,3},{3,1},{4,6},{6,4},{5,7},{7,5},{8,10},{10,8},{9,1... | collective-permute-start | bytes 786440 | tf_op jit(solution)/shard_map/ppermute | solution.py:268
  73.3 1.3 %collective-permute-start.16 = (f32[128,128]{1,0:T(8,128)S(1)}, f32[128,128]{1,0:T(8,128)S(1)}, u32[]{:S(2)}, u32[]{:S(2)}) collective-permute-start(f32[128,128]{1,0:T(8,128)S(1)} %get-tuple-element.74.refs_2_), channel_id=1, source_target_pairs={{0,1},{1,0},{2,3},{3,2},{4,5},{5,4},{6,7},{7,6},{8,9},{9,8},{10,11... | collective-permute-start | bytes 196616 | tf_op jit(solution)/shard_map/ppermute | solution.py:268
  76.5 8.3 %collective-permute-start.25 = (f32[1,2,128,128]{3,2,1,0:T(8,128)S(1)}, f32[1,2,128,128]{3,2,1,0:T(8,128)S(1)}, u32[]{:S(2)}, u32[]{:S(2)}) collective-permute-start(f32[1,2,128,128]{3,2,1,0:T(8,128)S(1)} %get-tuple-element.90), channel_id=1, source_target_pairs={{0,2},{2,0},{1,3},{3,1},{4,6},{6,4},{5,7},{7,5},{8,10},{10,8},{9,1... | collective-permute-start | bytes 393224 | tf_op jit(solution)/shard_map/ppermute | solution.py:268
  80.0 6.6 %collective-permute-start.27 = (f32[1,2,128,128]{3,2,1,0:T(8,128)S(1)}, f32[1,2,128,128]{3,2,1,0:T(8,128)S(1)}, u32[]{:S(2)}, u32[]{:S(2)}) collective-permute-start(f32[1,2,128,128]{3,2,1,0:T(8,128)S(1)} %get-tuple-element.91), channel_id=1, source_target_pairs={{0,2},{2,0},{1,3},{3,1},{4,6},{6,4},{5,7},{7,5},{8,10},{10,8},{9,1... | collective-permute-start | bytes 393224 | tf_op jit(solution)/shard_map/ppermute | solution.py:268

commit v4 on v3

--- a/solution.py
+++ b/solution.py
@@ -13,6 +13,7 @@
 PRECISE = lax.Precision.HIGHEST
 THREE_PASS = lax.Precision.HIGH
 F32 = jnp.float32
+LIMIT = 24 * 1024 * 1024
 SMEM = pl.BlockSpec(memory_space=pltpu.SMEM)
 VMEM = pl.BlockSpec(memory_space=pltpu.VMEM)
 
@@ -39,7 +40,7 @@
         in_specs=[SMEM] + [VMEM] * len(operands),
         out_specs=tuple([VMEM] * len(out_shapes)),
         scratch_shapes=[pltpu.VMEM(s, F32) for s in scratch],
-        compiler_params=pltpu.CompilerParams(vmem_limit_bytes=40 * 1024 * 1024),
+        compiler_params=pltpu.CompilerParams(vmem_limit_bytes=LIMIT),
         cost_estimate=pl.CostEstimate(flops=flops, bytes_accessed=0, transcendentals=0),
     )(table, *operands)
 
@@ -98,12 +99,22 @@
             out[pl.ds(pl.multiple_of(at + first, rows // 2), part.shape[0]), b * width : (b + 1) * width] = part[:, b, :]
 
 
-SINGLE, LATE = (1, 3), 2
-GROUPS = ((0,), SINGLE, (LATE,))
-LONG = 20_000_000_000
-
-
-def early_kernel(sizes, table, root, own, beside, first, spread, total):
+def plain(body, out_shapes, *operands):
+    return pl.pallas_call(
+        body,
+        out_shape=tuple(array(*o.shape) for o in out_shapes),
+        in_specs=[VMEM] * len(operands),
+        out_specs=tuple([VMEM] * len(out_shapes)),
+        compiler_params=pltpu.CompilerParams(vmem_limit_bytes=8 * 1024 * 1024),
+    )(*operands)
+
+
+ORDER = (0, 2, 1, 3)
+SPARE = {1: 8, 3: 8}
+
+
+def early_kernel(sizes, table, root, own, *refs):
+    *beside, first, spread, total = refs
     tree = Tree(table, *sizes)
     per_one, blocks, rows, cols = own.shape
     fill_rows(first, 0, rows, [(0, root)])
@@ -113,20 +124,20 @@
             at, valid = tree.ancestor(one, a), tree.live(one, a)
             lanes = slice(g * cols, (g + 1) * cols)
             spread[spot(at * 2 + tree.row, rows), lanes] = own[g, a] * valid
-            spread[spot(at * 2 + 1 - tree.row, rows), lanes] = beside[g, a] * valid
+            spread[spot(at * 2 + 1 - tree.row, rows), lanes] = beside[g][0, a] * valid
     total[...] = mm(first[...], spread[...])
 
 
-def late_kernel(sizes, table, spread, total, own, across, *refs):
+def level_one_kernel(sizes, table, spread, total, own, across, diagonal, *refs):
     tree = Tree(table, *sizes)
     shifts = tree.nodes - 1
     far, near = refs[:shifts], refs[shifts : 2 * shifts]
-    rest, cov, keep, send, *picks = refs[2 * shifts : 2 * shifts + 4 + tree.nodes]
+    rest, cov, keep, send, *parents = refs[2 * shifts : 2 * shifts + 4 + tree.nodes]
     wide, tall, part = refs[2 * shifts + 4 + tree.nodes :]
     per_one, blocks, rows, cols = own.shape
     half = rows // 2
     for i in range(shifts):
-        fill_rows(rest, i * rows, rows, [(tree.sub * half, far[i]), ((1 - tree.sub) * half, near[i])])
+        fill_rows(rest, i * rows, rows, [(tree.sub * half, far[i].at[:half]), ((1 - tree.sub) * half, near[i].at[:half])])
     others = mm(rest[...], spread[...])
     for g in range(per_one):
         lanes = slice(g * cols, (g + 1) * cols)
@@ -136,53 +147,42 @@
     for g in range(per_one):
         one = tree.me * per_one + g
         for a in range(blocks):
-            cov[g, a] = tall[g, tree.back(tree.ancestor(one, a))] * (-tree.live(one, a))
+            valid = tree.live(one, a)
+            cov[g, a] = tall[g, tree.back(tree.ancestor(one, a))] * -valid
+            wide[a * rows : (a + 1) * rows, spot(tree.sub, cols)] = own[g, a] * valid
+            wide[a * rows : (a + 1) * rows, spot(1 - tree.sub, cols)] = across[g, a] * valid
+        part[...] = -mm_t(wide[...], cov[g].reshape(blocks * rows, cols))
+        keep[g] = diagonal[g] + part[spot(tree.row, rows), :]
+        send[g] = part[spot(1 - tree.row, rows), :]
     for k in range(tree.nodes):
         target = tree.node(k)
         h = target * tree.per_two + tree.child(target, tree.me)
         for t in range(blocks - 1):
-            picks[k][t] = cov[tree.slot(h), tree.offset(h, t)]
-    for g in range(per_one):
-        one = tree.me * per_one + g
-        for a in range(blocks):
-            valid = tree.live(one, a)
-            wide[a * rows : (a + 1) * rows, spot(tree.sub, cols)] = own[g, a] * valid
-            wide[a * rows : (a + 1) * rows, spot(1 - tree.sub, cols)] = across[g, a] * valid
-        part[...] = -mm_t(wide[...], cov[g].reshape(blocks * rows, cols))
-        keep[g] = part[spot(tree.row, rows), :]
-        send[g] = part[spot(1 - tree.row, rows), :]
-
-
-def diag_one_kernel(sizes, table, diagonal, keep, got, pick, out, *tops):
-    tree = Tree(table, *sizes)
-    out[...] = diagonal[...] + (keep[...] + got[...])
-    for k in range(tree.nodes):
-        target = tree.node(k)
-        slot = tree.slot(target * tree.per_two + tree.child(target, tree.me))
-        if k == LATE:
-            tops[k][: A - 1] = pick[...]
-            tops[k][A - 1] = out[slot]
-        else:
-            tops[k][...] = out[slot]
-
-
-def first_blocks_kernel(sizes, table, panel, later, out):
-    soon = panel.shape[0]
-    out[:soon] = panel[:, 0]
-    out[soon:] = later[:, 0]
-
-
-def root_two_kernel(sizes, table, first, rest, own, beside, later, across, lower, inner, spread, wide, tall):
+            parents[k][t * rows : (t + 1) * rows] = cov[tree.slot(h), tree.offset(h, t)]
+        parents[k][(blocks - 1) * rows : blocks * rows] = keep[tree.slot(h)]
+        parents[k][blocks * rows : (blocks + 1) * rows] = send[tree.slot(h)]
+        if parents[k].shape[0] > (blocks + 1) * rows:
+            parents[k][(blocks + 1) * rows :] = jnp.zeros_like(parents[k][(blocks + 1) * rows :])
+
+
+def add_kernel(keep, got, out):
+    out[...] = keep[...] + got[...]
+
+
+def first_blocks_kernel(panel, out):
+    out[...] = panel[:, 0]
+
+
+def root_two_kernel(sizes, table, first, rest, own, beside, across, lower, inner, spread, wide, tall):
     tree = Tree(table, *sizes)
     per_two, blocks, rows, cols = own.shape
-    soon = beside.shape[0]
     spread[...] = jnp.zeros_like(spread)
     for h in range(per_two):
         valid, at = tree.level_two(h)
         lanes = slice(h * cols, (h + 1) * cols)
         for t in range(1, blocks):
             spread[spot(at[t - 1] * 2 + tree.row, rows), lanes] = own[h, t] * valid[t]
-            spread[spot(at[t - 1] * 2 + 1 - tree.row, rows), lanes] = (beside[h, t] if h < soon else later[h - soon, t]) * valid[t]
+            spread[spot(at[t - 1] * 2 + 1 - tree.row, rows), lanes] = beside[h, t] * valid[t]
     mine = mm(first[...], spread[...])
     others = mm(rest[...], spread[...])
     for h in range(per_two):
@@ -199,50 +199,39 @@
         inner[h] = mm_t(wide[...], lower[h].reshape((blocks - 1) * rows, cols))
 
 
-def parent_two_kernel(sizes, shifts, table, own, first_beside, across, corner, lower, inner, diagonal, *refs):
+def parent_two_kernel(sizes, shifts, table, own, beside, across, corner, lower, inner, diagonal, *refs):
     tree = Tree(table, *sizes)
     row, sub = tree.row, tree.sub
     blocks, rows, cols = own.shape[1:]
-    refs = list(refs)
-    ins = []
-    for k in shifts:
-        if k == LATE:
-            mine, side = refs[:2]
-            del refs[:2]
-            ins.append((mine, side, mine.at[A - 1], side.at[A - 1]))
-        else:
-            ins.append(refs[:4])
-            del refs[:4]
-    panel, diag, sends, cross, top, first, local, wide, part, more = refs
+    n = len(shifts)
+    panel, diag, sends, cross, top, first, local, wide, part, more = refs[2 * n :]
     low = (blocks - 1) * rows
     for i, k in enumerate(shifts):
-        cross_own, cross_side, top_own, top_side = ins[i]
         h = tree.child(tree.me, tree.node(-k))
         valid, _ = tree.level_two(h)
+        for got, lanes in (refs[2 * i], spot(sub, cols)), (refs[2 * i + 1], spot(1 - sub, cols)):
+            cross[:, lanes] = got[:low]
+            top[spot(row, rows), lanes] = got[low : low + rows]
+            top[spot(1 - row, rows), lanes] = got[low + rows : low + 2 * rows]
         for t in range(1, blocks):
             span = slice((t - 1) * rows, t * rows)
-            cross[span, spot(sub, cols)] = cross_own[t - 1]
-            cross[span, spot(1 - sub, cols)] = cross_side[t - 1]
             local[span, :] = own[h, t] * valid[t]
-            wide[span, spot(sub, cols)] = own[h, t] * valid[t]
+            wide[span, spot(sub, cols)] = local[span, :]
             wide[span, spot(1 - sub, cols)] = across[h, t] * valid[t]
-        top[:, spot(sub, cols)] = top_own[...]
-        top[:, spot(1 - sub, cols)] = top_side[...]
         first[spot(row, rows), :] = own[h, 0]
-        first[spot(1 - row, rows), :] = first_beside[h]
+        first[spot(1 - row, rows), :] = beside[h]
         mine = spot(blocks - 1 + row, rows)
         other = spot(blocks - row, rows)
         wide[mine, spot(sub, cols)] = own[h, 0]
         wide[mine, spot(1 - sub, cols)] = across[h, 0]
-        wide[other, spot(sub, cols)] = first_beside[h]
+        wide[other, spot(sub, cols)] = beside[h]
         wide[other, spot(1 - sub, cols)] = corner[h]
         below = mm(cross[...], first[...])
         for t in range(1, blocks):
             span = slice((t - 1) * rows, t * rows)
             part[span, :] = below[span, :] * valid[t]
             panel[i, t] = -(lower[h, t - 1] + part[span, :])
-        part[low:, :] = mm_t(cross[...], local[...])
-        part[mine, :] += mm(top[...], first[...])
+        part[low:, :] = mm_t(cross[...], local[...]) + mm(top[...], first[...])
         more[...] = inner[h] + mm_t(wide[...], part[...])
         panel[i, 0] = -part[mine, :]
         sends[i, 0] = part[other, :]
@@ -284,75 +273,60 @@
         [jnp.stack([me, row, sub]).astype(jnp.int32), counts, owners, slots, ancestors.T.reshape(-1), offsets.T.reshape(-1)]
     )
     bind = lambda kernel, *more: functools.partial(kernel, sizes, *more)
-
-    root = root_inverse[0]
-    half = lax.dynamic_slice_in_dim(root, sub * (rows // 2), rows // 2, 0)
+    together = lax.optimization_barrier
+
+    half = lax.dynamic_slice_in_dim(root_inverse[0], sub * (rows // 2), rows // 2, 0)
+    half = jnp.pad(half, ((0, 2), (0, 0), (0, 0)))
     far = [shift(half, "node", k) for k in range(1, nodes)]
-    beside_one = shift(panel_one, "row", 1)
-    soon = per_two // 2
-    beside_soon = shift(panel_two[:soon], "row", 1)
+    source = after(panel_one, table)
+    beside_one = [shift(source[g : g + 1], "row", 1) for g in range(per_one)]
     first, spread, total = call(
         bind(early_kernel),
         [array(rows, full), array(full, per_one * cols), array(rows, per_one * cols)],
         table,
-        [root, panel_one, beside_one],
-    )
-    *far, beside_soon, total = lax.optimization_barrier((*far, beside_soon, total))
+        [root_inverse[0], panel_one, *beside_one],
+    )
+    *far, total = together((*far, total))
     near = [shift(x, "sub", 1) for x in far]
-    across_one = shift(after(panel_one, total), "sub", 1)
-    out = call(
-        bind(late_kernel),
+    across_one = shift(after(panel_one, far[0]), "sub", 1)
+    beside_two = shift(after(panel_two, far[0]), "row", 1)
+
+    rest, cov_panel_one, keep, send, *parents = call(
+        bind(level_one_kernel),
         [array((nodes - 1) * rows, full), array(*panel_one.shape), array(per_one, rows, cols), array(per_one, rows, cols)]
-        + [array(blocks - 1, rows, cols)] * nodes,
+        + [array((blocks + 1) * rows + SPARE.get(k, 0), cols) for k in range(nodes)],
         table,
-        [spread, total, panel_one, across_one] + far + near,
+        [spread, total, panel_one, across_one, diag_one] + far + near,
         [(blocks * rows, 2 * cols), (per_one, nodes, rows, cols), (2 * rows, cols)],
     )
-    rest, cov_panel_one, keep, send = out[:4]
-    picks = out[4:]
-    got = shift(send, "row", 1)
-    beside_later = shift(after(panel_two[soon:], got), "row", 1)
-    cross = {k: shift(picks[k], "node", k) for k in SINGLE}
+    parents = [x if k == 0 else shift(x, "node", k) for k, x in enumerate(parents)]
     across_two = shift(after(panel_two, send), "sub", 1)
-    out = call(
-        bind(diag_one_kernel),
-        [array(*diag_one.shape)] + [array(blocks, rows, cols) if k == LATE else array(rows, cols) for k in range(nodes)],
-        table,
-        [diag_one, keep, got, picks[LATE]],
-    )
-    cov_diag_one = out[0]
-    tops = {k: out[1 + k] if k == 0 else shift(out[1 + k], "node", k) for k in range(nodes)}
-    (first_beside,) = call(bind(first_blocks_kernel), [array(per_two, rows, cols)], table, [beside_soon, beside_later])
+    (cov_diag_one,) = plain(add_kernel, [diag_one], keep, shift(send, "row", 1))
+
+    (first_beside,) = plain(first_blocks_kernel, [array(per_two, rows, cols)], beside_two)
     corner_two = shift(first_beside, "sub", 1)
-    *arrived, panel_early = lax.optimization_barrier((*cross.values(), picks[0], tops[0], panel_two))
-    cross_side = [shift(x, "sub", 1) for x in arrived]
     lower, inner = call(
         bind(root_two_kernel),
         [array(per_two, blocks - 1, rows, cols), array(per_two, 2 * rows, cols)],
         table,
-        [first, rest, panel_early, beside_soon, beside_later, across_two],
+        [first, rest, panel_two, beside_two, across_two],
         [(full, per_two * cols), (low, 2 * cols), (per_two, nodes, rows, cols)],
-        flops=LONG,
-    )
-    parent = {0: [arrived[-2], cross_side[-2], arrived[-1], cross_side[-1]]}
-    for i, k in enumerate(SINGLE):
-        top = after(tops[k], lower)
-        parent[k] = [arrived[i], cross_side[i], top, shift(top, "sub", 1)]
-    groups = GROUPS
-    panels, diags, gots = [], [], []
-    for shifts in groups:
-        if shifts == (LATE,):
-            both = after(tops[LATE], sends)
-            parent[LATE] = [both, shift(both, "sub", 1)]
+    )
+    panels, diags, gots, waits = [], [], [], []
+    for k in ORDER:
+        mine = parents[k]
+        if k == ORDER[1]:
+            mine = after(mine, lower)
+        if k in ORDER[2:]:
+            mine = after(mine, *waits[:2])
         panel, diag, sends = call(
-            bind(parent_two_kernel, shifts),
-            [array(len(shifts), blocks, rows, cols), array(len(shifts), rows, cols), array(len(shifts), 2, rows, cols)],
+            bind(parent_two_kernel, (k,)),
+            [array(1, blocks, rows, cols), array(1, rows, cols), array(1, 2, rows, cols)],
             table,
-            [panel_two, first_beside, across_two, corner_two, lower, inner, diag_two]
-            + [x for k in shifts for x in parent[k]],
+            [panel_two, first_beside, across_two, corner_two, lower, inner, diag_two, mine, shift(mine, "sub", 1)],
             [
                 (low, 2 * cols),
-                (rows, 2 * cols),
+                (2 * rows, 2 * cols),
                 (2 * rows, cols),
                 (low, cols),
                 (low + 2 * rows, 2 * cols),
@@ -360,11 +334,12 @@
                 (2 * rows, cols),
             ],
         )
+        waits.append(sends)
         panels.append(panel)
         diags.append(diag)
         gots.append(shift(sends, "row", 1))
     cov_panel_two, cov_diag_two = call(
-        bind(finish_kernel, groups),
+        bind(finish_kernel, tuple((k,) for k in ORDER)),
         [array(*panel_two.shape), array(*diag_two.shape)],
         table,
         panels + diags + gots,

time: 88.4 us -> 84.3 us (0.954)
  the two profiles are of different devices: /device:TPU:0 before, /device:TPU:18 now
where the time goes in v4:
time: 84.3 us; the launch traced here: 84.1 us
  waiting for transfers between devices  44 us (52%)
  Pallas kernels  17.9 us (21%)
  starting transfers between devices  16.9 us (20%)
  local copies, waits for them, and re-layouts  4.49 us (5%)
    ppermute x24, waiting for transfers between devices, shift(): return lax.ppermute(x, axis, [(i, (i + k) % n) for i in range(n)])  44 us
    pallas_call x8, Pallas kernels, call(): pl.pallas_call(body, out_shape=tuple(out_shapes), in_specs=[SMEM] + [VMEM...  17.2 us
    ppermute x24, starting transfers between devices, shift(): return lax.ppermute(x, axis, [(i, (i + k) % n) for i in range(n)])  16.9 us
  transfers between devices with their start and end apart: 24, of which 14 were waited for; matrix products, arithmetic and copies ran while one was open for 4% of the time, Pallas kernels for 19%

profile of v4, /device:TPU:18, one launch (start us, length us, event | category | flops | bytes accessed | tf_op | source)
XLA Modules:
  0.0 84.1 jit_solution(11195398054678687554)
XLA Ops:
  0.6 0.0 copy-start.1
  0.7 1.1 %dynamic-slice_bitcast_fusion = f32[64,4,256]{2,1,0:T(4,128)S(1)} fusion(f32[1,128,4,256]{3,2,1,0:T(4,128)} %param.10, s32[]{:T(128)S(6)} %select_n.3), kind=kLoop, calls=%fused_computation | loop fusion | bytes 524292 | tf_op jit(solution)/shard_map/dynamic_slice | solution.py:278
  1.7 0.0 copy-start
  1.7 0.0 copy-start.4
  1.8 1.6 %collective-permute-start.2 = (f32[66,4,256]{2,1,0:T(4,128)S(1)}, f32[66,4,256]{2,1,0:T(4,128)S(1)}, u32[]{:S(2)}, u32[]{:S(2)}) collective-permute-start(f32[66,4,256]{2,1,0:T(4,128)S(1)} %pad.4), channel_id=1, source_target_pairs={{0,4},{4,8},{8,12},{12,0},{1,5},{5,9},{9,13},{13,1},{2,6},{6,10},{... | collective-permute-start | bytes 811016 | tf_op jit(solution)/shard_map/ppermute | solution.py:257
  3.4 0.3 collective-permute-start.3
  3.8 1.3 %collective-permute-start.4 = (f32[66,4,256]{2,1,0:T(4,128)S(1)}, f32[66,4,256]{2,1,0:T(4,128)S(1)}, u32[]{:S(2)}, u32[]{:S(2)}) collective-permute-start(f32[66,4,256]{2,1,0:T(4,128)S(1)} %pad.4), channel_id=1, source_target_pairs={{0,12},{4,0},{8,4},{12,8},{1,13},{5,1},{9,5},{13,9},{2,14},{6,2},{... | collective-permute-start | bytes 811016 | tf_op jit(solution)/shard_map/ppermute | solution.py:257
  5.1 0.8 reshape.15
  5.9 0.8 reshape.16
  6.6 0.8 concatenate.3.table
  7.4 1.1 %fusion = (f32[1,4,128,128]{3,2,1,0:T(8,128)S(1)}, f32[1,4,128,128]{3,2,1,0:T(8,128)S(1)}) fusion(f32[2,4,128,128]{3,2,1,0:T(8,128)} %own.8), kind=kLoop, calls=%fused_computation.1 | loop fusion | bytes 1048576 | tf_op jit(solution)/shard_map/slice | solution.py:282
  8.5 0.5 collective-permute-start
  8.9 1.6 %collective-permute-start.1 = (f32[1,4,128,128]{3,2,1,0:T(8,128)S(1)}, f32[1,4,128,128]{3,2,1,0:T(8,128)S(1)}, u32[]{:S(2)}, u32[]{:S(2)}) collective-permute-start(f32[1,4,128,128]{3,2,1,0:T(8,128)S(1)} %get-tuple-element.80), channel_id=1, source_target_pairs={{0,2},{2,0},{1,3},{3,1},{4,6},{6,4},{5,7},{7,5},{8,10},{10,8},{9,1... | collective-permute-start | bytes 786440 | tf_op jit(solution)/shard_map/ppermute | solution.py:257
  10.6 7.2 %collective-permute-done.refs_0_ = f32[1,4,128,128]{3,2,1,0:T(8,128)S(1)} collective-permute-done((f32[1,4,128,128]{3,2,1,0:T(8,128)S(1)}, f32[1,4,128,128]{3,2,1,0:T(8,128)S(1)}, u32[]{:S(2)}, u32[]{:S(2)}) %collective-permute-start) | collective-permute-done | bytes 262176 | tf_op jit(solution)/shard_map/ppermute | solution.py:257
  17.8 3.7 %collective-permute-done.1.refs_1_ = f32[1,4,128,128]{3,2,1,0:T(8,128)S(1)} collective-permute-done((f32[1,4,128,128]{3,2,1,0:T(8,128)S(1)}, f32[1,4,128,128]{3,2,1,0:T(8,128)S(1)}, u32[]{:S(2)}, u32[]{:S(2)}) %collective-permute-start.1) | collective-permute-done | bytes 262176 | tf_op jit(solution)/shard_map/ppermute | solution.py:257
  21.5 1.3 %shard_map.129 = (f32[128,1024]{1,0:T(8,128)S(1)}, f32[1024,256]{1,0:T(8,128)S(1)}, f32[128,256]{1,0:T(8,128)S(1)}) custom-call(s32[123]{0:T(128)S(1)} %concatenate.3.table, f32[128,4,256]{2,1,0:T(4,128)S(1)} %bitcast.8, f32[2,4,128,128]{3,2,1,0:T(8,128)S(1)} %copy-done.1, f32[1,4,128,128]{3,2,1,0:T(8,128)S(1)} %collective-permute-done.refs_0_, ...), custom_call_target="tpu_custom_call" | custom-call | tf_op jit(solution)/shard_map/pallas_call | solution.py:37
  22.8 0.0 collective-permute-done.2.refs_0_
  22.8 0.0 collective-permute-done.3.refs_1_
  22.8 3.5 %collective-permute-done.4.refs_2_ = f32[66,4,256]{2,1,0:T(4,128)S(1)} collective-permute-done((f32[66,4,256]{2,1,0:T(4,128)S(1)}, f32[66,4,256]{2,1,0:T(4,128)S(1)}, u32[]{:S(2)}, u32[]{:S(2)}) %collective-permute-start.4) | collective-permute-done | bytes 270368 | tf_op jit(solution)/shard_map/ppermute | solution.py:257
  26.3 0.0 collective-permute-start.5
  26.3 0.5 collective-permute-start.6
  26.8 0.0 collective-permute-start.7
  26.8 0.5 collective-permute-start.8
  27.3 0.5 collective-permute-start.10
  27.9 0.7 collective-permute-done.6.refs_3_
  28.6 0.4 collective-permute-done.7.refs_4_
  29.0 0.4 collective-permute-done.8.refs_5_
  29.4 0.0 collective-permute-done.5.across
  29.4 3.5 %shard_map.130 = (f32[384,1024]{1,0:T(8,128)S(1)}, f32[2,4,128,128]{3,2,1,0:T(8,128)}, f32[2,128,128]{2,1,0:T(8,128)S(1)}, f32[2,128,128]{2,1,0:T(8,128)S(1)}, f...) custom-call(s32[123]{0:T(128)S(1)} %concatenate.3.table, ...), custom_call_target="tpu_custom_call" | custom-call | tf_op jit(solution)/shard_map/pallas_call | solution.py:37
  32.9 0.1 collective-permute-start.11
  33.1 0.0 collective-permute-start.14
  33.1 4.1 %collective-permute-start.18 = (f32[648,128]{1,0:T(8,128)S(1)}, f32[648,128]{1,0:T(8,128)S(1)}, u32[]{:S(2)}, u32[]{:S(2)}) collective-permute-start(f32[648,128]{1,0:T(8,128)S(1)} %get-tuple-element.69), channel_id=1, source_target_pairs={{0,12},{4,0},{8,4},{12,8},{1,13},{5,1},{9,5},{13,9},{2,14},{6,2},{... | collective-permute-start | bytes 995336 | tf_op jit(solution)/shard_map/ppermute | solution.py:257
  37.1 0.0 collective-permute-start.16
  37.1 15.3 %collective-permute-done.10.panel.beside = f32[4,4,128,128]{3,2,1,0:T(8,128)S(1)} collective-permute-done((f32[4,4,128,128]{3,2,1,0:T(8,128)S(1)}, f32[4,4,128,128]{3,2,1,0:T(8,128)S(1)}, u32[]{:S(2)}, u32[]{:S(2)}) %collective-permute-start.10) | collective-permute-done | bytes 1048608 | tf_op jit(solution)/shard_map/ppermute | solution.py:257
  52.4 0.0 collective-permute-start.13
  52.4 0.0 collective-permute-done.11.across
  52.4 3.8 %shard_map.133 = (f32[4,3,128,128]{3,2,1,0:T(8,128)S(1)}, f32[4,256,128]{2,1,0:T(8,128)S(1)}) custom-call(s32[123]{0:T(128)S(1)} %concatenate.3.table, f32[128,1024]{1,0:T(8,128)S(1)} %get-tuple-element.55.first, f32[384,1024]{1,0:T(8,128)S(1)} %get-tuple-element.56.rest, f32[4,4,128,128]{3,2,1,0:T(8,128)S(1)} %copy-done, ...), custom_call_target="tpu_custom_call" | custom-call | tf_op jit(solution)/shard_map/pallas_call | solution.py:37
  56.3 0.0 collective-permute-done.14.refs_0_
  56.3 0.6 collective-permute-start.15
  56.9 0.1 collective-permute-start.12
  56.9 0.0 collective-permute-done.13.refs_1_
  57.0 1.5 %collective-permute-done.12.corner = f32[4,128,128]{2,1,0:T(8,128)S(1)} collective-permute-done((f32[4,128,128]{2,1,0:T(8,128)S(1)}, f32[4,128,128]{2,1,0:T(8,128)S(1)}, u32[]{:S(2)}, u32[]{:S(2)}) %collective-permute-start.12) | collective-permute-done | bytes 262176 | tf_op jit(solution)/shard_map/ppermute | solution.py:257
  58.5 1.7 %shard_map.134 = (f32[1,4,128,128]{3,2,1,0:T(8,128)S(1)}, f32[1,128,128]{2,1,0:T(8,128)S(1)}, f32[1,2,128,128]{3,2,1,0:T(8,128)S(1)}) custom-call(s32[123]{0:T(128)S(1)} %concatenate.3.table, f32[4,4,128,128]{3,2,1,0:T(8,128)S(1)} %copy-done, f32[4,128,128]{2,1,0:T(8,128)S(1)} %shard_map.132.beside, f32[4,4,128,128]{3,2,1,0:T(8,128)S(1)} %collective-permute-done.11.across, ...), custom_call_target="tpu_custom_call" | custom-call | tf_op jit(solution)/shard_map/pallas_call | solution.py:37
  60.2 0.0 collective-permute-done.15.refs_1_
  60.2 1.7 %shard_map.135 = (f32[1,4,128,128]{3,2,1,0:T(8,128)S(1)}, f32[1,128,128]{2,1,0:T(8,128)S(1)}, f32[1,2,128,128]{3,2,1,0:T(8,128)S(1)}) custom-call(s32[123]{0:T(128)S(1)} %concatenate.3.table, f32[4,4,128,128]{3,2,1,0:T(8,128)S(1)} %copy-done, f32[4,128,128]{2,1,0:T(8,128)S(1)} %shard_map.132.beside, f32[4,4,128,128]{3,2,1,0:T(8,128)S(1)} %collective-permute-done.11.across, ...), custom_call_target="tpu_custom_call" | custom-call | tf_op jit(solution)/shard_map/pallas_call | solution.py:37
  62.0 0.2 collective-permute-done.18.refs_0_
  62.1 0.3 collective-permute-start.19
  62.4 2.8 %collective-permute-done.16.refs_0_ = f32[648,128]{1,0:T(8,128)S(1)} collective-permute-done((f32[648,128]{1,0:T(8,128)S(1)}, f32[648,128]{1,0:T(8,128)S(1)}, u32[]{:S(2)}, u32[]{:S(2)}) %collective-permute-start.16) | collective-permute-done | bytes 331808 | tf_op jit(solution)/shard_map/ppermute | solution.py:257
  65.2 0.1 collective-permute-start.17
  65.3 0.5 collective-permute-start.9
  65.8 1.5 %collective-permute-start.20 = (f32[1,2,128,128]{3,2,1,0:T(8,128)S(1)}, f32[1,2,128,128]{3,2,1,0:T(8,128)S(1)}, u32[]{:S(2)}, u32[]{:S(2)}) collective-permute-start(f32[1,2,128,128]{3,2,1,0:T(8,128)S(1)} %get-tuple-element.65), channel_id=1, source_target_pairs={{0,2},{2,0},{1,3},{3,1},{4,6},{6,4},{5,7},{7,5},{8,10},{10,8},{9,1... | collective-permute-start | bytes 393224 | tf_op jit(solution)/shard_map/ppermute | solution.py:257
  67.3 0.5 collective-permute-start.21
  67.8 0.0 collective-permute-done.19.refs_1_
  67.9 1.7 %shard_map.137 = (f32[1,4,128,128]{3,2,1,0:T(8,128)S(1)}, f32[1,128,128]{2,1,0:T(8,128)S(1)}, f32[1,2,128,128]{3,2,1,0:T(8,128)S(1)}) custom-call(s32[123]{0:T(128)S(1)} %concatenate.3.table, f32[4,4,128,128]{3,2,1,0:T(8,128)S(1)} %copy-done, f32[4,128,128]{2,1,0:T(8,128)S(1)} %shard_map.132.beside, f32[4,4,128,128]{3,2,1,0:T(8,128)S(1)} %collective-permute-done.11.across, ...), custom_call_target="tpu_custom_call" | custom-call | tf_op jit(solution)/shard_map/pallas_call | solution.py:37
  69.6 1.6 %collective-permute-start.23 = (f32[1,2,128,128]{3,2,1,0:T(8,128)S(1)}, f32[1,2,128,128]{3,2,1,0:T(8,128)S(1)}, u32[]{:S(2)}, u32[]{:S(2)}) collective-permute-start(f32[1,2,128,128]{3,2,1,0:T(8,128)S(1)} %get-tuple-element.77), channel_id=1, source_target_pairs={{0,2},{2,0},{1,3},{3,1},{4,6},{6,4},{5,7},{7,5},{8,10},{10,8},{9,1... | collective-permute-start | bytes 393224 | tf_op jit(solution)/shard_map/ppermute | solution.py:257
  71.1 0.0 collective-permute-done.17.refs_1_
  71.1 1.7 %shard_map.136 = (f32[1,4,128,128]{3,2,1,0:T(8,128)S(1)}, f32[1,128,128]{2,1,0:T(8,128)S(1)}, f32[1,2,128,128]{3,2,1,0:T(8,128)S(1)}) custom-call(s32[123]{0:T(128)S(1)} %concatenate.3.table, f32[4,4,128,128]{3,2,1,0:T(8,128)S(1)} %copy-done, f32[4,128,128]{2,1,0:T(8,128)S(1)} %shard_map.132.beside, f32[4,4,128,128]{3,2,1,0:T(8,128)S(1)} %collective-permute-done.11.across, ...), custom_call_target="tpu_custom_call" | custom-call | tf_op jit(solution)/shard_map/pallas_call | solution.py:37
  72.9 0.6 collective-permute-start.22
  73.5 0.7 shard_map.131
  74.1 0.2 collective-permute-done.20.refs_8_
  74.4 2.8 %collective-permute-done.21.refs_9_ = f32[1,2,128,128]{3,2,1,0:T(8,128)S(1)} collective-permute-done((f32[1,2,128,128]{3,2,1,0:T(8,128)S(1)}, f32[1,2,128,128]{3,2,1,0:T(8,128)S(1)}, u32[]{:S(2)}, u32[]{:S(2)}) %collective-permute-start.21) | collective-permute-done | bytes 131104 | tf_op jit(solution)/shard_map/ppermute | solution.py:257
  77.2 2.8 %collective-permute-done.23.refs_11_ = f32[1,2,128,128]{3,2,1,0:T(8,128)S(1)} collective-permute-done((f32[1,2,128,128]{3,2,1,0:T(8,128)S(1)}, f32[1,2,128,128]{3,2,1,0:T(8,128)S(1)}, u32[]{:S(2)}, u32[]{:S(2)}) %collective-permute-start.23) | collective-permute-done | bytes 131104 | tf_op jit(solution)/shard_map/ppermute | solution.py:257
  80.0 2.4 %collective-permute-done.22.refs_10_ = f32[1,2,128,128]{3,2,1,0:T(8,128)S(1)} collective-permute-done((f32[1,2,128,128]{3,2,1,0:T(8,128)S(1)}, f32[1,2,128,128]{3,2,1,0:T(8,128)S(1)}, u32[]{:S(2)}, u32[]{:S(2)}) %collective-permute-start.22) | collective-permute-done | bytes 131104 | tf_op jit(solution)/shard_map/ppermute | solution.py:257
  82.4 1.7 %shard_map.138 = (f32[4,4,128,128]{3,2,1,0:T(8,128)}, f32[4,128,128]{2,1,0:T(8,128)}) custom-call(s32[123]{0:T(128)S(1)} %concatenate.3.table, f32[1,4,128,128]{3,2,1,0:T(8,128)S(1)} %get-tuple-element.60.refs_0_, f32[1,4,128,128]{3,2,1,0:T(8,128)S(1)} %get-tuple-element.63.refs_1_, f32[1,4,128,128]{3,2,1,0:T(8,128)S(1)} %get-tuple-element.68.refs_2_, ...), custom_call_target="tpu_custom_call" | custom-call | tf_op jit(solution)/shard_map/pallas_call | solution.py:37
  (10 shorter events, 0.1 us)
Async XLA Ops:
  0.6 20.9 %copy-start.3 = (f32[1,128,4,256]{3,2,1,0:T(4,128)S(1)}, f32[1,128,4,256]{3,2,1,0:T(4,128)}, u32[]{:S(2)}) copy-start(f32[1,128,4,256]{3,2,1,0:T(4,128)} %param.10) | copy-start | bytes 1572868
  0.6 20.9 %copy-start.1 = (f32[2,4,128,128]{3,2,1,0:T(8,128)S(1)}, f32[2,4,128,128]{3,2,1,0:T(8,128)}, u32[]{:S(2)}) copy-start(f32[2,4,128,128]{3,2,1,0:T(8,128)} %own.8) | copy-start | bytes 1572868
  1.7 25.6 %copy-start = (f32[4,4,128,128]{3,2,1,0:T(8,128)S(1)}, f32[4,4,128,128]{3,2,1,0:T(8,128)}, u32[]{:S(2)}) copy-start(f32[4,4,128,128]{3,2,1,0:T(8,128)} %own.13) | copy-start | bytes 3145732
  1.7 27.7 %copy-start.4 = (f32[2,128,128]{2,1,0:T(8,128)S(1)}, f32[2,128,128]{2,1,0:T(8,128)}, u32[]{:S(2)}) copy-start(f32[2,128,128]{2,1,0:T(8,128)} %diagonal.5) | copy-start | bytes 393220
  1.8 21.0 %collective-permute-start.2 = (f32[66,4,256]{2,1,0:T(4,128)S(1)}, f32[66,4,256]{2,1,0:T(4,128)S(1)}, u32[]{:S(2)}, u32[]{:S(2)}) collective-permute-start(f32[66,4,256]{2,1,0:T(4,128)S(1)} %pad.4), channel_id=1, source_target_pairs={{0,4},{4,8},{8,12},{12,0},{1,5},{5,9},{9,13},{13,1},{2,6},{6,10},{... | collective-permute-start | bytes 811016 | tf_op jit(solution)/shard_map/ppermute | solution.py:257
  3.4 19.4 %collective-permute-start.3 = (f32[66,4,256]{2,1,0:T(4,128)S(1)}, f32[66,4,256]{2,1,0:T(4,128)S(1)}, u32[]{:S(2)}, u32[]{:S(2)}) collective-permute-start(f32[66,4,256]{2,1,0:T(4,128)S(1)} %pad.4), channel_id=1, source_target_pairs={{0,8},{4,12},{8,0},{12,4},{1,9},{5,13},{9,1},{13,5},{2,10},{6,14},... | collective-permute-start | bytes 811016 | tf_op jit(solution)/shard_map/ppermute | solution.py:257
  3.8 22.5 %collective-permute-start.4 = (f32[66,4,256]{2,1,0:T(4,128)S(1)}, f32[66,4,256]{2,1,0:T(4,128)S(1)}, u32[]{:S(2)}, u32[]{:S(2)}) collective-permute-start(f32[66,4,256]{2,1,0:T(4,128)S(1)} %pad.4), channel_id=1, source_target_pairs={{0,12},{4,0},{8,4},{12,8},{1,13},{5,1},{9,5},{13,9},{2,14},{6,2},{... | collective-permute-start | bytes 811016 | tf_op jit(solution)/shard_map/ppermute | solution.py:257
  8.5 9.3 %collective-permute-start = (f32[1,4,128,128]{3,2,1,0:T(8,128)S(1)}, f32[1,4,128,128]{3,2,1,0:T(8,128)S(1)}, u32[]{:S(2)}, u32[]{:S(2)}) collective-permute-start(f32[1,4,128,128]{3,2,1,0:T(8,128)S(1)} %get-tuple-element.81), channel_id=1, source_target_pairs={{0,2},{2,0},{1,3},{3,1},{4,6},{6,4},{5,7},{7,5},{8,10},{10,8},{9,1... | collective-permute-start | bytes 786440 | tf_op jit(solution)/shard_map/ppermute | solution.py:257
  8.9 12.6 %collective-permute-start.1 = (f32[1,4,128,128]{3,2,1,0:T(8,128)S(1)}, f32[1,4,128,128]{3,2,1,0:T(8,128)S(1)}, u32[]{:S(2)}, u32[]{:S(2)}) collective-permute-start(f32[1,4,128,128]{3,2,1,0:T(8,128)S(1)} %get-tuple-element.80), channel_id=1, source_target_pairs={{0,2},{2,0},{1,3},{3,1},{4,6},{6,4},{5,7},{7,5},{8,10},{10,8},{9,1... | collective-permute-start | bytes 786440 | tf_op jit(solution)/shard_map/ppermute | solution.py:257
  26.3 3.1 %collective-permute-start.5 = (f32[2,4,128,128]{3,2,1,0:T(8,128)S(1)}, f32[2,4,128,128]{3,2,1,0:T(8,128)S(1)}, u32[]{:S(2)}, u32[]{:S(2)}) collective-permute-start(f32[2,4,128,128]{3,2,1,0:T(8,128)S(1)} %copy-done.1), channel_id=1, source_target_pairs={{0,1},{1,0},{2,3},{3,2},{4,5},{5,4},{6,7},{7,6},{8,9},{9,8},{10,11... | collective-permute-start | bytes 1572872 | tf_op jit(solution)/shard_map/ppermute | solution.py:257
  26.3 2.3 %collective-permute-start.6 = (f32[66,4,256]{2,1,0:T(4,128)S(1)}, f32[66,4,256]{2,1,0:T(4,128)S(1)}, u32[]{:S(2)}, u32[]{:S(2)}) collective-permute-start(f32[66,4,256]{2,1,0:T(4,128)S(1)} %collective-permute-done.2.refs_0_), channel_id=1, source_target_pairs={{0,1},{1,0},{2,3},{3,2},{4,5},{5,4},{6,7},{7,6},{8,9},{9,8},{10,11... | collective-permute-start | bytes 811016 | tf_op jit(solution)/shard_map/ppermute | solution.py:257
  26.8 2.2 %collective-permute-start.7 = (f32[66,4,256]{2,1,0:T(4,128)S(1)}, f32[66,4,256]{2,1,0:T(4,128)S(1)}, u32[]{:S(2)}, u32[]{:S(2)}) collective-permute-start(f32[66,4,256]{2,1,0:T(4,128)S(1)} %collective-permute-done.3.refs_1_), channel_id=1, source_target_pairs={{0,1},{1,0},{2,3},{3,2},{4,5},{5,4},{6,7},{7,6},{8,9},{9,8},{10,11... | collective-permute-start | bytes 811016 | tf_op jit(solution)/shard_map/ppermute | solution.py:257
  26.8 2.5 %collective-permute-start.8 = (f32[66,4,256]{2,1,0:T(4,128)S(1)}, f32[66,4,256]{2,1,0:T(4,128)S(1)}, u32[]{:S(2)}, u32[]{:S(2)}) collective-permute-start(f32[66,4,256]{2,1,0:T(4,128)S(1)} %collective-permute-done.4.refs_2_), channel_id=1, source_target_pairs={{0,1},{1,0},{2,3},{3,2},{4,5},{5,4},{6,7},{7,6},{8,9},{9,8},{10,11... | collective-permute-start | bytes 811016 | tf_op jit(solution)/shard_map/ppermute | solution.py:257
  27.3 25.1 %collective-permute-start.10 = (f32[4,4,128,128]{3,2,1,0:T(8,128)S(1)}, f32[4,4,128,128]{3,2,1,0:T(8,128)S(1)}, u32[]{:S(2)}, u32[]{:S(2)}) collective-permute-start(f32[4,4,128,128]{3,2,1,0:T(8,128)S(1)} %copy-done), channel_id=1, source_target_pairs={{0,2},{2,0},{1,3},{3,1},{4,6},{6,4},{5,7},{7,5},{8,10},{10,8},{9,1... | collective-permute-start | bytes 3145736 | tf_op jit(solution)/shard_map/ppermute | solution.py:257
  32.9 19.5 %collective-permute-start.11 = (f32[4,4,128,128]{3,2,1,0:T(8,128)S(1)}, f32[4,4,128,128]{3,2,1,0:T(8,128)S(1)}, u32[]{:S(2)}, u32[]{:S(2)}) collective-permute-start(f32[4,4,128,128]{3,2,1,0:T(8,128)S(1)} %copy-done), channel_id=1, source_target_pairs={{0,1},{1,0},{2,3},{3,2},{4,5},{5,4},{6,7},{7,6},{8,9},{9,8},{10,11... | collective-permute-start | bytes 3145736 | tf_op jit(solution)/shard_map/ppermute | solution.py:257
  33.1 23.2 %collective-permute-start.14 = (f32[640,128]{1,0:T(8,128)S(1)}, f32[640,128]{1,0:T(8,128)S(1)}, u32[]{:S(2)}, u32[]{:S(2)}) collective-permute-start(f32[640,128]{1,0:T(8,128)S(1)} %get-tuple-element.61), channel_id=1, source_target_pairs={{0,8},{4,12},{8,0},{12,4},{1,9},{5,13},{9,1},{13,5},{2,10},{6,14},... | collective-permute-start | bytes 983048 | tf_op jit(solution)/shard_map/ppermute | solution.py:257
  33.1 29.1 %collective-permute-start.18 = (f32[648,128]{1,0:T(8,128)S(1)}, f32[648,128]{1,0:T(8,128)S(1)}, u32[]{:S(2)}, u32[]{:S(2)}) collective-permute-start(f32[648,128]{1,0:T(8,128)S(1)} %get-tuple-element.69), channel_id=1, source_target_pairs={{0,12},{4,0},{8,4},{12,8},{1,13},{5,1},{9,5},{13,9},{2,14},{6,2},{... | collective-permute-start | bytes 995336 | tf_op jit(solution)/shard_map/ppermute | solution.py:257
  37.1 28.1 %collective-permute-start.16 = (f32[648,128]{1,0:T(8,128)S(1)}, f32[648,128]{1,0:T(8,128)S(1)}, u32[]{:S(2)}, u32[]{:S(2)}) collective-permute-start(f32[648,128]{1,0:T(8,128)S(1)} %get-tuple-element.64), channel_id=1, source_target_pairs={{0,4},{4,8},{8,12},{12,0},{1,5},{5,9},{9,13},{13,1},{2,6},{6,10},{... | collective-permute-start | bytes 995336 | tf_op jit(solution)/shard_map/ppermute | solution.py:257
  52.4 4.5 %collective-permute-start.13 = (f32[640,128]{1,0:T(8,128)S(1)}, f32[640,128]{1,0:T(8,128)S(1)}, u32[]{:S(2)}, u32[]{:S(2)}) collective-permute-start(f32[640,128]{1,0:T(8,128)S(1)} %get-tuple-element.59.refs_0_), channel_id=1, source_target_pairs={{0,1},{1,0},{2,3},{3,2},{4,5},{5,4},{6,7},{7,6},{8,9},{9,8},{10,11... | collective-permute-start | bytes 983048 | tf_op jit(solution)/shard_map/ppermute | solution.py:257
  52.4 6.1 %copy-start.2 = (f32[4,128,128]{2,1,0:T(8,128)S(1)}, f32[4,128,128]{2,1,0:T(8,128)}, u32[]{:S(2)}) copy-start(f32[4,128,128]{2,1,0:T(8,128)} %diagonal.9) | copy-start | bytes 786436
  56.3 3.9 %collective-permute-start.15 = (f32[640,128]{1,0:T(8,128)S(1)}, f32[640,128]{1,0:T(8,128)S(1)}, u32[]{:S(2)}, u32[]{:S(2)}) collective-permute-start(f32[640,128]{1,0:T(8,128)S(1)} %collective-permute-done.14.refs_0_), channel_id=1, source_target_pairs={{0,1},{1,0},{2,3},{3,2},{4,5},{5,4},{6,7},{7,6},{8,9},{9,8},{10,11... | collective-permute-start | bytes 983048 | tf_op jit(solution)/shard_map/ppermute | solution.py:257
  56.9 1.6 %collective-permute-start.12 = (f32[4,128,128]{2,1,0:T(8,128)S(1)}, f32[4,128,128]{2,1,0:T(8,128)S(1)}, u32[]{:S(2)}, u32[]{:S(2)}) collective-permute-start(f32[4,128,128]{2,1,0:T(8,128)S(1)} %shard_map.132.beside), channel_id=1, source_target_pairs={{0,1},{1,0},{2,3},{3,2},{4,5},{5,4},{6,7},{7,6},{8,9},{9,8},{10,11... | collective-permute-start | bytes 786440 | tf_op jit(solution)/shard_map/ppermute | solution.py:257
  62.1 5.7 %collective-permute-start.19 = (f32[648,128]{1,0:T(8,128)S(1)}, f32[648,128]{1,0:T(8,128)S(1)}, u32[]{:S(2)}, u32[]{:S(2)}) collective-permute-start(f32[648,128]{1,0:T(8,128)S(1)} %collective-permute-done.18.refs_0_), channel_id=1, source_target_pairs={{0,1},{1,0},{2,3},{3,2},{4,5},{5,4},{6,7},{7,6},{8,9},{9,8},{10,11... | collective-permute-start | bytes 995336 | tf_op jit(solution)/shard_map/ppermute | solution.py:257
  65.2 5.9 %collective-permute-start.17 = (f32[648,128]{1,0:T(8,128)S(1)}, f32[648,128]{1,0:T(8,128)S(1)}, u32[]{:S(2)}, u32[]{:S(2)}) collective-permute-start(f32[648,128]{1,0:T(8,128)S(1)} %collective-permute-done.16.refs_0_), channel_id=1, source_target_pairs={{0,1},{1,0},{2,3},{3,2},{4,5},{5,4},{6,7},{7,6},{8,9},{9,8},{10,11... | collective-permute-start | bytes 995336 | tf_op jit(solution)/shard_map/ppermute | solution.py:257
  65.3 8.2 %collective-permute-start.9 = (f32[2,128,128]{2,1,0:T(8,128)S(1)}, f32[2,128,128]{2,1,0:T(8,128)S(1)}, u32[]{:S(2)}, u32[]{:S(2)}) collective-permute-start(f32[2,128,128]{2,1,0:T(8,128)S(1)} %get-tuple-element.52), channel_id=1, source_target_pairs={{0,2},{2,0},{1,3},{3,1},{4,6},{6,4},{5,7},{7,5},{8,10},{10,8},{9,1... | collective-permute-start | bytes 393224 | tf_op jit(solution)/shard_map/ppermute | solution.py:257
  65.8 8.6 %collective-permute-start.20 = (f32[1,2,128,128]{3,2,1,0:T(8,128)S(1)}, f32[1,2,128,128]{3,2,1,0:T(8,128)S(1)}, u32[]{:S(2)}, u32[]{:S(2)}) collective-permute-start(f32[1,2,128,128]{3,2,1,0:T(8,128)S(1)} %get-tuple-element.65), channel_id=1, source_target_pairs={{0,2},{2,0},{1,3},{3,1},{4,6},{6,4},{5,7},{7,5},{8,10},{10,8},{9,1... | collective-permute-start | bytes 393224 | tf_op jit(solution)/shard_map/ppermute | solution.py:257
  67.3 9.9 %collective-permute-start.21 = (f32[1,2,128,128]{3,2,1,0:T(8,128)S(1)}, f32[1,2,128,128]{3,2,1,0:T(8,128)S(1)}, u32[]{:S(2)}, u32[]{:S(2)}) collective-permute-start(f32[1,2,128,128]{3,2,1,0:T(8,128)S(1)} %get-tuple-element.66), channel_id=1, source_target_pairs={{0,2},{2,0},{1,3},{3,1},{4,6},{6,4},{5,7},{7,5},{8,10},{10,8},{9,1... | collective-permute-start | bytes 393224 | tf_op jit(solution)/shard_map/ppermute | solution.py:257
  69.6 10.4 %collective-permute-start.23 = (f32[1,2,128,128]{3,2,1,0:T(8,128)S(1)}, f32[1,2,128,128]{3,2,1,0:T(8,128)S(1)}, u32[]{:S(2)}, u32[]{:S(2)}) collective-permute-start(f32[1,2,128,128]{3,2,1,0:T(8,128)S(1)} %get-tuple-element.77), channel_id=1, source_target_pairs={{0,2},{2,0},{1,3},{3,1},{4,6},{6,4},{5,7},{7,5},{8,10},{10,8},{9,1... | collective-permute-start | bytes 393224 | tf_op jit(solution)/shard_map/ppermute | solution.py:257
  72.9 9.5 %collective-permute-start.22 = (f32[1,2,128,128]{3,2,1,0:T(8,128)S(1)}, f32[1,2,128,128]{3,2,1,0:T(8,128)S(1)}, u32[]{:S(2)}, u32[]{:S(2)}) collective-permute-start(f32[1,2,128,128]{3,2,1,0:T(8,128)S(1)} %get-tuple-element.76), channel_id=1, source_target_pairs={{0,2},{2,0},{1,3},{3,1},{4,6},{6,4},{5,7},{7,5},{8,10},{10,8},{9,1... | collective-permute-start | bytes 393224 | tf_op jit(solution)/shard_map/ppermute | solution.py:257

commit v5 on v4

--- a/solution.py
+++ b/solution.py
@@ -165,46 +165,61 @@
             parents[k][(blocks + 1) * rows :] = jnp.zeros_like(parents[k][(blocks + 1) * rows :])
 
 
-def add_kernel(keep, got, out):
-    out[...] = keep[...] + got[...]
-
-
 def first_blocks_kernel(panel, out):
-    out[...] = panel[:, 0]
-
-
-def root_two_kernel(sizes, table, first, rest, own, beside, across, lower, inner, spread, wide, tall):
+    for h in range(out.shape[0]):
+        start = A * h * out.shape[1]
+        out[h] = panel[start : start + out.shape[1]]
+
+
+def prepare_two_kernel(sizes, table, first, rest, own, across, mine, others, turned, near_rows, spread, wide):
     tree = Tree(table, *sizes)
+    row, sub = tree.row, tree.sub
     per_two, blocks, rows, cols = own.shape
+    for b in range(first.shape[1] // (2 * rows)):
+        lanes = slice(b * rows, (b + 1) * rows)
+        for out, half in (near_rows, row), (others, 1 - row):
+            out[:rows, lanes] = first[:, spot(2 * b + half, rows)]
+            out[rows:, lanes] = rest[:, spot(2 * b + half, rows)]
     spread[...] = jnp.zeros_like(spread)
     for h in range(per_two):
         valid, at = tree.level_two(h)
-        lanes = slice(h * cols, (h + 1) * cols)
         for t in range(1, blocks):
-            spread[spot(at[t - 1] * 2 + tree.row, rows), lanes] = own[h, t] * valid[t]
-            spread[spot(at[t - 1] * 2 + 1 - tree.row, rows), lanes] = beside[h, t] * valid[t]
-    mine = mm(first[...], spread[...])
-    others = mm(rest[...], spread[...])
+            span = slice((t - 1) * rows, t * rows)
+            spread[spot(at[t - 1], rows), h * cols : (h + 1) * cols] = own[h, t] * valid[t]
+            wide[span, spot(sub, cols)] = own[h, t] * valid[t]
+            wide[span, spot(1 - sub, cols)] = across[h, t] * valid[t]
+        wide[(blocks - 1) * rows :, spot(sub, cols)] = own[h, 0]
+        wide[(blocks - 1) * rows :, spot(1 - sub, cols)] = across[h, 0]
+        turned[h] = wide[...].T
+    mine[...] = mm(near_rows[...], spread[...])
+
+
+def root_two_kernel(sizes, table, mine, others, turned, beside, lower, inner, spread, tall):
+    tree = Tree(table, *sizes)
+    per_two, rows, cols = lower.shape[0], lower.shape[2], lower.shape[3]
+    blocks = lower.shape[1] + 1
+    spread[...] = jnp.zeros_like(spread)
     for h in range(per_two):
-        lanes = slice(h * cols, (h + 1) * cols)
-        tall[h, 0] = mine[:, lanes]
-        for k in range(1, tree.nodes):
-            tall[h, k] = others[(k - 1) * rows : k * rows, lanes]
+        valid, at = tree.level_two(h)
+        for t in range(1, blocks):
+            spread[spot(at[t - 1], rows), h * cols : (h + 1) * cols] = beside[(blocks * h + t) * rows : (blocks * h + t + 1) * rows] * valid[t]
+    total = mine[...] + mm(others[...], spread[...])
+    for h in range(per_two):
+        for k in range(tree.nodes):
+            tall[h, k] = total[k * rows : (k + 1) * rows, h * cols : (h + 1) * cols]
     for h in range(per_two):
         valid, at = tree.level_two(h)
         for t in range(1, blocks):
             lower[h, t - 1] = tall[h, tree.back(at[t - 1])] * valid[t]
-            wide[(t - 1) * rows : t * rows, spot(tree.sub, cols)] = own[h, t] * valid[t]
-            wide[(t - 1) * rows : t * rows, spot(1 - tree.sub, cols)] = across[h, t] * valid[t]
-        inner[h] = mm_t(wide[...], lower[h].reshape((blocks - 1) * rows, cols))
-
-
-def parent_two_kernel(sizes, shifts, table, own, beside, across, corner, lower, inner, diagonal, *refs):
+        inner[h] = mm(turned[h, :, : (blocks - 1) * rows], lower[h].reshape((blocks - 1) * rows, cols))
+
+
+def parent_two_kernel(sizes, shifts, table, own, beside, corner, turned, lower, inner, diagonal, *refs):
     tree = Tree(table, *sizes)
     row, sub = tree.row, tree.sub
     blocks, rows, cols = own.shape[1:]
     n = len(shifts)
-    panel, diag, sends, cross, top, first, local, wide, part, more = refs[2 * n :]
+    panel, diag, sends, cross, top, first, far, part, lead, more = refs[2 * n :]
     low = (blocks - 1) * rows
     for i, k in enumerate(shifts):
         h = tree.child(tree.me, tree.node(-k))
@@ -213,28 +228,21 @@
             cross[:, lanes] = got[:low]
             top[spot(row, rows), lanes] = got[low : low + rows]
             top[spot(1 - row, rows), lanes] = got[low + rows : low + 2 * rows]
-        for t in range(1, blocks):
-            span = slice((t - 1) * rows, t * rows)
-            local[span, :] = own[h, t] * valid[t]
-            wide[span, spot(sub, cols)] = local[span, :]
-            wide[span, spot(1 - sub, cols)] = across[h, t] * valid[t]
         first[spot(row, rows), :] = own[h, 0]
         first[spot(1 - row, rows), :] = beside[h]
-        mine = spot(blocks - 1 + row, rows)
-        other = spot(blocks - row, rows)
-        wide[mine, spot(sub, cols)] = own[h, 0]
-        wide[mine, spot(1 - sub, cols)] = across[h, 0]
-        wide[other, spot(sub, cols)] = beside[h]
-        wide[other, spot(1 - sub, cols)] = corner[h]
+        far[:, spot(sub, cols)] = beside[h]
+        far[:, spot(1 - sub, cols)] = corner[h]
         below = mm(cross[...], first[...])
         for t in range(1, blocks):
             span = slice((t - 1) * rows, t * rows)
             part[span, :] = below[span, :] * valid[t]
             panel[i, t] = -(lower[h, t - 1] + part[span, :])
-        part[low:, :] = mm_t(cross[...], local[...]) + mm(top[...], first[...])
-        more[...] = inner[h] + mm_t(wide[...], part[...])
-        panel[i, 0] = -part[mine, :]
-        sends[i, 0] = part[other, :]
+        lead[...] = mm(turned[h, spot(sub, cols), :low], cross[...]).T + mm(top[...], first[...])
+        mine, other = lead[spot(row, rows), :], lead[spot(1 - row, rows), :]
+        part[low:, :] = mine
+        more[...] = inner[h] + mm(turned[h], part[...]) + mm_t(far[...], other)
+        panel[i, 0] = -mine
+        sends[i, 0] = other
         diag[i] = diagonal[h] + more[spot(row, rows), :]
         sends[i, 1] = more[spot(1 - row, rows), :]
 
@@ -243,7 +251,8 @@
     tree = Tree(table, *sizes)
     n = len(groups)
     panels, diags, gots = refs[:n], refs[n : 2 * n], refs[2 * n : 3 * n]
-    panel_out, diag_out = refs[3 * n :]
+    keep, got_one, panel_out, diag_out, one_out = refs[3 * n :]
+    one_out[...] = keep[...] + got_one[...]
     for j, shifts in enumerate(groups):
         for i, k in enumerate(shifts):
             h = tree.child(tree.me, tree.node(-k))
@@ -289,7 +298,8 @@
     *far, total = together((*far, total))
     near = [shift(x, "sub", 1) for x in far]
     across_one = shift(after(panel_one, far[0]), "sub", 1)
-    beside_two = shift(after(panel_two, far[0]), "row", 1)
+    flat = jnp.pad(panel_two.reshape(per_two * blocks * rows, cols), ((0, 16), (0, 0)))
+    beside_two = shift(after(flat, far[0]), "row", 1)
 
     rest, cov_panel_one, keep, send, *parents = call(
         bind(level_one_kernel),
@@ -300,49 +310,60 @@
         [(blocks * rows, 2 * cols), (per_one, nodes, rows, cols), (2 * rows, cols)],
     )
     parents = [x if k == 0 else shift(x, "node", k) for k, x in enumerate(parents)]
+    got_one = shift(send, "row", 1)
     across_two = shift(after(panel_two, send), "sub", 1)
-    (cov_diag_one,) = plain(add_kernel, [diag_one], keep, shift(send, "row", 1))
-
+
+    own_part, others, turned = call(
+        bind(prepare_two_kernel),
+        [array(nodes * rows, per_two * cols), array(nodes * rows, full // 2), array(per_two, 2 * rows, low + rows)],
+        table,
+        [first, rest, panel_two, across_two],
+        [(nodes * rows, full // 2), (full // 2, per_two * cols), (low + rows, 2 * cols)],
+    )
+    beside_two, own_part = together((beside_two, own_part))
     (first_beside,) = plain(first_blocks_kernel, [array(per_two, rows, cols)], beside_two)
     corner_two = shift(first_beside, "sub", 1)
     lower, inner = call(
         bind(root_two_kernel),
         [array(per_two, blocks - 1, rows, cols), array(per_two, 2 * rows, cols)],
         table,
-        [first, rest, panel_two, beside_two, across_two],
-        [(full, per_two * cols), (low, 2 * cols), (per_two, nodes, rows, cols)],
-    )
-    panels, diags, gots, waits = [], [], [], []
+        [own_part, others, turned, beside_two],
+        [(full // 2, per_two * cols), (per_two, nodes, rows, cols)],
+    )
+    panels, diags, gots, sent = [], [], [], []
     for k in ORDER:
         mine = parents[k]
         if k == ORDER[1]:
             mine = after(mine, lower)
         if k in ORDER[2:]:
-            mine = after(mine, *waits[:2])
+            mine = after(mine, *sent[:2])
+        side = shift(mine, "sub", 1)
+        if k == ORDER[1]:
+            mine = after(mine, got_one)
         panel, diag, sends = call(
             bind(parent_two_kernel, (k,)),
             [array(1, blocks, rows, cols), array(1, rows, cols), array(1, 2, rows, cols)],
             table,
-            [panel_two, first_beside, across_two, corner_two, lower, inner, diag_two, mine, shift(mine, "sub", 1)],
+            [panel_two, first_beside, corner_two, turned, lower, inner, diag_two, mine, side],
             [
                 (low, 2 * cols),
                 (2 * rows, 2 * cols),
                 (2 * rows, cols),
-                (low, cols),
-                (low + 2 * rows, 2 * cols),
-                (low + 2 * rows, cols),
+                (rows, 2 * cols),
+                (low + rows, cols),
+                (2 * rows, cols),
                 (2 * rows, cols),
             ],
         )
-        waits.append(sends)
+        sent.append(sends)
         panels.append(panel)
         diags.append(diag)
         gots.append(shift(sends, "row", 1))
-    cov_panel_two, cov_diag_two = call(
+    cov_panel_two, cov_diag_two, cov_diag_one = call(
         bind(finish_kernel, tuple((k,) for k in ORDER)),
-        [array(*panel_two.shape), array(*diag_two.shape)],
+        [array(*panel_two.shape), array(*diag_two.shape), array(*diag_one.shape)],
         table,
-        panels + diags + gots,
+        panels + diags + gots + [keep, got_one],
     )
     return (cov_panel_one, cov_diag_one, cov_panel_two, cov_diag_two)
 

time: 84.3 us -> 81.5 us (0.967)
  waiting for transfers between devices: 44 us -> 41.6 us
    ppermute x24, waiting for transfers between devices: 44 us -> 41.6 us  [shift(): return lax.ppermute(x, axis, [(i, (i + k) % n) for i in range(n)])]
    pallas_call x8 -> x9, Pallas kernels: 17.2 us -> 17.2 us  [call(): pl.pallas_call(body, out_shape=tuple(out_shapes), in_specs=[SMEM] + [VMEM...]
  transfers between devices with their start and end apart: 24 -> 24, of which waited for: 14 -> 13; matrix products, arithmetic and copies ran while one was open for 4% -> 4% of each run, Pallas kernels for 19% -> 19%
where the time goes in v5:
time: 81.5 us; the launch traced here: 81.3 us
  waiting for transfers between devices  41.6 us (51%)
  starting transfers between devices  17.2 us (21%)
  Pallas kernels  17.2 us (21%)
  local copies, waits for them, and re-layouts  4.55 us (6%)
    ppermute x24, waiting for transfers between devices, shift(): return lax.ppermute(x, axis, [(i, (i + k) % n) for i in range(n)])  41.6 us
    pallas_call x9, Pallas kernels, call(): pl.pallas_call(body, out_shape=tuple(out_shapes), in_specs=[SMEM] + [VMEM...  17.2 us
    ppermute x24, starting transfers between devices, shift(): return lax.ppermute(x, axis, [(i, (i + k) % n) for i in range(n)])  17.2 us
  transfers between devices with their start and end apart: 24, of which 13 were waited for; matrix products, arithmetic and copies ran while one was open for 4% of the time, Pallas kernels for 19%

profile of v5, /device:TPU:18, one launch (start us, length us, event | category | flops | bytes accessed | tf_op | source)
XLA Modules:
  0.0 81.3 jit_solution(5420572954486305991)
XLA Ops:
  0.6 0.0 copy-start.1
  0.7 1.1 %dynamic-slice_bitcast_fusion = f32[64,4,256]{2,1,0:T(4,128)S(1)} fusion(f32[1,128,4,256]{3,2,1,0:T(4,128)} %param.10, s32[]{:T(128)S(6)} %select_n.3), kind=kLoop, calls=%fused_computation | loop fusion | bytes 524292 | tf_op jit(solution)/shard_map/dynamic_slice | solution.py:287
  1.7 0.0 copy-start
  1.8 1.6 %collective-permute-start.2 = (f32[66,4,256]{2,1,0:T(4,128)S(1)}, f32[66,4,256]{2,1,0:T(4,128)S(1)}, u32[]{:S(2)}, u32[]{:S(2)}) collective-permute-start(f32[66,4,256]{2,1,0:T(4,128)S(1)} %pad.8), channel_id=1, source_target_pairs={{0,4},{4,8},{8,12},{12,0},{1,5},{5,9},{9,13},{13,1},{2,6},{6,10},{... | collective-permute-start | bytes 811016 | tf_op jit(solution)/shard_map/ppermute | solution.py:266
  3.4 0.3 collective-permute-start.3
  3.7 1.3 %collective-permute-start.4 = (f32[66,4,256]{2,1,0:T(4,128)S(1)}, f32[66,4,256]{2,1,0:T(4,128)S(1)}, u32[]{:S(2)}, u32[]{:S(2)}) collective-permute-start(f32[66,4,256]{2,1,0:T(4,128)S(1)} %pad.8), channel_id=1, source_target_pairs={{0,12},{4,0},{8,4},{12,8},{1,13},{5,1},{9,5},{13,9},{2,14},{6,2},{... | collective-permute-start | bytes 811016 | tf_op jit(solution)/shard_map/ppermute | solution.py:266
  5.1 0.8 reshape.18
  5.9 0.8 reshape.19
  6.6 0.8 concatenate.3.table
  7.4 1.1 %fusion = (f32[1,4,128,128]{3,2,1,0:T(8,128)S(1)}, f32[1,4,128,128]{3,2,1,0:T(8,128)S(1)}) fusion(f32[2,4,128,128]{3,2,1,0:T(8,128)} %own.8), kind=kLoop, calls=%fused_computation.1 | loop fusion | bytes 1048576 | tf_op jit(solution)/shard_map/slice | solution.py:291
  8.5 0.5 collective-permute-start
  8.9 1.6 %collective-permute-start.1 = (f32[1,4,128,128]{3,2,1,0:T(8,128)S(1)}, f32[1,4,128,128]{3,2,1,0:T(8,128)S(1)}, u32[]{:S(2)}, u32[]{:S(2)}) collective-permute-start(f32[1,4,128,128]{3,2,1,0:T(8,128)S(1)} %get-tuple-element.94), channel_id=1, source_target_pairs={{0,2},{2,0},{1,3},{3,1},{4,6},{6,4},{5,7},{7,5},{8,10},{10,8},{9,1... | collective-permute-start | bytes 786440 | tf_op jit(solution)/shard_map/ppermute | solution.py:266
  10.6 7.2 %collective-permute-done.refs_0_ = f32[1,4,128,128]{3,2,1,0:T(8,128)S(1)} collective-permute-done((f32[1,4,128,128]{3,2,1,0:T(8,128)S(1)}, f32[1,4,128,128]{3,2,1,0:T(8,128)S(1)}, u32[]{:S(2)}, u32[]{:S(2)}) %collective-permute-start) | collective-permute-done | bytes 262176 | tf_op jit(solution)/shard_map/ppermute | solution.py:266
  17.8 3.7 %collective-permute-done.1.refs_1_ = f32[1,4,128,128]{3,2,1,0:T(8,128)S(1)} collective-permute-done((f32[1,4,128,128]{3,2,1,0:T(8,128)S(1)}, f32[1,4,128,128]{3,2,1,0:T(8,128)S(1)}, u32[]{:S(2)}, u32[]{:S(2)}) %collective-permute-start.1) | collective-permute-done | bytes 262176 | tf_op jit(solution)/shard_map/ppermute | solution.py:266
  21.5 1.3 %shard_map.129 = (f32[128,1024]{1,0:T(8,128)S(1)}, f32[1024,256]{1,0:T(8,128)S(1)}, f32[128,256]{1,0:T(8,128)S(1)}) custom-call(s32[123]{0:T(128)S(1)} %concatenate.3.table, f32[128,4,256]{2,1,0:T(4,128)S(1)} %bitcast.10, f32[2,4,128,128]{3,2,1,0:T(8,128)S(1)} %copy-done.1, f32[1,4,128,128]{3,2,1,0:T(8,128)S(1)} %collective-permute-done.refs_0_, ...), custom_call_target="tpu_custom_call" | custom-call | tf_op jit(solution)/shard_map/pallas_call | solution.py:37
  22.8 0.0 collective-permute-done.2.refs_0_
  22.8 0.0 collective-permute-done.3.refs_1_
  22.8 3.5 %collective-permute-done.4.refs_2_ = f32[66,4,256]{2,1,0:T(4,128)S(1)} collective-permute-done((f32[66,4,256]{2,1,0:T(4,128)S(1)}, f32[66,4,256]{2,1,0:T(4,128)S(1)}, u32[]{:S(2)}, u32[]{:S(2)}) %collective-permute-start.4) | collective-permute-done | bytes 270368 | tf_op jit(solution)/shard_map/ppermute | solution.py:266
  26.3 0.0 collective-permute-start.5
  26.3 0.5 collective-permute-start.6
  26.8 0.0 collective-permute-start.7
  26.8 0.5 collective-permute-start.8
  27.3 0.1 pad.9
  27.4 0.6 collective-permute-start.9
  28.0 0.6 collective-permute-done.6.refs_3_
  28.6 0.4 collective-permute-done.7.refs_4_
  29.0 0.4 collective-permute-done.8.refs_5_
  29.4 0.0 collective-permute-done.5.across
  29.4 3.5 %shard_map.130 = (f32[384,1024]{1,0:T(8,128)S(1)}, f32[2,4,128,128]{3,2,1,0:T(8,128)}, f32[2,128,128]{2,1,0:T(8,128)S(1)}, f32[2,128,128]{2,1,0:T(8,128)S(1)}, f...) custom-call(s32[123]{0:T(128)S(1)} %concatenate.3.table, ...), custom_call_target="tpu_custom_call" | custom-call | tf_op jit(solution)/shard_map/pallas_call | solution.py:37
  32.9 0.1 collective-permute-start.10
  33.0 0.0 collective-permute-start.13
  33.0 0.5 collective-permute-start.14
  33.6 4.1 %collective-permute-start.18 = (f32[648,128]{1,0:T(8,128)S(1)}, f32[648,128]{1,0:T(8,128)S(1)}, u32[]{:S(2)}, u32[]{:S(2)}) collective-permute-start(f32[648,128]{1,0:T(8,128)S(1)} %get-tuple-element.81), channel_id=1, source_target_pairs={{0,12},{4,0},{8,4},{12,8},{1,13},{5,1},{9,5},{13,9},{2,14},{6,2},{... | collective-permute-start | bytes 995336 | tf_op jit(solution)/shard_map/ppermute | solution.py:266
  37.7 0.0 collective-permute-done.10.across
  37.7 0.5 collective-permute-start.16
  38.2 1.9 %shard_map.131 = (f32[512,512]{1,0:T(8,128)S(1)}, f32[512,512]{1,0:T(8,128)S(1)}, f32[4,256,512]{2,1,0:T(8,128)S(1)}) custom-call(s32[123]{0:T(128)S(1)} %concatenate.3.table, f32[128,1024]{1,0:T(8,128)S(1)} %get-tuple-element.59.first, f32[384,1024]{1,0:T(8,128)S(1)} %get-tuple-element.60.rest, f32[4,4,128,128]{3,2,1,0:T(8,128)S(1)} %copy-done, ...), custom_call_target="tpu_custom_call" | custom-call | tf_op jit(solution)/shard_map/pallas_call | solution.py:37
  40.1 13.5 %collective-permute-done.9.panel.beside = f32[2064,128]{1,0:T(8,128)S(1)} collective-permute-done((f32[2064,128]{1,0:T(8,128)S(1)}, f32[2064,128]{1,0:T(8,128)S(1)}, u32[]{:S(2)}, u32[]{:S(2)}) %collective-permute-start.9) | collective-permute-done | bytes 1056800 | tf_op jit(solution)/shard_map/ppermute | solution.py:266
  53.7 0.0 collective-permute-start.12
  53.7 2.7 %shard_map.133 = (f32[4,3,128,128]{3,2,1,0:T(8,128)S(1)}, f32[4,256,128]{2,1,0:T(8,128)S(1)}) custom-call(s32[123]{0:T(128)S(1)} %concatenate.3.table, f32[512,512]{1,0:T(8,128)S(1)} %get-tuple-element.66.mine, f32[512,512]{1,0:T(8,128)S(1)} %get-tuple-element.67.others, f32[4,256,512]{2,1,0:T(8,128)S(1)} %get-tuple-element.65.turned, ...), custom_call_target="tpu_custom_call" | custom-call | tf_op jit(solution)/shard_map/pallas_call | solution.py:37
  56.4 0.0 collective-permute-done.13.refs_0_
  56.4 0.6 collective-permute-start.15
  57.0 0.0 collective-permute-done.14.refs_13_
  57.0 0.1 collective-permute-start.11
  57.1 0.0 collective-permute-done.12.refs_1_
  57.1 1.5 %collective-permute-done.11.corner = f32[4,128,128]{2,1,0:T(8,128)S(1)} collective-permute-done((f32[4,128,128]{2,1,0:T(8,128)S(1)}, f32[4,128,128]{2,1,0:T(8,128)S(1)}, u32[]{:S(2)}, u32[]{:S(2)}) %collective-permute-start.11) | collective-permute-done | bytes 262176 | tf_op jit(solution)/shard_map/ppermute | solution.py:266
  58.6 1.5 %shard_map.134 = (f32[1,4,128,128]{3,2,1,0:T(8,128)S(1)}, f32[1,128,128]{2,1,0:T(8,128)S(1)}, f32[1,2,128,128]{3,2,1,0:T(8,128)S(1)}) custom-call(s32[123]{0:T(128)S(1)} %concatenate.3.table, f32[4,4,128,128]{3,2,1,0:T(8,128)S(1)} %copy-done, f32[4,128,128]{2,1,0:T(8,128)S(1)} %shard_map.132.beside, f32[4,128,128]{2,1,0:T(8,128)S(1)} %collective-permute-done.11.corner, ...), custom_call_target="tpu_custom_call" | custom-call | tf_op jit(solution)/shard_map/pallas_call | solution.py:37
  60.1 0.0 collective-permute-done.15.refs_1_
  60.1 1.5 %shard_map.135 = (f32[1,4,128,128]{3,2,1,0:T(8,128)S(1)}, f32[1,128,128]{2,1,0:T(8,128)S(1)}, f32[1,2,128,128]{3,2,1,0:T(8,128)S(1)}) custom-call(s32[123]{0:T(128)S(1)} %concatenate.3.table, f32[4,4,128,128]{3,2,1,0:T(8,128)S(1)} %copy-done, f32[4,128,128]{2,1,0:T(8,128)S(1)} %shard_map.132.beside, f32[4,128,128]{2,1,0:T(8,128)S(1)} %collective-permute-done.11.corner, ...), custom_call_target="tpu_custom_call" | custom-call | tf_op jit(solution)/shard_map/pallas_call | solution.py:37
  61.6 0.5 collective-permute-done.18.refs_0_
  62.1 0.0 collective-permute-start.19
  62.1 3.1 %collective-permute-done.16.refs_0_ = f32[648,128]{1,0:T(8,128)S(1)} collective-permute-done((f32[648,128]{1,0:T(8,128)S(1)}, f32[648,128]{1,0:T(8,128)S(1)}, u32[]{:S(2)}, u32[]{:S(2)}) %collective-permute-start.16) | collective-permute-done | bytes 331808 | tf_op jit(solution)/shard_map/ppermute | solution.py:266
  65.2 0.1 collective-permute-start.17
  65.3 0.5 collective-permute-start.20
  65.8 1.5 %collective-permute-start.21 = (f32[1,2,128,128]{3,2,1,0:T(8,128)S(1)}, f32[1,2,128,128]{3,2,1,0:T(8,128)S(1)}, u32[]{:S(2)}, u32[]{:S(2)}) collective-permute-start(f32[1,2,128,128]{3,2,1,0:T(8,128)S(1)} %get-tuple-element.78), channel_id=1, source_target_pairs={{0,2},{2,0},{1,3},{3,1},{4,6},{6,4},{5,7},{7,5},{8,10},{10,8},{9,1... | collective-permute-start | bytes 393224 | tf_op jit(solution)/shard_map/ppermute | solution.py:266
  67.3 1.5 %shard_map.137 = (f32[1,4,128,128]{3,2,1,0:T(8,128)S(1)}, f32[1,128,128]{2,1,0:T(8,128)S(1)}, f32[1,2,128,128]{3,2,1,0:T(8,128)S(1)}) custom-call(s32[123]{0:T(128)S(1)} %concatenate.3.table, f32[4,4,128,128]{3,2,1,0:T(8,128)S(1)} %copy-done, f32[4,128,128]{2,1,0:T(8,128)S(1)} %shard_map.132.beside, f32[4,128,128]{2,1,0:T(8,128)S(1)} %collective-permute-done.11.corner, ...), custom_call_target="tpu_custom_call" | custom-call | tf_op jit(solution)/shard_map/pallas_call | solution.py:37
  68.8 0.6 collective-permute-start.23
  69.4 0.0 collective-permute-done.17.refs_1_
  69.4 1.5 %shard_map.136 = (f32[1,4,128,128]{3,2,1,0:T(8,128)S(1)}, f32[1,128,128]{2,1,0:T(8,128)S(1)}, f32[1,2,128,128]{3,2,1,0:T(8,128)S(1)}) custom-call(s32[123]{0:T(128)S(1)} %concatenate.3.table, f32[4,4,128,128]{3,2,1,0:T(8,128)S(1)} %copy-done, f32[4,128,128]{2,1,0:T(8,128)S(1)} %shard_map.132.beside, f32[4,128,128]{2,1,0:T(8,128)S(1)} %collective-permute-done.11.corner, ...), custom_call_target="tpu_custom_call" | custom-call | tf_op jit(solution)/shard_map/pallas_call | solution.py:37
  70.9 1.6 %collective-permute-start.22 = (f32[1,2,128,128]{3,2,1,0:T(8,128)S(1)}, f32[1,2,128,128]{3,2,1,0:T(8,128)S(1)}, u32[]{:S(2)}, u32[]{:S(2)}) collective-permute-start(f32[1,2,128,128]{3,2,1,0:T(8,128)S(1)} %get-tuple-element.88), channel_id=1, source_target_pairs={{0,2},{2,0},{1,3},{3,1},{4,6},{6,4},{5,7},{7,5},{8,10},{10,8},{9,1... | collective-permute-start | bytes 393224 | tf_op jit(solution)/shard_map/ppermute | solution.py:266
  72.5 0.0 collective-permute-done.20.refs_8_
  72.5 1.9 %collective-permute-done.21.refs_9_ = f32[1,2,128,128]{3,2,1,0:T(8,128)S(1)} collective-permute-done((f32[1,2,128,128]{3,2,1,0:T(8,128)S(1)}, f32[1,2,128,128]{3,2,1,0:T(8,128)S(1)}, u32[]{:S(2)}, u32[]{:S(2)}) %collective-permute-start.21) | collective-permute-done | bytes 131104 | tf_op jit(solution)/shard_map/ppermute | solution.py:266
  74.4 2.8 %collective-permute-done.23.refs_11_ = f32[1,2,128,128]{3,2,1,0:T(8,128)S(1)} collective-permute-done((f32[1,2,128,128]{3,2,1,0:T(8,128)S(1)}, f32[1,2,128,128]{3,2,1,0:T(8,128)S(1)}, u32[]{:S(2)}, u32[]{:S(2)}) %collective-permute-start.23) | collective-permute-done | bytes 131104 | tf_op jit(solution)/shard_map/ppermute | solution.py:266
  77.2 2.4 %collective-permute-done.22.refs_10_ = f32[1,2,128,128]{3,2,1,0:T(8,128)S(1)} collective-permute-done((f32[1,2,128,128]{3,2,1,0:T(8,128)S(1)}, f32[1,2,128,128]{3,2,1,0:T(8,128)S(1)}, u32[]{:S(2)}, u32[]{:S(2)}) %collective-permute-start.22) | collective-permute-done | bytes 131104 | tf_op jit(solution)/shard_map/ppermute | solution.py:266
  79.6 1.8 %shard_map.138 = (f32[4,4,128,128]{3,2,1,0:T(8,128)}, f32[4,128,128]{2,1,0:T(8,128)}, f32[2,128,128]{2,1,0:T(8,128)}) custom-call(s32[123]{0:T(128)S(1)} %concatenate.3.table, f32[1,4,128,128]{3,2,1,0:T(8,128)S(1)} %get-tuple-element.71.refs_0_, f32[1,4,128,128]{3,2,1,0:T(8,128)S(1)} %get-tuple-element.75.refs_1_, ...), custom_call_target="tpu_custom_call" | custom-call | tf_op jit(solution)/shard_map/pallas_call | solution.py:37
  (11 shorter events, 0.1 us)
Async XLA Ops:
  0.6 20.9 %copy-start.3 = (f32[1,128,4,256]{3,2,1,0:T(4,128)S(1)}, f32[1,128,4,256]{3,2,1,0:T(4,128)}, u32[]{:S(2)}) copy-start(f32[1,128,4,256]{3,2,1,0:T(4,128)} %param.10) | copy-start | bytes 1572868
  0.6 20.9 %copy-start.1 = (f32[2,4,128,128]{3,2,1,0:T(8,128)S(1)}, f32[2,4,128,128]{3,2,1,0:T(8,128)}, u32[]{:S(2)}) copy-start(f32[2,4,128,128]{3,2,1,0:T(8,128)} %own.8) | copy-start | bytes 1572868
  1.7 25.6 %copy-start = (f32[4,4,128,128]{3,2,1,0:T(8,128)S(1)}, f32[4,4,128,128]{3,2,1,0:T(8,128)}, u32[]{:S(2)}) copy-start(f32[4,4,128,128]{3,2,1,0:T(8,128)} %own.13) | copy-start | bytes 3145732
  1.8 21.0 %collective-permute-start.2 = (f32[66,4,256]{2,1,0:T(4,128)S(1)}, f32[66,4,256]{2,1,0:T(4,128)S(1)}, u32[]{:S(2)}, u32[]{:S(2)}) collective-permute-start(f32[66,4,256]{2,1,0:T(4,128)S(1)} %pad.8), channel_id=1, source_target_pairs={{0,4},{4,8},{8,12},{12,0},{1,5},{5,9},{9,13},{13,1},{2,6},{6,10},{... | collective-permute-start | bytes 811016 | tf_op jit(solution)/shard_map/ppermute | solution.py:266
  3.4 19.4 %collective-permute-start.3 = (f32[66,4,256]{2,1,0:T(4,128)S(1)}, f32[66,4,256]{2,1,0:T(4,128)S(1)}, u32[]{:S(2)}, u32[]{:S(2)}) collective-permute-start(f32[66,4,256]{2,1,0:T(4,128)S(1)} %pad.8), channel_id=1, source_target_pairs={{0,8},{4,12},{8,0},{12,4},{1,9},{5,13},{9,1},{13,5},{2,10},{6,14},... | collective-permute-start | bytes 811016 | tf_op jit(solution)/shard_map/ppermute | solution.py:266
  3.7 22.5 %collective-permute-start.4 = (f32[66,4,256]{2,1,0:T(4,128)S(1)}, f32[66,4,256]{2,1,0:T(4,128)S(1)}, u32[]{:S(2)}, u32[]{:S(2)}) collective-permute-start(f32[66,4,256]{2,1,0:T(4,128)S(1)} %pad.8), channel_id=1, source_target_pairs={{0,12},{4,0},{8,4},{12,8},{1,13},{5,1},{9,5},{13,9},{2,14},{6,2},{... | collective-permute-start | bytes 811016 | tf_op jit(solution)/shard_map/ppermute | solution.py:266
  8.5 9.3 %collective-permute-start = (f32[1,4,128,128]{3,2,1,0:T(8,128)S(1)}, f32[1,4,128,128]{3,2,1,0:T(8,128)S(1)}, u32[]{:S(2)}, u32[]{:S(2)}) collective-permute-start(f32[1,4,128,128]{3,2,1,0:T(8,128)S(1)} %get-tuple-element.95), channel_id=1, source_target_pairs={{0,2},{2,0},{1,3},{3,1},{4,6},{6,4},{5,7},{7,5},{8,10},{10,8},{9,1... | collective-permute-start | bytes 786440 | tf_op jit(solution)/shard_map/ppermute | solution.py:266
  8.9 12.6 %collective-permute-start.1 = (f32[1,4,128,128]{3,2,1,0:T(8,128)S(1)}, f32[1,4,128,128]{3,2,1,0:T(8,128)S(1)}, u32[]{:S(2)}, u32[]{:S(2)}) collective-permute-start(f32[1,4,128,128]{3,2,1,0:T(8,128)S(1)} %get-tuple-element.94), channel_id=1, source_target_pairs={{0,2},{2,0},{1,3},{3,1},{4,6},{6,4},{5,7},{7,5},{8,10},{10,8},{9,1... | collective-permute-start | bytes 786440 | tf_op jit(solution)/shard_map/ppermute | solution.py:266
  21.5 7.9 %copy-start.4 = (f32[2,128,128]{2,1,0:T(8,128)S(1)}, f32[2,128,128]{2,1,0:T(8,128)}, u32[]{:S(2)}) copy-start(f32[2,128,128]{2,1,0:T(8,128)} %diagonal.5) | copy-start | bytes 393220
  26.3 3.1 %collective-permute-start.5 = (f32[2,4,128,128]{3,2,1,0:T(8,128)S(1)}, f32[2,4,128,128]{3,2,1,0:T(8,128)S(1)}, u32[]{:S(2)}, u32[]{:S(2)}) collective-permute-start(f32[2,4,128,128]{3,2,1,0:T(8,128)S(1)} %copy-done.1), channel_id=1, source_target_pairs={{0,1},{1,0},{2,3},{3,2},{4,5},{5,4},{6,7},{7,6},{8,9},{9,8},{10,11... | collective-permute-start | bytes 1572872 | tf_op jit(solution)/shard_map/ppermute | solution.py:266
  26.3 2.3 %collective-permute-start.6 = (f32[66,4,256]{2,1,0:T(4,128)S(1)}, f32[66,4,256]{2,1,0:T(4,128)S(1)}, u32[]{:S(2)}, u32[]{:S(2)}) collective-permute-start(f32[66,4,256]{2,1,0:T(4,128)S(1)} %collective-permute-done.2.refs_0_), channel_id=1, source_target_pairs={{0,1},{1,0},{2,3},{3,2},{4,5},{5,4},{6,7},{7,6},{8,9},{9,8},{10,11... | collective-permute-start | bytes 811016 | tf_op jit(solution)/shard_map/ppermute | solution.py:266
  26.8 2.2 %collective-permute-start.7 = (f32[66,4,256]{2,1,0:T(4,128)S(1)}, f32[66,4,256]{2,1,0:T(4,128)S(1)}, u32[]{:S(2)}, u32[]{:S(2)}) collective-permute-start(f32[66,4,256]{2,1,0:T(4,128)S(1)} %collective-permute-done.3.refs_1_), channel_id=1, source_target_pairs={{0,1},{1,0},{2,3},{3,2},{4,5},{5,4},{6,7},{7,6},{8,9},{9,8},{10,11... | collective-permute-start | bytes 811016 | tf_op jit(solution)/shard_map/ppermute | solution.py:266
  26.8 2.5 %collective-permute-start.8 = (f32[66,4,256]{2,1,0:T(4,128)S(1)}, f32[66,4,256]{2,1,0:T(4,128)S(1)}, u32[]{:S(2)}, u32[]{:S(2)}) collective-permute-start(f32[66,4,256]{2,1,0:T(4,128)S(1)} %collective-permute-done.4.refs_2_), channel_id=1, source_target_pairs={{0,1},{1,0},{2,3},{3,2},{4,5},{5,4},{6,7},{7,6},{8,9},{9,8},{10,11... | collective-permute-start | bytes 811016 | tf_op jit(solution)/shard_map/ppermute | solution.py:266
  27.4 26.3 %collective-permute-start.9 = (f32[2064,128]{1,0:T(8,128)S(1)}, f32[2064,128]{1,0:T(8,128)S(1)}, u32[]{:S(2)}, u32[]{:S(2)}) collective-permute-start(f32[2064,128]{1,0:T(8,128)S(1)} %pad.9), channel_id=1, source_target_pairs={{0,2},{2,0},{1,3},{3,1},{4,6},{6,4},{5,7},{7,5},{8,10},{10,8},{9,1... | collective-permute-start | bytes 3170312 | tf_op jit(solution)/shard_map/ppermute | solution.py:266
  32.9 4.8 %collective-permute-start.10 = (f32[4,4,128,128]{3,2,1,0:T(8,128)S(1)}, f32[4,4,128,128]{3,2,1,0:T(8,128)S(1)}, u32[]{:S(2)}, u32[]{:S(2)}) collective-permute-start(f32[4,4,128,128]{3,2,1,0:T(8,128)S(1)} %copy-done), channel_id=1, source_target_pairs={{0,1},{1,0},{2,3},{3,2},{4,5},{5,4},{6,7},{7,6},{8,9},{9,8},{10,11... | collective-permute-start | bytes 3145736 | tf_op jit(solution)/shard_map/ppermute | solution.py:266
  33.0 23.3 %collective-permute-start.13 = (f32[640,128]{1,0:T(8,128)S(1)}, f32[640,128]{1,0:T(8,128)S(1)}, u32[]{:S(2)}, u32[]{:S(2)}) collective-permute-start(f32[640,128]{1,0:T(8,128)S(1)} %get-tuple-element.72), channel_id=1, source_target_pairs={{0,8},{4,12},{8,0},{12,4},{1,9},{5,13},{9,1},{13,5},{2,10},{6,14},... | collective-permute-start | bytes 983048 | tf_op jit(solution)/shard_map/ppermute | solution.py:266
  33.0 23.9 %collective-permute-start.14 = (f32[2,128,128]{2,1,0:T(8,128)S(1)}, f32[2,128,128]{2,1,0:T(8,128)S(1)}, u32[]{:S(2)}, u32[]{:S(2)}) collective-permute-start(f32[2,128,128]{2,1,0:T(8,128)S(1)} %get-tuple-element.61), channel_id=1, source_target_pairs={{0,2},{2,0},{1,3},{3,1},{4,6},{6,4},{5,7},{7,5},{8,10},{10,8},{9,1... | collective-permute-start | bytes 393224 | tf_op jit(solution)/shard_map/ppermute | solution.py:266
  33.6 28.5 %collective-permute-start.18 = (f32[648,128]{1,0:T(8,128)S(1)}, f32[648,128]{1,0:T(8,128)S(1)}, u32[]{:S(2)}, u32[]{:S(2)}) collective-permute-start(f32[648,128]{1,0:T(8,128)S(1)} %get-tuple-element.81), channel_id=1, source_target_pairs={{0,12},{4,0},{8,4},{12,8},{1,13},{5,1},{9,5},{13,9},{2,14},{6,2},{... | collective-permute-start | bytes 995336 | tf_op jit(solution)/shard_map/ppermute | solution.py:266
  37.7 27.6 %collective-permute-start.16 = (f32[648,128]{1,0:T(8,128)S(1)}, f32[648,128]{1,0:T(8,128)S(1)}, u32[]{:S(2)}, u32[]{:S(2)}) collective-permute-start(f32[648,128]{1,0:T(8,128)S(1)} %get-tuple-element.76), channel_id=1, source_target_pairs={{0,4},{4,8},{8,12},{12,0},{1,5},{5,9},{9,13},{13,1},{2,6},{6,10},{... | collective-permute-start | bytes 995336 | tf_op jit(solution)/shard_map/ppermute | solution.py:266
  53.7 3.4 %collective-permute-start.12 = (f32[640,128]{1,0:T(8,128)S(1)}, f32[640,128]{1,0:T(8,128)S(1)}, u32[]{:S(2)}, u32[]{:S(2)}) collective-permute-start(f32[640,128]{1,0:T(8,128)S(1)} %get-tuple-element.70.refs_0_), channel_id=1, source_target_pairs={{0,1},{1,0},{2,3},{3,2},{4,5},{5,4},{6,7},{7,6},{8,9},{9,8},{10,11... | collective-permute-start | bytes 983048 | tf_op jit(solution)/shard_map/ppermute | solution.py:266
  53.7 4.9 %copy-start.2 = (f32[4,128,128]{2,1,0:T(8,128)S(1)}, f32[4,128,128]{2,1,0:T(8,128)}, u32[]{:S(2)}) copy-start(f32[4,128,128]{2,1,0:T(8,128)} %diagonal.9) | copy-start | bytes 786436
  56.4 3.7 %collective-permute-start.15 = (f32[640,128]{1,0:T(8,128)S(1)}, f32[640,128]{1,0:T(8,128)S(1)}, u32[]{:S(2)}, u32[]{:S(2)}) collective-permute-start(f32[640,128]{1,0:T(8,128)S(1)} %collective-permute-done.13.refs_0_), channel_id=1, source_target_pairs={{0,1},{1,0},{2,3},{3,2},{4,5},{5,4},{6,7},{7,6},{8,9},{9,8},{10,11... | collective-permute-start | bytes 983048 | tf_op jit(solution)/shard_map/ppermute | solution.py:266
  57.0 1.6 %collective-permute-start.11 = (f32[4,128,128]{2,1,0:T(8,128)S(1)}, f32[4,128,128]{2,1,0:T(8,128)S(1)}, u32[]{:S(2)}, u32[]{:S(2)}) collective-permute-start(f32[4,128,128]{2,1,0:T(8,128)S(1)} %shard_map.132.beside), channel_id=1, source_target_pairs={{0,1},{1,0},{2,3},{3,2},{4,5},{5,4},{6,7},{7,6},{8,9},{9,8},{10,11... | collective-permute-start | bytes 786440 | tf_op jit(solution)/shard_map/ppermute | solution.py:266
  62.1 5.2 %collective-permute-start.19 = (f32[648,128]{1,0:T(8,128)S(1)}, f32[648,128]{1,0:T(8,128)S(1)}, u32[]{:S(2)}, u32[]{:S(2)}) collective-permute-start(f32[648,128]{1,0:T(8,128)S(1)} %collective-permute-done.18.refs_0_), channel_id=1, source_target_pairs={{0,1},{1,0},{2,3},{3,2},{4,5},{5,4},{6,7},{7,6},{8,9},{9,8},{10,11... | collective-permute-start | bytes 995336 | tf_op jit(solution)/shard_map/ppermute | solution.py:266
  65.2 4.2 %collective-permute-start.17 = (f32[648,128]{1,0:T(8,128)S(1)}, f32[648,128]{1,0:T(8,128)S(1)}, u32[]{:S(2)}, u32[]{:S(2)}) collective-permute-start(f32[648,128]{1,0:T(8,128)S(1)} %collective-permute-done.16.refs_0_), channel_id=1, source_target_pairs={{0,1},{1,0},{2,3},{3,2},{4,5},{5,4},{6,7},{7,6},{8,9},{9,8},{10,11... | collective-permute-start | bytes 995336 | tf_op jit(solution)/shard_map/ppermute | solution.py:266
  65.3 7.2 %collective-permute-start.20 = (f32[1,2,128,128]{3,2,1,0:T(8,128)S(1)}, f32[1,2,128,128]{3,2,1,0:T(8,128)S(1)}, u32[]{:S(2)}, u32[]{:S(2)}) collective-permute-start(f32[1,2,128,128]{3,2,1,0:T(8,128)S(1)} %get-tuple-element.77), channel_id=1, source_target_pairs={{0,2},{2,0},{1,3},{3,1},{4,6},{6,4},{5,7},{7,5},{8,10},{10,8},{9,1... | collective-permute-start | bytes 393224 | tf_op jit(solution)/shard_map/ppermute | solution.py:266
  65.8 8.6 %collective-permute-start.21 = (f32[1,2,128,128]{3,2,1,0:T(8,128)S(1)}, f32[1,2,128,128]{3,2,1,0:T(8,128)S(1)}, u32[]{:S(2)}, u32[]{:S(2)}) collective-permute-start(f32[1,2,128,128]{3,2,1,0:T(8,128)S(1)} %get-tuple-element.78), channel_id=1, source_target_pairs={{0,2},{2,0},{1,3},{3,1},{4,6},{6,4},{5,7},{7,5},{8,10},{10,8},{9,1... | collective-permute-start | bytes 393224 | tf_op jit(solution)/shard_map/ppermute | solution.py:266
  68.8 8.4 %collective-permute-start.23 = (f32[1,2,128,128]{3,2,1,0:T(8,128)S(1)}, f32[1,2,128,128]{3,2,1,0:T(8,128)S(1)}, u32[]{:S(2)}, u32[]{:S(2)}) collective-permute-start(f32[1,2,128,128]{3,2,1,0:T(8,128)S(1)} %get-tuple-element.89), channel_id=1, source_target_pairs={{0,2},{2,0},{1,3},{3,1},{4,6},{6,4},{5,7},{7,5},{8,10},{10,8},{9,1... | collective-permute-start | bytes 393224 | tf_op jit(solution)/shard_map/ppermute | solution.py:266
  70.9 8.6 %collective-permute-start.22 = (f32[1,2,128,128]{3,2,1,0:T(8,128)S(1)}, f32[1,2,128,128]{3,2,1,0:T(8,128)S(1)}, u32[]{:S(2)}, u32[]{:S(2)}) collective-permute-start(f32[1,2,128,128]{3,2,1,0:T(8,128)S(1)} %get-tuple-element.88), channel_id=1, source_target_pairs={{0,2},{2,0},{1,3},{3,1},{4,6},{6,4},{5,7},{7,5},{8,10},{10,8},{9,1... | collective-permute-start | bytes 393224 | tf_op jit(solution)/shard_map/ppermute | solution.py:266

commit v6 on v5

--- a/solution.py
+++ b/solution.py
@@ -94,6 +94,11 @@
 
 def fill_rows(out, at, rows, parts):
     for first, part in parts:
+        if len(part.shape) == 2:
+            high, wide = rows // 2, part.shape[1]
+            for c in range(out.shape[1] // wide):
+                out[pl.ds(pl.multiple_of(at + first, high), high), c * wide : (c + 1) * wide] = part[c * high : (c + 1) * high]
+            continue
         width = part.shape[2]
         for b in range(part.shape[1]):
             out[pl.ds(pl.multiple_of(at + first, rows // 2), part.shape[0]), b * width : (b + 1) * width] = part[:, b, :]
@@ -137,7 +142,7 @@
     per_one, blocks, rows, cols = own.shape
     half = rows // 2
     for i in range(shifts):
-        fill_rows(rest, i * rows, rows, [(tree.sub * half, far[i].at[:half]), ((1 - tree.sub) * half, near[i].at[:half])])
+        fill_rows(rest, i * rows, rows, [(tree.sub * half, far[i]), ((1 - tree.sub) * half, near[i])])
     others = mm(rest[...], spread[...])
     for g in range(per_one):
         lanes = slice(g * cols, (g + 1) * cols)
@@ -285,7 +290,8 @@
     together = lax.optimization_barrier
 
     half = lax.dynamic_slice_in_dim(root_inverse[0], sub * (rows // 2), rows // 2, 0)
-    half = jnp.pad(half, ((0, 2), (0, 0), (0, 0)))
+    half = half.reshape(rows // 2, full // cols, cols).transpose(1, 0, 2).reshape(-1, cols)
+    half = jnp.pad(half, ((0, 8), (0, 0)))
     far = [shift(half, "node", k) for k in range(1, nodes)]
     source = after(panel_one, table)
     beside_one = [shift(source[g : g + 1], "row", 1) for g in range(per_one)]

time: 81.5 us -> 80.9 us (level)
  local copies, waits for them, and re-layouts: 4.55 us -> 1.63 us
  waiting for transfers between devices: 41.6 us -> 43.9 us
    ppermute x24, waiting for transfers between devices: 41.6 us -> 43.9 us  [shift(): return lax.ppermute(x, axis, [(i, (i + k) % n) for i in range(n)])]
    slice x1, local copies, waits for them, and re-layouts: 1.07 us -> 0.04 us  [paired_shards(): beside_one = [shift(source[g:g + 1], 'row', 1) for g in range(per_one)]]
  transfers between devices with their start and end apart: 24 -> 24, of which waited for: 13 -> 14; matrix products, arithmetic and copies ran while one was open for 4% -> 0% of each run, Pallas kernels for 19% -> 19%
where the time goes in v6:
time: 80.9 us; the launch traced here: 80.8 us
  waiting for transfers between devices  43.9 us (54%)
  starting transfers between devices  17.5 us (22%)
  Pallas kernels  16.8 us (21%)
  local copies, waits for them, and re-layouts  1.63 us (2%)
  between operations  0.86 us (1%)
    ppermute x24, waiting for transfers between devices, shift(): return lax.ppermute(x, axis, [(i, (i + k) % n) for i in range(n)])  43.9 us
    ppermute x24, starting transfers between devices, shift(): return lax.ppermute(x, axis, [(i, (i + k) % n) for i in range(n)])  17.5 us
    pallas_call x9, Pallas kernels, call(): pl.pallas_call(body, out_shape=tuple(out_shapes), in_specs=[SMEM] + [VMEM...  16.8 us
  transfers between devices with their start and end apart: 24, of which 14 were waited for; matrix products, arithmetic and copies ran while one was open for 0% of the time, Pallas kernels for 19%

profile of v6, /device:TPU:18, one launch (start us, length us, event | category | flops | bytes accessed | tf_op | source)
XLA Modules:
  0.0 80.8 jit_solution(11280380794893792088)
XLA Ops:
  0.7 1.1 %constant_dynamic-slice_fusion = f32[1,64,4,256]{3,2,1,0:T(4,128)S(1)} fusion(f32[1,128,4,256]{3,2,1,0:T(4,128)} %param.10, s32[]{:T(128)S(6)} %select_n.3), kind=kLoop, calls=%fused_computation | loop fusion | bytes 524292 | tf_op jit(solution)/shard_map/dynamic_slice | solution.py:292
  1.8 0.1 reshape.27
  1.9 0.1 copy.14
  1.9 0.0 copy-start
  2.0 1.6 %collective-permute-start.2 = (f32[520,128]{1,0:T(8,128)S(1)}, f32[520,128]{1,0:T(8,128)S(1)}, u32[]{:S(2)}, u32[]{:S(2)}) collective-permute-start(f32[520,128]{1,0:T(8,128)S(1)} %pad.8), channel_id=1, source_target_pairs={{0,4},{4,8},{8,12},{12,0},{1,5},{5,9},{9,13},{13,1},{2,6},{6,10},{... | collective-permute-start | bytes 798728 | tf_op jit(solution)/shard_map/ppermute | solution.py:271
  3.6 0.3 collective-permute-start.3
  4.0 1.3 %collective-permute-start.4 = (f32[520,128]{1,0:T(8,128)S(1)}, f32[520,128]{1,0:T(8,128)S(1)}, u32[]{:S(2)}, u32[]{:S(2)}) collective-permute-start(f32[520,128]{1,0:T(8,128)S(1)} %pad.8), channel_id=1, source_target_pairs={{0,12},{4,0},{8,4},{12,8},{1,13},{5,1},{9,5},{13,9},{2,14},{6,2},{... | collective-permute-start | bytes 798728 | tf_op jit(solution)/shard_map/ppermute | solution.py:271
  5.3 0.1 reshape.25
  5.4 0.1 reshape.26
  5.5 0.1 concatenate.3.table
  5.6 0.5 collective-permute-start
  6.1 1.6 %collective-permute-start.1 = (f32[1,4,128,128]{3,2,1,0:T(8,128)S(1)}, f32[1,4,128,128]{3,2,1,0:T(8,128)S(1)}, u32[]{:S(2)}, u32[]{:S(2)}) collective-permute-start(f32[1,4,128,128]{3,2,1,0:T(8,128)S(1)} %get-tuple-element.94), channel_id=1, source_target_pairs={{0,2},{2,0},{1,3},{3,1},{4,6},{6,4},{5,7},{7,5},{8,10},{10,8},{9,1... | collective-permute-start | bytes 786440 | tf_op jit(solution)/shard_map/ppermute | solution.py:271
  7.7 7.2 %collective-permute-done.refs_0_ = f32[1,4,128,128]{3,2,1,0:T(8,128)S(1)} collective-permute-done((f32[1,4,128,128]{3,2,1,0:T(8,128)S(1)}, f32[1,4,128,128]{3,2,1,0:T(8,128)S(1)}, u32[]{:S(2)}, u32[]{:S(2)}) %collective-permute-start) | collective-permute-done | bytes 262176 | tf_op jit(solution)/shard_map/ppermute | solution.py:271
  14.9 3.7 %collective-permute-done.1.refs_1_ = f32[1,4,128,128]{3,2,1,0:T(8,128)S(1)} collective-permute-done((f32[1,4,128,128]{3,2,1,0:T(8,128)S(1)}, f32[1,4,128,128]{3,2,1,0:T(8,128)S(1)}, u32[]{:S(2)}, u32[]{:S(2)}) %collective-permute-start.1) | collective-permute-done | bytes 262176 | tf_op jit(solution)/shard_map/ppermute | solution.py:271
  18.6 1.3 %shard_map.129 = (f32[128,1024]{1,0:T(8,128)S(1)}, f32[1024,256]{1,0:T(8,128)S(1)}, f32[128,256]{1,0:T(8,128)S(1)}) custom-call(s32[123]{0:T(128)S(1)} %concatenate.3.table, f32[128,4,256]{2,1,0:T(4,128)S(1)} %bitcast.10, f32[2,4,128,128]{3,2,1,0:T(8,128)S(1)} %copy-done.1, f32[1,4,128,128]{3,2,1,0:T(8,128)S(1)} %collective-permute-done.refs_0_, ...), custom_call_target="tpu_custom_call" | custom-call | tf_op jit(solution)/shard_map/pallas_call | solution.py:37
  19.9 2.8 %collective-permute-done.2.refs_0_ = f32[520,128]{1,0:T(8,128)S(1)} collective-permute-done((f32[520,128]{1,0:T(8,128)S(1)}, f32[520,128]{1,0:T(8,128)S(1)}, u32[]{:S(2)}, u32[]{:S(2)}) %collective-permute-start.2) | collective-permute-done | bytes 266272 | tf_op jit(solution)/shard_map/ppermute | solution.py:271
  22.7 0.0 collective-permute-done.3.refs_1_
  22.7 3.4 %collective-permute-done.4.refs_2_ = f32[520,128]{1,0:T(8,128)S(1)} collective-permute-done((f32[520,128]{1,0:T(8,128)S(1)}, f32[520,128]{1,0:T(8,128)S(1)}, u32[]{:S(2)}, u32[]{:S(2)}) %collective-permute-start.4) | collective-permute-done | bytes 266272 | tf_op jit(solution)/shard_map/ppermute | solution.py:271
  26.2 0.0 collective-permute-start.5
  26.2 0.5 collective-permute-start.6
  26.7 0.0 collective-permute-start.7
  26.7 0.5 collective-permute-start.8
  27.2 0.1 pad.9
  27.2 0.6 collective-permute-start.9
  27.8 0.6 collective-permute-done.6.refs_3_
  28.4 0.4 collective-permute-done.7.refs_4_
  28.8 0.4 collective-permute-done.8.refs_5_
  29.2 0.0 collective-permute-done.5.across
  29.2 3.1 %shard_map.130 = (f32[384,1024]{1,0:T(8,128)S(1)}, f32[2,4,128,128]{3,2,1,0:T(8,128)}, f32[2,128,128]{2,1,0:T(8,128)S(1)}, f32[2,128,128]{2,1,0:T(8,128)S(1)}, f...) custom-call(s32[123]{0:T(128)S(1)} %concatenate.3.table, ...), custom_call_target="tpu_custom_call" | custom-call | tf_op jit(solution)/shard_map/pallas_call | solution.py:37
  32.3 0.1 collective-permute-start.10
  32.5 0.0 collective-permute-start.13
  32.5 0.5 collective-permute-start.14
  33.0 4.1 %collective-permute-start.18 = (f32[648,128]{1,0:T(8,128)S(1)}, f32[648,128]{1,0:T(8,128)S(1)}, u32[]{:S(2)}, u32[]{:S(2)}) collective-permute-start(f32[648,128]{1,0:T(8,128)S(1)} %get-tuple-element.81), channel_id=1, source_target_pairs={{0,12},{4,0},{8,4},{12,8},{1,13},{5,1},{9,5},{13,9},{2,14},{6,2},{... | collective-permute-start | bytes 995336 | tf_op jit(solution)/shard_map/ppermute | solution.py:271
  37.1 0.0 collective-permute-done.10.across
  37.1 0.5 collective-permute-start.16
  37.6 1.9 %shard_map.131 = (f32[512,512]{1,0:T(8,128)S(1)}, f32[512,512]{1,0:T(8,128)S(1)}, f32[4,256,512]{2,1,0:T(8,128)S(1)}) custom-call(s32[123]{0:T(128)S(1)} %concatenate.3.table, f32[128,1024]{1,0:T(8,128)S(1)} %get-tuple-element.59.first, f32[384,1024]{1,0:T(8,128)S(1)} %get-tuple-element.60.rest, f32[4,4,128,128]{3,2,1,0:T(8,128)S(1)} %copy-done, ...), custom_call_target="tpu_custom_call" | custom-call | tf_op jit(solution)/shard_map/pallas_call | solution.py:37
  39.6 13.9 %collective-permute-done.9.panel.beside = f32[2064,128]{1,0:T(8,128)S(1)} collective-permute-done((f32[2064,128]{1,0:T(8,128)S(1)}, f32[2064,128]{1,0:T(8,128)S(1)}, u32[]{:S(2)}, u32[]{:S(2)}) %collective-permute-start.9) | collective-permute-done | bytes 1056800 | tf_op jit(solution)/shard_map/ppermute | solution.py:271
  53.5 0.0 collective-permute-start.12
  53.5 2.7 %shard_map.133 = (f32[4,3,128,128]{3,2,1,0:T(8,128)S(1)}, f32[4,256,128]{2,1,0:T(8,128)S(1)}) custom-call(s32[123]{0:T(128)S(1)} %concatenate.3.table, f32[512,512]{1,0:T(8,128)S(1)} %get-tuple-element.66.mine, f32[512,512]{1,0:T(8,128)S(1)} %get-tuple-element.67.others, f32[4,256,512]{2,1,0:T(8,128)S(1)} %get-tuple-element.65.turned, ...), custom_call_target="tpu_custom_call" | custom-call | tf_op jit(solution)/shard_map/pallas_call | solution.py:37
  56.2 0.0 collective-permute-done.13.refs_0_
  56.2 0.6 collective-permute-start.15
  56.8 0.0 collective-permute-done.14.refs_13_
  56.8 0.1 collective-permute-start.11
  56.9 1.5 %collective-permute-done.11.corner = f32[4,128,128]{2,1,0:T(8,128)S(1)} collective-permute-done((f32[4,128,128]{2,1,0:T(8,128)S(1)}, f32[4,128,128]{2,1,0:T(8,128)S(1)}, u32[]{:S(2)}, u32[]{:S(2)}) %collective-permute-start.11) | collective-permute-done | bytes 262176 | tf_op jit(solution)/shard_map/ppermute | solution.py:271
  58.4 1.5 %shard_map.134 = (f32[1,4,128,128]{3,2,1,0:T(8,128)S(1)}, f32[1,128,128]{2,1,0:T(8,128)S(1)}, f32[1,2,128,128]{3,2,1,0:T(8,128)S(1)}) custom-call(s32[123]{0:T(128)S(1)} %concatenate.3.table, f32[4,4,128,128]{3,2,1,0:T(8,128)S(1)} %copy-done, f32[4,128,128]{2,1,0:T(8,128)S(1)} %shard_map.132.beside, f32[4,128,128]{2,1,0:T(8,128)S(1)} %collective-permute-done.11.corner, ...), custom_call_target="tpu_custom_call" | custom-call | tf_op jit(solution)/shard_map/pallas_call | solution.py:37
  59.9 0.0 collective-permute-done.15.refs_1_
  59.9 1.5 %shard_map.135 = (f32[1,4,128,128]{3,2,1,0:T(8,128)S(1)}, f32[1,128,128]{2,1,0:T(8,128)S(1)}, f32[1,2,128,128]{3,2,1,0:T(8,128)S(1)}) custom-call(s32[123]{0:T(128)S(1)} %concatenate.3.table, f32[4,4,128,128]{3,2,1,0:T(8,128)S(1)} %copy-done, f32[4,128,128]{2,1,0:T(8,128)S(1)} %shard_map.132.beside, f32[4,128,128]{2,1,0:T(8,128)S(1)} %collective-permute-done.11.corner, ...), custom_call_target="tpu_custom_call" | custom-call | tf_op jit(solution)/shard_map/pallas_call | solution.py:37
  61.5 0.1 collective-permute-done.18.refs_0_
  61.6 0.4 collective-permute-start.19
  61.9 2.7 %collective-permute-done.16.refs_0_ = f32[648,128]{1,0:T(8,128)S(1)} collective-permute-done((f32[648,128]{1,0:T(8,128)S(1)}, f32[648,128]{1,0:T(8,128)S(1)}, u32[]{:S(2)}, u32[]{:S(2)}) %collective-permute-start.16) | collective-permute-done | bytes 331808 | tf_op jit(solution)/shard_map/ppermute | solution.py:271
  64.7 0.1 collective-permute-start.17
  64.7 0.5 collective-permute-start.20
  65.3 1.5 %collective-permute-start.21 = (f32[1,2,128,128]{3,2,1,0:T(8,128)S(1)}, f32[1,2,128,128]{3,2,1,0:T(8,128)S(1)}, u32[]{:S(2)}, u32[]{:S(2)}) collective-permute-start(f32[1,2,128,128]{3,2,1,0:T(8,128)S(1)} %get-tuple-element.78), channel_id=1, source_target_pairs={{0,2},{2,0},{1,3},{3,1},{4,6},{6,4},{5,7},{7,5},{8,10},{10,8},{9,1... | collective-permute-start | bytes 393224 | tf_op jit(solution)/shard_map/ppermute | solution.py:271
  66.7 0.0 collective-permute-done.19.refs_1_
  66.8 1.5 %shard_map.137 = (f32[1,4,128,128]{3,2,1,0:T(8,128)S(1)}, f32[1,128,128]{2,1,0:T(8,128)S(1)}, f32[1,2,128,128]{3,2,1,0:T(8,128)S(1)}) custom-call(s32[123]{0:T(128)S(1)} %concatenate.3.table, f32[4,4,128,128]{3,2,1,0:T(8,128)S(1)} %copy-done, f32[4,128,128]{2,1,0:T(8,128)S(1)} %shard_map.132.beside, f32[4,128,128]{2,1,0:T(8,128)S(1)} %collective-permute-done.11.corner, ...), custom_call_target="tpu_custom_call" | custom-call | tf_op jit(solution)/shard_map/pallas_call | solution.py:37
  68.3 0.6 collective-permute-start.23
  68.9 0.0 collective-permute-done.17.refs_1_
  68.9 1.5 %shard_map.136 = (f32[1,4,128,128]{3,2,1,0:T(8,128)S(1)}, f32[1,128,128]{2,1,0:T(8,128)S(1)}, f32[1,2,128,128]{3,2,1,0:T(8,128)S(1)}) custom-call(s32[123]{0:T(128)S(1)} %concatenate.3.table, f32[4,4,128,128]{3,2,1,0:T(8,128)S(1)} %copy-done, f32[4,128,128]{2,1,0:T(8,128)S(1)} %shard_map.132.beside, f32[4,128,128]{2,1,0:T(8,128)S(1)} %collective-permute-done.11.corner, ...), custom_call_target="tpu_custom_call" | custom-call | tf_op jit(solution)/shard_map/pallas_call | solution.py:37
  70.4 1.6 %collective-permute-start.22 = (f32[1,2,128,128]{3,2,1,0:T(8,128)S(1)}, f32[1,2,128,128]{3,2,1,0:T(8,128)S(1)}, u32[]{:S(2)}, u32[]{:S(2)}) collective-permute-start(f32[1,2,128,128]{3,2,1,0:T(8,128)S(1)} %get-tuple-element.88), channel_id=1, source_target_pairs={{0,2},{2,0},{1,3},{3,1},{4,6},{6,4},{5,7},{7,5},{8,10},{10,8},{9,1... | collective-permute-start | bytes 393224 | tf_op jit(solution)/shard_map/ppermute | solution.py:271
  71.9 0.0 collective-permute-done.20.refs_8_
  71.9 1.9 %collective-permute-done.21.refs_9_ = f32[1,2,128,128]{3,2,1,0:T(8,128)S(1)} collective-permute-done((f32[1,2,128,128]{3,2,1,0:T(8,128)S(1)}, f32[1,2,128,128]{3,2,1,0:T(8,128)S(1)}, u32[]{:S(2)}, u32[]{:S(2)}) %collective-permute-start.21) | collective-permute-done | bytes 131104 | tf_op jit(solution)/shard_map/ppermute | solution.py:271
  73.8 2.8 %collective-permute-done.23.refs_11_ = f32[1,2,128,128]{3,2,1,0:T(8,128)S(1)} collective-permute-done((f32[1,2,128,128]{3,2,1,0:T(8,128)S(1)}, f32[1,2,128,128]{3,2,1,0:T(8,128)S(1)}, u32[]{:S(2)}, u32[]{:S(2)}) %collective-permute-start.23) | collective-permute-done | bytes 131104 | tf_op jit(solution)/shard_map/ppermute | solution.py:271
  76.6 2.4 %collective-permute-done.22.refs_10_ = f32[1,2,128,128]{3,2,1,0:T(8,128)S(1)} collective-permute-done((f32[1,2,128,128]{3,2,1,0:T(8,128)S(1)}, f32[1,2,128,128]{3,2,1,0:T(8,128)S(1)}, u32[]{:S(2)}, u32[]{:S(2)}) %collective-permute-start.22) | collective-permute-done | bytes 131104 | tf_op jit(solution)/shard_map/ppermute | solution.py:271
  79.0 1.8 %shard_map.138 = (f32[4,4,128,128]{3,2,1,0:T(8,128)}, f32[4,128,128]{2,1,0:T(8,128)}, f32[2,128,128]{2,1,0:T(8,128)}) custom-call(s32[123]{0:T(128)S(1)} %concatenate.3.table, f32[1,4,128,128]{3,2,1,0:T(8,128)S(1)} %get-tuple-element.71.refs_0_, f32[1,4,128,128]{3,2,1,0:T(8,128)S(1)} %get-tuple-element.75.refs_1_, ...), custom_call_target="tpu_custom_call" | custom-call | tf_op jit(solution)/shard_map/pallas_call | solution.py:37
  (23 shorter events, 0.1 us)
Async XLA Ops:
  0.6 4.7 %copy-start.5 = (s32[8,4]{0,1:T(4,128)S(1)}, s32[8,4]{0,1:T(4,128)}, u32[]{:S(2)}) copy-start(s32[8,4]{0,1:T(4,128)} %param.15) | copy-start | bytes 388
  0.6 4.7 %copy-start.6 = (s32[16,3]{0,1:T(4,128)S(1)}, s32[16,3]{0,1:T(4,128)}, u32[]{:S(2)}) copy-start(s32[16,3]{0,1:T(4,128)} %param.19) | copy-start | bytes 580
  0.7 4.8 %copy-start.7 = (s32[8]{0:T(128)S(1)}, s32[8]{0:T(128)}, u32[]{:S(2)}) copy-start(s32[8]{0:T(128)} %param.16) | copy-start | bytes 100
  0.7 4.8 %copy-start.8 = (s32[16]{0:T(128)S(1)}, s32[16]{0:T(128)}, u32[]{:S(2)}) copy-start(s32[16]{0:T(128)} %param.17) | copy-start | bytes 196
  0.7 4.8 %copy-start.9 = (s32[16]{0:T(128)S(1)}, s32[16]{0:T(128)}, u32[]{:S(2)}) copy-start(s32[16]{0:T(128)} %param.18) | copy-start | bytes 196
  0.7 4.9 %copy-start.1 = (f32[2,4,128,128]{3,2,1,0:T(8,128)S(1)}, f32[2,4,128,128]{3,2,1,0:T(8,128)}, u32[]{:S(2)}) copy-start(f32[2,4,128,128]{3,2,1,0:T(8,128)} %own.8) | copy-start | bytes 1572868
  0.7 17.9 %copy-start.3 = (f32[1,128,4,256]{3,2,1,0:T(4,128)S(1)}, f32[1,128,4,256]{3,2,1,0:T(4,128)}, u32[]{:S(2)}) copy-start(f32[1,128,4,256]{3,2,1,0:T(4,128)} %param.10) | copy-start | bytes 1572868
  1.9 25.2 %copy-start = (f32[4,4,128,128]{3,2,1,0:T(8,128)S(1)}, f32[4,4,128,128]{3,2,1,0:T(8,128)}, u32[]{:S(2)}) copy-start(f32[4,4,128,128]{3,2,1,0:T(8,128)} %own.13) | copy-start | bytes 3145732
  2.0 20.7 %collective-permute-start.2 = (f32[520,128]{1,0:T(8,128)S(1)}, f32[520,128]{1,0:T(8,128)S(1)}, u32[]{:S(2)}, u32[]{:S(2)}) collective-permute-start(f32[520,128]{1,0:T(8,128)S(1)} %pad.8), channel_id=1, source_target_pairs={{0,4},{4,8},{8,12},{12,0},{1,5},{5,9},{9,13},{13,1},{2,6},{6,10},{... | collective-permute-start | bytes 798728 | tf_op jit(solution)/shard_map/ppermute | solution.py:271
  3.6 19.1 %collective-permute-start.3 = (f32[520,128]{1,0:T(8,128)S(1)}, f32[520,128]{1,0:T(8,128)S(1)}, u32[]{:S(2)}, u32[]{:S(2)}) collective-permute-start(f32[520,128]{1,0:T(8,128)S(1)} %pad.8), channel_id=1, source_target_pairs={{0,8},{4,12},{8,0},{12,4},{1,9},{5,13},{9,1},{13,5},{2,10},{6,14},... | collective-permute-start | bytes 798728 | tf_op jit(solution)/shard_map/ppermute | solution.py:271
  4.0 22.2 %collective-permute-start.4 = (f32[520,128]{1,0:T(8,128)S(1)}, f32[520,128]{1,0:T(8,128)S(1)}, u32[]{:S(2)}, u32[]{:S(2)}) collective-permute-start(f32[520,128]{1,0:T(8,128)S(1)} %pad.8), channel_id=1, source_target_pairs={{0,12},{4,0},{8,4},{12,8},{1,13},{5,1},{9,5},{13,9},{2,14},{6,2},{... | collective-permute-start | bytes 798728 | tf_op jit(solution)/shard_map/ppermute | solution.py:271
  5.6 9.3 %collective-permute-start = (f32[1,4,128,128]{3,2,1,0:T(8,128)S(1)}, f32[1,4,128,128]{3,2,1,0:T(8,128)S(1)}, u32[]{:S(2)}, u32[]{:S(2)}) collective-permute-start(f32[1,4,128,128]{3,2,1,0:T(8,128)S(1)} %get-tuple-element.95), channel_id=1, source_target_pairs={{0,2},{2,0},{1,3},{3,1},{4,6},{6,4},{5,7},{7,5},{8,10},{10,8},{9,1... | collective-permute-start | bytes 786440 | tf_op jit(solution)/shard_map/ppermute | solution.py:271
  6.1 12.6 %collective-permute-start.1 = (f32[1,4,128,128]{3,2,1,0:T(8,128)S(1)}, f32[1,4,128,128]{3,2,1,0:T(8,128)S(1)}, u32[]{:S(2)}, u32[]{:S(2)}) collective-permute-start(f32[1,4,128,128]{3,2,1,0:T(8,128)S(1)} %get-tuple-element.94), channel_id=1, source_target_pairs={{0,2},{2,0},{1,3},{3,1},{4,6},{6,4},{5,7},{7,5},{8,10},{10,8},{9,1... | collective-permute-start | bytes 786440 | tf_op jit(solution)/shard_map/ppermute | solution.py:271
  18.6 10.6 %copy-start.4 = (f32[2,128,128]{2,1,0:T(8,128)S(1)}, f32[2,128,128]{2,1,0:T(8,128)}, u32[]{:S(2)}) copy-start(f32[2,128,128]{2,1,0:T(8,128)} %diagonal.5) | copy-start | bytes 393220
  26.2 3.1 %collective-permute-start.5 = (f32[2,4,128,128]{3,2,1,0:T(8,128)S(1)}, f32[2,4,128,128]{3,2,1,0:T(8,128)S(1)}, u32[]{:S(2)}, u32[]{:S(2)}) collective-permute-start(f32[2,4,128,128]{3,2,1,0:T(8,128)S(1)} %copy-done.1), channel_id=1, source_target_pairs={{0,1},{1,0},{2,3},{3,2},{4,5},{5,4},{6,7},{7,6},{8,9},{9,8},{10,11... | collective-permute-start | bytes 1572872 | tf_op jit(solution)/shard_map/ppermute | solution.py:271
  26.2 2.3 %collective-permute-start.6 = (f32[520,128]{1,0:T(8,128)S(1)}, f32[520,128]{1,0:T(8,128)S(1)}, u32[]{:S(2)}, u32[]{:S(2)}) collective-permute-start(f32[520,128]{1,0:T(8,128)S(1)} %collective-permute-done.2.refs_0_), channel_id=1, source_target_pairs={{0,1},{1,0},{2,3},{3,2},{4,5},{5,4},{6,7},{7,6},{8,9},{9,8},{10,11... | collective-permute-start | bytes 798728 | tf_op jit(solution)/shard_map/ppermute | solution.py:271
  26.7 2.2 %collective-permute-start.7 = (f32[520,128]{1,0:T(8,128)S(1)}, f32[520,128]{1,0:T(8,128)S(1)}, u32[]{:S(2)}, u32[]{:S(2)}) collective-permute-start(f32[520,128]{1,0:T(8,128)S(1)} %collective-permute-done.3.refs_1_), channel_id=1, source_target_pairs={{0,1},{1,0},{2,3},{3,2},{4,5},{5,4},{6,7},{7,6},{8,9},{9,8},{10,11... | collective-permute-start | bytes 798728 | tf_op jit(solution)/shard_map/ppermute | solution.py:271
  26.7 2.5 %collective-permute-start.8 = (f32[520,128]{1,0:T(8,128)S(1)}, f32[520,128]{1,0:T(8,128)S(1)}, u32[]{:S(2)}, u32[]{:S(2)}) collective-permute-start(f32[520,128]{1,0:T(8,128)S(1)} %collective-permute-done.4.refs_2_), channel_id=1, source_target_pairs={{0,1},{1,0},{2,3},{3,2},{4,5},{5,4},{6,7},{7,6},{8,9},{9,8},{10,11... | collective-permute-start | bytes 798728 | tf_op jit(solution)/shard_map/ppermute | solution.py:271
  27.2 26.3 %collective-permute-start.9 = (f32[2064,128]{1,0:T(8,128)S(1)}, f32[2064,128]{1,0:T(8,128)S(1)}, u32[]{:S(2)}, u32[]{:S(2)}) collective-permute-start(f32[2064,128]{1,0:T(8,128)S(1)} %pad.9), channel_id=1, source_target_pairs={{0,2},{2,0},{1,3},{3,1},{4,6},{6,4},{5,7},{7,5},{8,10},{10,8},{9,1... | collective-permute-start | bytes 3170312 | tf_op jit(solution)/shard_map/ppermute | solution.py:271
  32.3 4.8 %collective-permute-start.10 = (f32[4,4,128,128]{3,2,1,0:T(8,128)S(1)}, f32[4,4,128,128]{3,2,1,0:T(8,128)S(1)}, u32[]{:S(2)}, u32[]{:S(2)}) collective-permute-start(f32[4,4,128,128]{3,2,1,0:T(8,128)S(1)} %copy-done), channel_id=1, source_target_pairs={{0,1},{1,0},{2,3},{3,2},{4,5},{5,4},{6,7},{7,6},{8,9},{9,8},{10,11... | collective-permute-start | bytes 3145736 | tf_op jit(solution)/shard_map/ppermute | solution.py:271
  32.5 23.7 %collective-permute-start.13 = (f32[640,128]{1,0:T(8,128)S(1)}, f32[640,128]{1,0:T(8,128)S(1)}, u32[]{:S(2)}, u32[]{:S(2)}) collective-permute-start(f32[640,128]{1,0:T(8,128)S(1)} %get-tuple-element.72), channel_id=1, source_target_pairs={{0,8},{4,12},{8,0},{12,4},{1,9},{5,13},{9,1},{13,5},{2,10},{6,14},... | collective-permute-start | bytes 983048 | tf_op jit(solution)/shard_map/ppermute | solution.py:271
  32.5 24.3 %collective-permute-start.14 = (f32[2,128,128]{2,1,0:T(8,128)S(1)}, f32[2,128,128]{2,1,0:T(8,128)S(1)}, u32[]{:S(2)}, u32[]{:S(2)}) collective-permute-start(f32[2,128,128]{2,1,0:T(8,128)S(1)} %get-tuple-element.61), channel_id=1, source_target_pairs={{0,2},{2,0},{1,3},{3,1},{4,6},{6,4},{5,7},{7,5},{8,10},{10,8},{9,1... | collective-permute-start | bytes 393224 | tf_op jit(solution)/shard_map/ppermute | solution.py:271
  33.0 28.5 %collective-permute-start.18 = (f32[648,128]{1,0:T(8,128)S(1)}, f32[648,128]{1,0:T(8,128)S(1)}, u32[]{:S(2)}, u32[]{:S(2)}) collective-permute-start(f32[648,128]{1,0:T(8,128)S(1)} %get-tuple-element.81), channel_id=1, source_target_pairs={{0,12},{4,0},{8,4},{12,8},{1,13},{5,1},{9,5},{13,9},{2,14},{6,2},{... | collective-permute-start | bytes 995336 | tf_op jit(solution)/shard_map/ppermute | solution.py:271
  37.1 27.6 %collective-permute-start.16 = (f32[648,128]{1,0:T(8,128)S(1)}, f32[648,128]{1,0:T(8,128)S(1)}, u32[]{:S(2)}, u32[]{:S(2)}) collective-permute-start(f32[648,128]{1,0:T(8,128)S(1)} %get-tuple-element.76), channel_id=1, source_target_pairs={{0,4},{4,8},{8,12},{12,0},{1,5},{5,9},{9,13},{13,1},{2,6},{6,10},{... | collective-permute-start | bytes 995336 | tf_op jit(solution)/shard_map/ppermute | solution.py:271
  53.5 3.4 %collective-permute-start.12 = (f32[640,128]{1,0:T(8,128)S(1)}, f32[640,128]{1,0:T(8,128)S(1)}, u32[]{:S(2)}, u32[]{:S(2)}) collective-permute-start(f32[640,128]{1,0:T(8,128)S(1)} %get-tuple-element.70.refs_0_), channel_id=1, source_target_pairs={{0,1},{1,0},{2,3},{3,2},{4,5},{5,4},{6,7},{7,6},{8,9},{9,8},{10,11... | collective-permute-start | bytes 983048 | tf_op jit(solution)/shard_map/ppermute | solution.py:271
  53.5 4.9 %copy-start.2 = (f32[4,128,128]{2,1,0:T(8,128)S(1)}, f32[4,128,128]{2,1,0:T(8,128)}, u32[]{:S(2)}) copy-start(f32[4,128,128]{2,1,0:T(8,128)} %diagonal.9) | copy-start | bytes 786436
  56.2 3.7 %collective-permute-start.15 = (f32[640,128]{1,0:T(8,128)S(1)}, f32[640,128]{1,0:T(8,128)S(1)}, u32[]{:S(2)}, u32[]{:S(2)}) collective-permute-start(f32[640,128]{1,0:T(8,128)S(1)} %collective-permute-done.13.refs_0_), channel_id=1, source_target_pairs={{0,1},{1,0},{2,3},{3,2},{4,5},{5,4},{6,7},{7,6},{8,9},{9,8},{10,11... | collective-permute-start | bytes 983048 | tf_op jit(solution)/shard_map/ppermute | solution.py:271
  56.8 1.6 %collective-permute-start.11 = (f32[4,128,128]{2,1,0:T(8,128)S(1)}, f32[4,128,128]{2,1,0:T(8,128)S(1)}, u32[]{:S(2)}, u32[]{:S(2)}) collective-permute-start(f32[4,128,128]{2,1,0:T(8,128)S(1)} %shard_map.132.beside), channel_id=1, source_target_pairs={{0,1},{1,0},{2,3},{3,2},{4,5},{5,4},{6,7},{7,6},{8,9},{9,8},{10,11... | collective-permute-start | bytes 786440 | tf_op jit(solution)/shard_map/ppermute | solution.py:271
  61.6 5.2 %collective-permute-start.19 = (f32[648,128]{1,0:T(8,128)S(1)}, f32[648,128]{1,0:T(8,128)S(1)}, u32[]{:S(2)}, u32[]{:S(2)}) collective-permute-start(f32[648,128]{1,0:T(8,128)S(1)} %collective-permute-done.18.refs_0_), channel_id=1, source_target_pairs={{0,1},{1,0},{2,3},{3,2},{4,5},{5,4},{6,7},{7,6},{8,9},{9,8},{10,11... | collective-permute-start | bytes 995336 | tf_op jit(solution)/shard_map/ppermute | solution.py:271
  64.7 4.2 %collective-permute-start.17 = (f32[648,128]{1,0:T(8,128)S(1)}, f32[648,128]{1,0:T(8,128)S(1)}, u32[]{:S(2)}, u32[]{:S(2)}) collective-permute-start(f32[648,128]{1,0:T(8,128)S(1)} %collective-permute-done.16.refs_0_), channel_id=1, source_target_pairs={{0,1},{1,0},{2,3},{3,2},{4,5},{5,4},{6,7},{7,6},{8,9},{9,8},{10,11... | collective-permute-start | bytes 995336 | tf_op jit(solution)/shard_map/ppermute | solution.py:271
  64.7 7.2 %collective-permute-start.20 = (f32[1,2,128,128]{3,2,1,0:T(8,128)S(1)}, f32[1,2,128,128]{3,2,1,0:T(8,128)S(1)}, u32[]{:S(2)}, u32[]{:S(2)}) collective-permute-start(f32[1,2,128,128]{3,2,1,0:T(8,128)S(1)} %get-tuple-element.77), channel_id=1, source_target_pairs={{0,2},{2,0},{1,3},{3,1},{4,6},{6,4},{5,7},{7,5},{8,10},{10,8},{9,1... | collective-permute-start | bytes 393224 | tf_op jit(solution)/shard_map/ppermute | solution.py:271
  65.3 8.6 %collective-permute-start.21 = (f32[1,2,128,128]{3,2,1,0:T(8,128)S(1)}, f32[1,2,128,128]{3,2,1,0:T(8,128)S(1)}, u32[]{:S(2)}, u32[]{:S(2)}) collective-permute-start(f32[1,2,128,128]{3,2,1,0:T(8,128)S(1)} %get-tuple-element.78), channel_id=1, source_target_pairs={{0,2},{2,0},{1,3},{3,1},{4,6},{6,4},{5,7},{7,5},{8,10},{10,8},{9,1... | collective-permute-start | bytes 393224 | tf_op jit(solution)/shard_map/ppermute | solution.py:271
  68.3 8.4 %collective-permute-start.23 = (f32[1,2,128,128]{3,2,1,0:T(8,128)S(1)}, f32[1,2,128,128]{3,2,1,0:T(8,128)S(1)}, u32[]{:S(2)}, u32[]{:S(2)}) collective-permute-start(f32[1,2,128,128]{3,2,1,0:T(8,128)S(1)} %get-tuple-element.89), channel_id=1, source_target_pairs={{0,2},{2,0},{1,3},{3,1},{4,6},{6,4},{5,7},{7,5},{8,10},{10,8},{9,1... | collective-permute-start | bytes 393224 | tf_op jit(solution)/shard_map/ppermute | solution.py:271
  70.4 8.6 %collective-permute-start.22 = (f32[1,2,128,128]{3,2,1,0:T(8,128)S(1)}, f32[1,2,128,128]{3,2,1,0:T(8,128)S(1)}, u32[]{:S(2)}, u32[]{:S(2)}) collective-permute-start(f32[1,2,128,128]{3,2,1,0:T(8,128)S(1)} %get-tuple-element.88), channel_id=1, source_target_pairs={{0,2},{2,0},{1,3},{3,1},{4,6},{6,4},{5,7},{7,5},{8,10},{10,8},{9,1... | collective-permute-start | bytes 393224 | tf_op jit(solution)/shard_map/ppermute | solution.py:271
